TPU v7x, 32 devices: a whole 2x2x4 slice. The times are simulated.
32 devices in a mesh: dp: 8 (over z, y), mp: 4 (over x, core).
Axes of the slice: x: 2, y: 2, z: 4, core: 2. Of those that a mesh axis runs over, the one named last changes fastest.
Arguments:
- token_ids: int32 [1024, 16], P('dp'), may hold values from 0 to 31999
- lengths: int32 [1024], P('dp'), may hold values from 1 to 16
- images: bfloat16 [1024, 768], P(('dp', 'mp')), may hold values from -6 to 6
- table: bfloat16 [32000, 768], P('mp'), may hold values from -6 to 6
- pos_table: bfloat16 [16, 768], replicated, may hold values from -4 to 4
- ln1_gain: bfloat16 [768], replicated, may hold values from 0.5 to 1.5
- ln1_bias: bfloat16 [768], replicated, may hold values from -2 to 2
- w_qkv: bfloat16 [3, 768, 768], P(None, None, 'mp'), may hold values from -0.21875 to 0.21875
- w_out: bfloat16 [768, 768], P('mp'), may hold values from -0.625 to 0.625
- b_out: bfloat16 [768], replicated, may hold values from -2 to 2
- ln2_gain: bfloat16 [768], replicated, may hold values from 0.5 to 1.5
- ln2_bias: bfloat16 [768], replicated, may hold values from -2 to 2
- w_up: bfloat16 [768, 3072], P(None, 'mp'), may hold values from -0.21875 to 0.21875
- b_up: bfloat16 [3072], P('mp'), may hold values from -2 to 2
- w_down: bfloat16 [3072, 768], P('mp'), may hold values from -0.109375 to 0.109375
- b_down: bfloat16 [768], replicated, may hold values from -2 to 2
- w_head: bfloat16 [768, 768], replicated, may hold values from -0.21875 to 0.21875
Outputs:
- loss: float32 [], replicated
- table_grad: float32 [32000, 768], P(('mp', 'dp'))
- pos_table_grad: float32 [16, 768], P(None, 'dp')
- ln1_gain_grad: float32 [768], P('dp')
- ln1_bias_grad: float32 [768], P('dp')
- w_qkv_grad: float32 [3, 768, 768], P(None, 'dp', 'mp')
- w_out_grad: float32 [768, 768], P('mp', 'dp')
- b_out_grad: float32 [768], P('dp')
- ln2_gain_grad: float32 [768], P('dp')
- ln2_bias_grad: float32 [768], P('dp')
- w_up_grad: float32 [768, 3072], P('dp', 'mp')
- b_up_grad: float32 [3072], P(('mp', 'dp'))
- w_down_grad: float32 [3072, 768], P('mp', 'dp')
- b_down_grad: float32 [768], P('dp')
- w_head_grad: float32 [768, 768], P('dp')
Inputs may be any that keep to these rules, and one draw needn't show every extreme that they name: Caption lengths; positions at or after a caption's length are padding.
All inputs are finite; a program needn't handle non-finite values.
Results may differ from a plain program's by a relative error of at most 0.014.
Values may be sent and summed in bfloat16 or wider, within the bound.
No kernel may reach another device: no remote copies, remote signals or barrier semaphores. Data moves between devices by JAX's collectives and lax.ppermute only.
A program may use at most 192 MiB of HBM per device.

v0:
```python
import functools
import math

import jax
import jax.numpy as jnp
from jax import lax
from jax.experimental import pallas as pl
from jax.experimental.pallas import tpu as pltpu
from jax.sharding import PartitionSpec as P

HEAD_DIM = 64
LOGIT_SCALE = 50.0
EPS = 1e-06
MASK_FILL = -1000000000.0
NO_KEY = -1e30
BF = jnp.bfloat16
F32 = jnp.float32
I32 = jnp.int32
GELU_C = math.sqrt(2.0 / math.pi)
CAP_BLOCK = 16
SMALLS = 32
NOTES = 8
VALID_BIT = 1 << 20
END_BIT = 1 << 21
NOTE_BASE = 32
WORK = 920000000
DOWN_BIT = 1
UP_BIT = 2


def nn(a, b):
    return lax.dot_general(a, b, (((1,), (0,)), ((), ())), preferred_element_type=F32)


def nt(a, b):
    return lax.dot_general(a, b, (((1,), (1,)), ((), ())), preferred_element_type=F32)


def tn(a, b):
    return lax.dot_general(a, b, (((0,), (0,)), ((), ())), preferred_element_type=F32)


def normalize(rows):
    centred = rows - jnp.mean(rows, -1, keepdims=True)
    inverse = lax.rsqrt(jnp.mean(centred * centred, -1, keepdims=True) + EPS)
    return centred * inverse, inverse


def norm_back(upstream, unit, inverse, gain):
    scaled = upstream * gain
    mean_scaled = jnp.mean(scaled, -1, keepdims=True)
    mean_unit = jnp.mean(scaled * unit, -1, keepdims=True)
    return inverse * (scaled - mean_scaled - unit * mean_unit)


def iota2(shape, dim):
    return lax.broadcasted_iota(I32, shape, dim)


class Late:
    def __init__(self, ref, pairs, sems):
        self.ref = ref
        self.copies = [
            pltpu.make_async_copy(src, dst, sem) for (src, dst), sem in zip(pairs, sems)
        ]
        self.waiting = set(range(len(self.copies)))

    def start(self):
        for copy in self.copies:
            copy.start()

    def wait(self, part=None):
        for k in sorted(self.waiting) if part is None else [part]:
            if k in self.waiting:
                self.copies[k].wait()
                self.waiting.discard(k)
        return self.ref

    def value(self):
        return self.wait()[...]


def fetch(array, parts=1, axis=0):
    return ("blocks", [array], parts, axis)


def fetch_weight(shards, which):
    return ("weight", list(shards), which, 0)


def vmem_call(body, outs, meta, args, late=(), scratch=(), flops=1, mib=40):
    vmem = pl.BlockSpec(memory_space=pltpu.VMEM)
    hbm = pl.BlockSpec(memory_space=pltpu.HBM)
    sources, buffers, counts = [], [], []
    for kind, arrays, parts, axis in late:
        sources += arrays
        if kind == "weight":
            _, rows, width = arrays[0].shape
            buffers.append(pltpu.VMEM((rows * len(arrays), width), arrays[0].dtype))
            counts.append(len(arrays))
        else:
            buffers.append(pltpu.VMEM(arrays[0].shape, arrays[0].dtype))
            counts.append(parts)

    staged = [k for k, o in enumerate(outs) if len(o) > 2 and o[2]]

    def kernel(meta_ref, *refs):
        arg_refs, refs = refs[: len(args)], refs[len(args) :]
        source_refs, refs = refs[: len(sources)], refs[len(sources) :]
        out_refs, refs = refs[: len(outs)], refs[len(outs) :]
        buffer_refs, refs = refs[: len(buffers)], refs[len(buffers) :]
        sems, stage_sems, refs = refs[0], refs[1], refs[2:]
        stages, refs = refs[: len(staged)], refs[len(staged) :]
        targets = list(out_refs)
        for k, stage in zip(staged, stages):
            targets[k] = stage
        handles, at, place = [], 0, 0
        for (kind, arrays, parts, axis), buffer in zip(late, buffer_refs):
            if kind == "weight":
                rows = arrays[0].shape[1]
                pairs = []
                for k in range(len(arrays)):
                    low = pl.multiple_of((meta_ref[0] ^ k) * rows, rows)
                    pairs.append((source_refs[place + k].at[parts], buffer.at[pl.ds(low, rows)]))
                place += len(arrays)
            else:
                size = arrays[0].shape[axis] // parts
                pairs = []
                for k in range(parts):
                    cut = (slice(None),) * axis + (pl.ds(k * size, size),)
                    pairs.append((source_refs[place].at[cut], buffer.at[cut]))
                place += 1
            handles.append(Late(buffer, pairs, [sems.at[at + k] for k in range(len(pairs))]))
            at += len(pairs)
        for handle in handles:
            handle.start()
        body(meta_ref, *arg_refs, *handles, *targets, *refs)
        copies = [
            pltpu.make_async_copy(stage, out_refs[k], stage_sems.at[i])
            for i, (k, stage) in enumerate(zip(staged, stages))
        ]
        for copy in copies:
            copy.start()
        for handle in handles:
            handle.wait()
        for copy in copies:
            copy.wait()

    return pl.pallas_call(
        kernel,
        out_shape=[
            pltpu.HBM(*o[:2]) if len(o) > 2 else jax.ShapeDtypeStruct(*o) for o in outs
        ],
        in_specs=[pl.BlockSpec(memory_space=pltpu.SMEM)]
        + [vmem] * len(args)
        + [hbm] * len(sources),
        out_specs=[hbm if len(o) > 2 else vmem for o in outs],
        scratch_shapes=[
            *buffers,
            pltpu.SemaphoreType.DMA((max(1, sum(counts)),)),
            pltpu.SemaphoreType.DMA((max(1, len(staged)),)),
            *(pltpu.VMEM(*outs[k][:2]) for k in staged),
            *scratch,
        ],
        compiler_params=pltpu.CompilerParams(vmem_limit_bytes=mib << 20),
        cost_estimate=pl.CostEstimate(flops=flops, bytes_accessed=1, transcendentals=0),
    )(meta, *args, *(pltpu.with_memory_space_constraint(x, pltpu.HBM) for x in sources))


def exchange_half(kept, sent, axis, bit, last):
    count = lax.axis_size(axis)
    got = lax.ppermute(sent, axis, [(i, i ^ bit) for i in range(count)])
    total = kept.astype(F32) + got.astype(F32)
    return total if last else total.astype(BF)


def halve(total, axis, bits, bit):
    low = 1 << bits.index(bit)
    pairs = total.reshape((total.shape[0] // (2 * low), 2, low) + total.shape[1:])
    shape = (total.shape[0] // 2,) + total.shape[1:]
    mine = (lax.axis_index(axis) // bit) % 2
    sent = lax.dynamic_index_in_dim(pairs, 1 - mine, 1, keepdims=False).reshape(shape)
    kept = lax.dynamic_index_in_dim(pairs, mine, 1, keepdims=False).reshape(shape)
    return exchange_half(kept, sent, axis, bit, len(bits) == 1)


def split_blocks(blocks, bit, mine, kept_ref, sent_ref):
    place = 0
    for i in range(len(blocks)):
        if i & bit == 0:
            first, second = blocks[i](), blocks[i | bit]()
            kept_ref[place] = jnp.where(mine == 0, first, second).astype(BF)
            sent_ref[place] = jnp.where(mine == 0, second, first).astype(BF)
            place += 1


def bits_of(axis):
    count = lax.axis_size(axis)
    return [1 << k for k in range(count.bit_length() - 1)]


def after(x, *others):
    return lax.optimization_barrier((x, others))[0]


def everyone(x, axis, before):
    count = lax.axis_size(axis)
    have = {0: x}
    bit = count // 2
    while bit:
        pairs = [(i, i ^ bit) for i in range(count)]
        for k, v in list(have.items()):
            have[k | bit] = lax.ppermute(after(v, before) if k else v, axis, pairs)
        bit //= 2
    return [have[k] for k in range(count)]


def own_columns(start, width, own_width):
    shape = (width, own_width)
    hit = iota2(shape, 0) == start + iota2(shape, 1)
    return jnp.where(hit, 1.0, 0.0).astype(BF)


def unpack(packed):
    return packed % VALID_BIT, packed // VALID_BIT % 2 > 0, packed // END_BIT > 0


def own_code(packed, rank, vocab_part):
    ids, valid, _ = unpack(packed)
    return jnp.where(ids // vocab_part == rank, jnp.where(valid, 2, 1), 0)


def head_mask(captions, span):
    shape = (span // HEAD_DIM * captions, span)
    return (iota2(shape, 0) // captions) == (iota2(shape, 1) // HEAD_DIM)


def spread_heads(rows, group, mask):
    span = mask.shape[1]
    part = rows[:, group * span : (group + 1) * span].astype(F32)
    tall = jnp.concatenate([part] * (span // HEAD_DIM), axis=0)
    return jnp.where(mask, tall, 0.0).astype(BF)


def fold_heads(tall, captions, mask):
    kept = jnp.where(mask, tall, 0.0)
    total = kept[:captions]
    for h in range(1, tall.shape[0] // captions):
        total = total + kept[h * captions : (h + 1) * captions]
    return total


def same_caption(heads, seq_len):
    shape = (heads * CAP_BLOCK, CAP_BLOCK * seq_len)
    return (iota2(shape, 0) % CAP_BLOCK) == (iota2(shape, 1) // seq_len)


def rows_body(
    vocab_part, meta_ref, pos_ref, vec_ref, packed_ref, emb,
    end_ref, rows_out, unit_out, inv_out, rows_ref, unit_ref, inv_ref, sems,
):
    captions = end_ref.shape[0]
    seq_len = pos_ref.shape[0]
    block_rows = CAP_BLOCK * seq_len
    gain, bias = vec_ref[0:1], vec_ref[1:2]
    pos = jnp.concatenate([pos_ref[...].astype(F32)] * CAP_BLOCK, axis=0)
    pending = []

    def write_back(src, dst):
        copy = pltpu.make_async_copy(src, dst, sems.at[len(pending)])
        copy.start()
        pending.append(copy)

    for block in range(captions // CAP_BLOCK):
        here = pl.ds(block * block_rows, block_rows)
        packed = packed_ref[:, block * block_rows : (block + 1) * block_rows]
        low = emb.wait(block)[here, :]
        ids, _, is_end = unpack(packed)
        shape = (CAP_BLOCK, block_rows)
        mark = jnp.logical_and(is_end, ids // vocab_part == meta_ref[0])
        mark = jnp.logical_and(iota2(shape, 0) == iota2(shape, 1) // seq_len, mark)
        ends = nn(jnp.where(mark, 1.0, 0.0).astype(BF), low)
        end_ref[block * CAP_BLOCK : (block + 1) * CAP_BLOCK] = ends.astype(BF)
        unit, inverse = normalize(low.astype(F32) + pos)
        unit_ref[here, :] = unit.astype(BF)
        write_back(unit_ref.at[here], unit_out.at[here])
        inv_ref[here, :] = jnp.broadcast_to(inverse, (block_rows, 128))
        write_back(inv_ref.at[here], inv_out.at[here])
        rows_ref[here, :] = (unit * gain + bias).astype(BF)
        write_back(rows_ref.at[here], rows_out.at[here])
    for copy in pending:
        copy.wait()


def attend_body(
    vocab_part, meta_ref, ends_ref, pos_pick_ref, pos_ref, vec_ref, packed_ref, wq, wk, rows_all, wv,
    pay_ref, qk_out, x0p_ref, q_ref, qk_ref, t_ref, sems,
):
    n_mp = ends_ref.shape[0]
    captions, width = x0p_ref.shape
    heads = width // HEAD_DIM
    span = width // n_mp
    per_group = span // HEAD_DIM
    seq_len = pos_ref.shape[0]
    block_rows = CAP_BLOCK * seq_len
    gain, bias = vec_ref[0:1], vec_ref[1:2]
    pooled_in = nn(pos_pick_ref[...], pos_ref[...])
    for i in range(n_mp):
        pooled_in = pooled_in + ends_ref[i].astype(F32)
    pending = []
    x0p_ref[...] = pooled_in
    unit, _ = normalize(pooled_in)
    q = nt((unit * gain + bias).astype(BF), wq.value()).astype(BF)
    q_ref[...] = q
    mask = head_mask(captions, span)
    scale = 1.0 / math.sqrt(HEAD_DIM)
    wk_ref = wk.wait()
    for g in range(n_mp):
        some = slice(g * per_group, (g + 1) * per_group)
        tall = nn(spread_heads(q, g, mask), wk_ref[g * span : (g + 1) * span]) * scale
        qk_ref[some] = tall.astype(BF).reshape(per_group, captions, width)
        copy = pltpu.make_async_copy(qk_ref.at[some], qk_out.at[some], sems.at[g])
        copy.start()
        pending.append(copy)
    lane = iota2((heads, CAP_BLOCK, 128), 2)
    head_of = iota2((heads, CAP_BLOCK, 128), 0)
    rows_ref = rows_all.wait()
    blocks = range(captions // CAP_BLOCK)
    cuts = [pl.ds(block * block_rows, block_rows) for block in blocks]
    caps = [pl.ds(block * CAP_BLOCK, CAP_BLOCK) for block in blocks]
    raw = [
        nt(qk_ref[:, caps[block], :].reshape(heads * CAP_BLOCK, width), rows_ref[cuts[block], :])
        for block in blocks
    ]
    same = same_caption(heads, seq_len)
    code = own_code(packed_ref[...], meta_ref[0], vocab_part)
    log_totals, weights = [], []
    for block in blocks:
        here = code[:, block * block_rows : (block + 1) * block_rows]
        own = jnp.logical_and(same, here > 0)
        scores = jnp.where(own, jnp.where(here > 1, raw[block], MASK_FILL), NO_KEY)
        top = jnp.max(scores, -1, keepdims=True)
        power = jnp.where(own, jnp.exp(scores - top), 0.0)
        total = jnp.sum(power, -1, keepdims=True)
        some = total > 0.0
        total = jnp.where(some, total, 1.0)
        log_totals.append(jnp.where(some, top + jnp.log(total), NO_KEY))
        weights.append((power * (1.0 / total)).astype(BF))
    for block in blocks:
        mixed = nn(weights[block], rows_ref[cuts[block], :])
        t_ref[:, caps[block], :] = mixed.astype(BF).reshape(heads, CAP_BLOCK, width)
    for block in blocks:
        log_total = log_totals[block]
        first = log_total.astype(BF).astype(F32)
        second = (log_total - first).astype(BF).astype(F32)
        third = log_total - first - second
        stat = jnp.zeros((heads, CAP_BLOCK, 128), F32)
        for k, piece in enumerate((first, second, third)):
            stat = stat + jnp.where(
                lane == head_of + 16 * k, piece.reshape(heads, CAP_BLOCK, 1), 0.0
            )
        pay_ref[caps[block], width:] = jnp.sum(stat, 0).astype(BF)
    wv_ref = wv.wait()
    for g in range(n_mp):
        tall = t_ref[g * per_group : (g + 1) * per_group].reshape(per_group * captions, width)
        piece = nt(tall, wv_ref[g * span : (g + 1) * span])
        pay_ref[:, g * span : (g + 1) * span] = fold_heads(piece, captions, mask).astype(BF)
    for copy in pending:
        copy.wait()


def hidden_body(
    meta_ref, pay_ref, vec_ref, x0p, wo, wup, wdown,
    ctx_ref, lse_ref, x1_ref, u_ref, part_ref,
):
    n_mp = pay_ref.shape[0]
    captions, width = ctx_ref.shape
    shape = (128, width)
    stat_row, head = iota2(shape, 0), iota2(shape, 1) // HEAD_DIM
    picks = jnp.logical_and(stat_row % 16 == head, stat_row < 48)
    expand = jnp.where(picks, 1.0, 0.0).astype(BF)
    logs = [nn(pay_ref[i, :, width:], expand) for i in range(n_mp)]
    top = functools.reduce(jnp.maximum, logs)
    total = jnp.zeros_like(top)
    ctx = jnp.zeros_like(top)
    for i in range(n_mp):
        weight = jnp.exp(logs[i] - top)
        total = total + weight
        ctx = ctx + weight * pay_ref[i, :, :width].astype(F32)
    ctx = ctx / total
    ctx_ref[...] = ctx
    lse_ref[...] = top + jnp.log(total)
    x1 = x0p.value() + nn(ctx.astype(BF), wo.value()) + vec_ref[2:3]
    x1_ref[...] = x1
    unit, _ = normalize(x1)
    h2 = (unit * vec_ref[3:4] + vec_ref[4:5]).astype(BF)
    u = nn(h2, wup.value()) + vec_ref[6:7]
    u_ref[...] = u
    hidden = (0.5 * u * (1.0 + jnp.tanh(GELU_C * (u + 0.044715 * u * u * u)))).astype(BF)
    part_ref[...] = nn(hidden, wdown.value()).astype(BF)


def logits_body(
    meta_ref, parts_ref, vec_ref, x1, wh, images,
    pooled_ref, proj_ref, e_ref, sums_ref,
):
    x2 = x1.value() + vec_ref[5:6]
    for i in range(parts_ref.shape[0]):
        x2 = x2 + parts_ref[i].astype(F32)
    pooled = x2.astype(BF)
    pooled_ref[...] = pooled
    proj = nn(pooled, wh.value())
    proj_ref[...] = proj
    text = (proj * lax.rsqrt(jnp.sum(proj * proj, -1, keepdims=True) + EPS)).astype(BF)
    logits = LOGIT_SCALE * nt(text, images.value())
    powers = jnp.exp(logits)
    e_ref[...] = powers
    n_all = powers.shape[1]
    is_diag = iota2(logits.shape, 1) == meta_ref[1] + iota2(logits.shape, 0)
    rows = jnp.log(jnp.sum(powers, -1, keepdims=True))
    rows = rows - 2.0 * jnp.sum(jnp.where(is_diag, logits, 0.0), -1, keepdims=True)
    cols = jnp.sum(powers, 0, keepdims=True)
    rows = jnp.broadcast_to(jnp.sum(rows, 0, keepdims=True), (1, 128))
    for i in range(sums_ref.shape[0]):
        sums_ref[i, :, :n_all] = cols
        sums_ref[i, :, n_all:] = rows


def loss_body(
    meta_ref, sums_ref, vec_ref, e, images, proj, wh, u, wdown, wup, x1, pooled,
    loss_ref, dpooled_ref, part_ref, down_kept, down_sent, up_kept, up_sent, small_ref,
    down_ref, up_ref,
):
    width = dpooled_ref.shape[1]
    sums = jnp.sum(sums_ref[...], 0)
    n_all = sums.shape[1] - 128
    cols = sums[:, :n_all]
    loss = jnp.sum(jnp.log(cols), -1, keepdims=True) + sums[:, n_all : n_all + 1]
    loss_ref[...] = jnp.broadcast_to(loss * (0.5 / n_all), (1, 128))
    powers = e.value()
    row_inv = 1.0 / jnp.sum(powers, -1, keepdims=True)
    is_diag = iota2(powers.shape, 1) == meta_ref[1] + iota2(powers.shape, 0)
    grad = powers * row_inv + powers * (1.0 / cols) - jnp.where(is_diag, 2.0, 0.0)
    grad = (grad * (0.5 / n_all)).astype(BF)
    dtext = LOGIT_SCALE * nn(grad, images.value())
    proj = proj.value()
    inv = lax.rsqrt(jnp.sum(proj * proj, -1, keepdims=True) + EPS)
    along = jnp.sum(proj * dtext, -1, keepdims=True)
    dproj = (inv * dtext - inv * inv * inv * proj * along).astype(BF)
    dpooled = nt(dproj, wh.value())
    dpooled_ref[...] = dpooled
    dy = dpooled.astype(BF)
    u = u.value()
    th = jnp.tanh(GELU_C * (u + 0.044715 * u * u * u))
    slope = 0.5 * (1.0 + th) + 0.5 * u * (1.0 - th * th) * (
        GELU_C * (1.0 + 3.0 * 0.044715 * u * u)
    )
    du = (nt(dy, wdown.value()) * slope).astype(BF)
    part_ref[...] = nt(du, wup.value()).astype(BF)
    hidden = (0.5 * u * (1.0 + th)).astype(BF)
    unit, _ = normalize(x1.value())
    h2 = (unit * vec_ref[3:4] + vec_ref[4:5]).astype(BF)
    ff = u.shape[1]
    own_width = down_ref.shape[1] - ff
    pick = own_columns(meta_ref[0] * own_width, width, own_width)
    down_ref[:, :ff] = tn(dy, hidden)
    up_ref[...] = tn(h2, du)
    down_ref[:, ff:] = tn(pooled.value(), nn(dproj, pick).astype(BF))
    chunk = down_kept.shape[1]
    n_dp = 2 * down_kept.shape[0]
    for ref, bit, kept, sent in (
        (down_ref, DOWN_BIT, down_kept, down_sent),
        (up_ref, UP_BIT, up_kept, up_sent),
    ):
        blocks = [
            functools.partial(lambda ref, i: ref[pl.ds(i * chunk, chunk), :], ref, i)
            for i in range(n_dp)
        ]
        split_blocks(blocks, bit, meta_ref[2] // bit % 2, kept, sent)
    small_ref[0:1] = jnp.sum(dy.astype(F32), 0, keepdims=True)
    small_ref[1:2] = jnp.sum(du.astype(F32), 0, keepdims=True)


def attend_back_body(
    vocab_part, meta_ref, parts_ref, packed_ref, vec_ref, dpooled_ref, x1, ctx, wo, wv, lse, qk_all, rows_all, wk, q,
    dx1_ref, wout_ref, kept_ref, sent_one, sent_two, a_ref, probs_ref, ds_ref, small_ref,
    t_ref, s_ref, wkv_ref, dq_ref,
):
    n_mp = wkv_ref.shape[0]
    captions, width = dpooled_ref.shape
    heads = width // HEAD_DIM
    span = width // n_mp
    per_group = span // HEAD_DIM
    block_rows = rows_all.ref.shape[0] // (captions // CAP_BLOCK)
    seq_len = block_rows // CAP_BLOCK
    rank = meta_ref[0]
    dh2 = parts_ref[0].astype(F32)
    for i in range(1, parts_ref.shape[0]):
        dh2 = dh2 + parts_ref[i].astype(F32)
    unit2, inv2 = normalize(x1.value())
    small_ref[0:1] = jnp.sum(dh2 * unit2, 0, keepdims=True)
    small_ref[1:2] = jnp.sum(dh2, 0, keepdims=True)
    dx1 = dpooled_ref[...] + norm_back(dh2, unit2, inv2, vec_ref[3:4])
    dx1_ref[...] = dx1
    da = dx1.astype(BF)
    small_ref[2:3] = jnp.sum(da.astype(F32), 0, keepdims=True)
    ctx = ctx.value()
    pick = own_columns(rank * span, width, span)
    wout_ref[...] = tn(da, nn(ctx.astype(BF), pick).astype(BF)).astype(BF)
    dctx = nt(da, wo.value()).astype(BF)
    mask = head_mask(captions, span)
    wv_ref = wv.wait()
    for g in range(n_mp):
        tall = nn(spread_heads(dctx, g, mask), wv_ref[g * span : (g + 1) * span])
        a_ref[g * per_group : (g + 1) * per_group] = tall.astype(BF).reshape(
            per_group, captions, width
        )
    prod = dctx.astype(F32) * ctx
    lse = lse.value()
    scale = 1.0 / math.sqrt(HEAD_DIM)
    tall_shape = (heads * CAP_BLOCK, width)
    of_head = (iota2(tall_shape, 0) // CAP_BLOCK) == (iota2(tall_shape, 1) // HEAD_DIM)
    at_head = (iota2(tall_shape, 0) // CAP_BLOCK) * HEAD_DIM == iota2(tall_shape, 1)
    rows_ref, qk_ref = rows_all.wait(), qk_all.wait()
    same = same_caption(heads, seq_len)
    code = own_code(packed_ref[...], rank, vocab_part)
    tall = (heads * CAP_BLOCK, width)
    blocks = range(captions // CAP_BLOCK)
    cuts = [pl.ds(block * block_rows, block_rows) for block in blocks]
    caps = [pl.ds(block * CAP_BLOCK, CAP_BLOCK) for block in blocks]
    raw = [nt(qk_ref[:, caps[block], :].reshape(tall), rows_ref[cuts[block], :]) for block in blocks]
    pulled = [nt(a_ref[:, caps[block], :].reshape(tall), rows_ref[cuts[block], :]) for block in blocks]
    probs_all, ds_all = [], []
    for block in blocks:
        low = block * CAP_BLOCK
        here = code[:, block * block_rows : (block + 1) * block_rows]
        own = jnp.logical_and(same, here > 0)
        scores = jnp.where(here > 1, raw[block], MASK_FILL)
        spread = jnp.concatenate([lse[low : low + CAP_BLOCK]] * heads, axis=0)
        log_total = jnp.sum(jnp.where(at_head, spread, 0.0), -1, keepdims=True)
        spread = jnp.concatenate([prod[low : low + CAP_BLOCK]] * heads, axis=0)
        row_sum = jnp.sum(jnp.where(of_head, spread, 0.0), -1, keepdims=True)
        probs = jnp.where(own, jnp.exp(scores - log_total), 0.0)
        dscores = (probs * (pulled[block] - row_sum)).astype(BF)
        probs = probs.astype(BF)
        probs_ref[block] = probs
        ds_ref[block] = dscores
        probs_all.append(probs)
        ds_all.append(dscores)
    for block in blocks:
        rows = rows_ref[cuts[block], :]
        t_ref[:, caps[block], :] = (
            nn(probs_all[block], rows).astype(BF).reshape(heads, CAP_BLOCK, width)
        )
        s_ref[:, caps[block], :] = (
            (nn(ds_all[block], rows) * scale).astype(BF).reshape(heads, CAP_BLOCK, width)
        )
    q = q.value()
    wk_ref = wk.wait()
    for g in range(n_mp):
        some = slice(g * per_group, (g + 1) * per_group)
        tall = s_ref[some].reshape(per_group * captions, width)
        piece = nt(tall, wk_ref[g * span : (g + 1) * span])
        dq_ref[:, g * span : (g + 1) * span] = fold_heads(piece, captions, mask).astype(BF)
        wkv_ref[g, :, :span] = tn(tall, spread_heads(q, g, mask)).astype(BF)
        tall = t_ref[some].reshape(per_group * captions, width)
        wkv_ref[g, :, span:] = tn(tall, spread_heads(dctx, g, mask)).astype(BF)
    half = sent_one.shape[0]

    def put(low, piece):
        inside = min(max(half - low, 0), piece.shape[0])
        if inside > 0:
            sent_one[low : low + inside] = piece[:inside]
        if inside < piece.shape[0]:
            sent_two[low + inside - half : low + piece.shape[0] - half] = piece[inside:]

    for g in range(0, n_mp, 2):
        at = slice(g // 2 * width, (g // 2 + 1) * width)
        first, second = wkv_ref[g], wkv_ref[g + 1]
        kept_ref[at] = jnp.where(rank % 2 == 0, first, second)
        put(g // 2 * width, jnp.where(rank % 2 == 0, second, first))
    for k in range(n_mp // 2):
        at = slice(n_mp // 2 * width + k * captions, n_mp // 2 * width + (k + 1) * captions)
        piece = dq_ref[:, 2 * k * span : 2 * (k + 1) * span]
        kept_ref[at] = piece
        put(n_mp // 2 * width + k * captions, piece)


def between_body(meta_ref, kept_ref, got_one, got_two, kept_out, sent_out):
    block = kept_ref.shape[0] - kept_out.shape[0]
    half = got_one.shape[0]

    def total(low, high):
        parts = []
        if low < half:
            parts.append(got_one[low : min(high, half)])
        if high > half:
            parts.append(got_two[max(low, half) - half : high - half])
        got = parts[0] if len(parts) == 1 else jnp.concatenate(parts, axis=0)
        return kept_ref[low:high].astype(F32) + got.astype(F32)

    first, second = total(0, block), total(block, 2 * block)
    both = total(2 * block, kept_ref.shape[0]).astype(BF)
    upper = meta_ref[0] // 2 % 2
    kept_out[:block] = jnp.where(upper == 0, first, second).astype(BF)
    sent_out[:block] = jnp.where(upper == 0, second, first).astype(BF)
    kept_out[block:] = both
    sent_out[block:] = both


def slot_body(owner_rows, n_dp, meta_ref, packed_ref, out_ref):
    rows = packed_ref.shape[1]
    side = 128
    ids, _, _ = unpack(packed_ref[...])
    owner = ids // owner_rows
    order = iota2((1, rows), 1)

    def columns(row, k):
        piece = row[:, k * side : (k + 1) * side].astype(F32)
        return jnp.transpose(jnp.broadcast_to(piece, (side, side))).astype(I32)

    def tall(column):
        return jnp.concatenate([column] * (rows // side), axis=1)

    first_at = jnp.full((1, rows), rows, I32)
    for k in range(rows // side):
        there = k * side + iota2((side, rows), 0)
        hit = jnp.where(tall(columns(ids, k)) == ids, there, rows)
        first_at = jnp.minimum(first_at, jnp.min(hit, 0, keepdims=True))
    is_first = first_at == order
    first_owner = jnp.where(is_first, owner, -1)
    slot = jnp.zeros((1, rows), I32)
    for k in range(rows // side):
        there = k * side + iota2((side, rows), 0)
        ahead = jnp.logical_and(tall(columns(first_owner, k)) == owner, there < first_at)
        slot = slot + jnp.sum(jnp.where(ahead, 1, 0), 0, keepdims=True)
    here = owner - meta_ref[0] * n_dp
    dest = jnp.where(jnp.logical_and(here >= 0, here < n_dp), here, -1)
    most = jnp.max(slot.astype(F32), 1, keepdims=True).astype(I32) + 1
    out_ref[0:1] = slot
    out_ref[1:2] = dest
    out_ref[2:3] = jnp.where(is_first, ids % owner_rows + 1, 0)
    out_ref[3:4] = jnp.broadcast_to(most, (1, rows))
    out_ref[4:8] = jnp.zeros((4, rows), I32)


def slot_sums(turn, slot_cap, seq_len, slots_ref, packed_ref, dx_ref, n_dp):
    slots = n_dp * slot_cap
    rows = dx_ref.shape[0]
    step = min(512, rows)
    captions_per_step = step // seq_len
    total, digits, pooled = None, None, []
    for low in range(0, rows, step):
        cut = slice(low, low + step)
        place = slots_ref[0:1, cut] - turn * slot_cap
        dest, row = slots_ref[1:2, cut], slots_ref[2:3, cut]
        inside = jnp.logical_and(dest >= 0, jnp.logical_and(place >= 0, place < slot_cap))
        key = jnp.where(inside, dest * slot_cap + place, -1)
        hit = jnp.where(iota2((slots, step), 0) == key, 1.0, 0.0).astype(BF)
        piece = nn(hit, dx_ref[cut])
        total = piece if total is None else total + piece
        which = iota2((16, step), 0)
        value = jnp.where(which == 0, row // NOTE_BASE, jnp.where(which == 1, row % NOTE_BASE, 0))
        piece = nt(value.astype(F32).astype(BF), hit)
        digits = piece if digits is None else digits + piece
        _, _, is_end = unpack(packed_ref[:, cut])
        caption = iota2((captions_per_step, step), 1) // seq_len
        mark = jnp.logical_and(caption == iota2((captions_per_step, step), 0), is_end)
        pooled.append(nt(hit, jnp.where(mark, 1.0, 0.0).astype(BF)))
    return total, digits, jnp.concatenate(pooled, axis=1).astype(BF)


def rows_back_body(
    slot_cap, meta_ref, probs_ref, ds_ref, a_ref, vec_ref, slots_ref, packed_ref, qk_all, unit_all, inv_all,
    dx_out, posg_ref, small_ref, seg_ref, digits_ref, pooled_ref, dx_ref, sems,
):
    blocks = probs_ref.shape[0]
    heads = a_ref.shape[0]
    seq_len, width = posg_ref.shape
    block_rows = dx_ref.shape[0] // blocks
    gain = vec_ref[0:1]
    qk_ref, unit_ref, inv_ref = qk_all.wait(), unit_all.wait(), inv_all.wait()
    pending = []
    gain_grad = jnp.zeros((1, width), F32)
    bias_grad = jnp.zeros((1, width), F32)
    pos_grad = jnp.zeros((seq_len, width), F32)
    for block in range(blocks):
        caps = pl.ds(block * CAP_BLOCK, CAP_BLOCK)
        here = pl.ds(block * block_rows, block_rows)
        a = a_ref[:, caps, :].reshape(heads * CAP_BLOCK, width)
        qk = qk_ref[:, caps, :].reshape(heads * CAP_BLOCK, width)
        unit = unit_ref[here, :].astype(F32)
        drows = tn(probs_ref[block], a) + tn(ds_ref[block], qk)
        gain_grad = gain_grad + jnp.sum(drows * unit, 0, keepdims=True)
        bias_grad = bias_grad + jnp.sum(drows, 0, keepdims=True)
        dx = norm_back(drows, unit, inv_ref[here, 0:1], gain).astype(BF)
        dx_ref[here, :] = dx
        pos_grad = pos_grad + jnp.sum(dx.astype(F32).reshape(CAP_BLOCK, seq_len, width), 0)
    for block in range(blocks):
        here = pl.ds(block * block_rows, block_rows)
        copy = pltpu.make_async_copy(dx_ref.at[here], dx_out.at[here], sems.at[block])
        copy.start()
        pending.append(copy)
    small_ref[0:1] = gain_grad
    small_ref[1:2] = bias_grad
    posg_ref[...] = pos_grad
    seg_ref[...], digits_ref[...], pooled_ref[...] = slot_sums(
        0, slot_cap, seq_len, slots_ref, packed_ref, dx_ref, seg_ref.shape[0] // slot_cap
    )
    for copy in pending:
        copy.wait()


def query_back_body(
    n_mp, meta_ref, kept_ref, got_ref, wout_ref, dx1_ref, vec_ref, pos_pick_ref, own_pick_ref, slots_ref,
    seg_ref, digits_ref, pooled_ref, pos_one_ref, small_one_ref, small_two_ref, small_three_ref, x0p, wq,
    dxp_ref, send_ref, kept_out, sent_out, rest_ref, smalls_ref, all_ref,
):
    captions, width = dx1_ref.shape
    n_dp = send_ref.shape[0]
    slots = seg_ref.shape[0]
    slot_cap = slots // n_dp
    lanes = send_ref.shape[2]
    span = width // n_mp
    rank = meta_ref[0]
    total = kept_ref[...].astype(F32) + got_ref[...].astype(F32)
    all_ref[:, : 2 * span] = total[:width]
    all_ref[:, 2 * span : 3 * span] = wout_ref[...].astype(F32)
    dq = jnp.concatenate(
        [total[width + k * captions : width + (k + 1) * captions] for k in range(n_mp // 2)], axis=1
    ).astype(BF)
    gain = vec_ref[0:1]
    unit, inverse = normalize(x0p.value())
    h1 = (unit * gain + vec_ref[1:2]).astype(BF)
    owned = jnp.sum(own_pick_ref[...].astype(F32), -1, keepdims=True)
    dh1 = nn(dq, wq.value()) * owned
    dxp = (dx1_ref[...] * owned + norm_back(dh1, unit, inverse, gain)).astype(BF)
    dxp_ref[...] = dxp
    seq_len = pos_one_ref.shape[0]
    smalls_ref[...] = jnp.zeros_like(smalls_ref)
    smalls_ref[:seq_len] = pos_one_ref[...] + tn(pos_pick_ref[...], dxp)
    at = seq_len
    smalls_ref[at : at + 1] = small_three_ref[0:1] + jnp.sum(dh1 * unit, 0, keepdims=True)
    smalls_ref[at + 1 : at + 2] = small_three_ref[1:2] + jnp.sum(dh1, 0, keepdims=True)
    smalls_ref[at + 2 : at + 5] = small_two_ref[...]
    smalls_ref[at + 5 : at + 7] = small_one_ref[...]
    smalls = smalls_ref[...]
    high = smalls.astype(BF)
    low = (smalls - high.astype(F32)).astype(BF)
    all_ref[:, 3 * span :] = tn(h1, nn(dq, own_columns(rank * span, width, span)).astype(BF))
    chunk = width // n_dp
    blocks = [
        functools.partial(lambda i: all_ref[pl.ds(i * chunk, chunk), :], i) for i in range(n_dp)
    ]
    split_blocks(blocks, DOWN_BIT, meta_ref[2] // DOWN_BIT % 2, kept_out, sent_out)
    shape = (SMALLS, 2 * SMALLS)
    place = iota2(shape, 1) - iota2(shape, 0)
    rest_ref[...] = tn(high, jnp.where(place == 0, 1.0, 0.0).astype(BF)) + tn(
        low, jnp.where(place == SMALLS, 1.0, 0.0).astype(BF)
    )
    seg = (seg_ref[...] + nn(pooled_ref[...], dxp)).astype(BF)
    most = slots_ref[3:4, :lanes]
    which = iota2((NOTES, lanes), 0)
    most = jnp.where(which == 2, most // NOTE_BASE, most % NOTE_BASE).astype(F32)
    chunk = width // n_dp
    base = (width // lanes) * slot_cap
    for i in range(n_dp):
        for j in range(width // lanes):
            send_ref[i, j * slot_cap : (j + 1) * slot_cap, :] = seg[
                i * slot_cap : (i + 1) * slot_cap, j * lanes : (j + 1) * lanes
            ]
        extra = send_ref.shape[1] - NOTES
        tall = extra - base
        if 4 * tall != chunk:
            send_ref[i, base:extra, :] = jnp.zeros((tall, lanes), BF)
        for k in range(4):
            count = min(tall, chunk - k * tall)
            if count > 0:
                send_ref[i, base : base + count, k * 2 * SMALLS : (k + 1) * 2 * SMALLS] = rest_ref[
                    pl.ds(i * chunk + k * tall, count), :
                ].astype(BF)
        digits = digits_ref[:NOTES, i * slot_cap : (i + 1) * slot_cap]
        note = jnp.concatenate([digits, jnp.zeros((NOTES, lanes - slot_cap), F32)], axis=1)
        send_ref[i, extra:, :] = jnp.where(which < 2, note, most).astype(BF)


def send_body(slot_cap, meta_ref, dx_ref, dxp_ref, slots_ref, packed_ref, send_ref, digits_ref):
    n_dp, _, lanes = send_ref.shape
    width = dx_ref.shape[1]
    seq_len = dx_ref.shape[0] // dxp_ref.shape[0]
    seg, digits_ref[...], pooled = slot_sums(
        meta_ref[0], slot_cap, seq_len, slots_ref, packed_ref, dx_ref, n_dp
    )
    seg = (seg + nn(pooled, dxp_ref[...])).astype(BF)
    for i in range(n_dp):
        for j in range(width // lanes):
            send_ref[i, j * slot_cap : (j + 1) * slot_cap, :] = seg[
                i * slot_cap : (i + 1) * slot_cap, j * lanes : (j + 1) * lanes
            ]


def place_rows(row, got_ref, table_ref, slot_cap, lanes):
    n_dp = got_ref.shape[0]
    shape = (table_ref.shape[0], n_dp * slot_cap)
    hit = jnp.where(iota2(shape, 0) == row, 1.0, 0.0).astype(BF)
    for j in range(table_ref.shape[1] // lanes):
        cut = slice(j * slot_cap, (j + 1) * slot_cap)
        rows = jnp.concatenate([got_ref[i, cut, :] for i in range(n_dp)], axis=0)
        table_ref[:, j * lanes : (j + 1) * lanes] = nn(hit, rows)


def place_body(slot_cap, chunk, meta_ref, got_ref, table_ref, rest_ref, most_ref, row_ref):
    lanes = got_ref.shape[2]
    extra = got_ref.shape[1] - NOTES
    most = jnp.zeros((1, 128), F32)
    for i in range(got_ref.shape[0]):
        note = got_ref[i, extra:, :].astype(F32)
        at = slice(i * slot_cap, (i + 1) * slot_cap)
        row_ref[:, at] = note[0:1, :slot_cap] * float(NOTE_BASE) + note[1:2, :slot_cap] - 1.0
        most = jnp.maximum(most, note[2:3, :128] * float(NOTE_BASE) + note[3:4, :128])
    most_ref[...] = most
    place_rows(row_ref[...].astype(I32), got_ref, table_ref, slot_cap, lanes)
    base = table_ref.shape[1] // lanes * slot_cap
    total = got_ref[0, base:extra, :].astype(F32)
    for i in range(1, got_ref.shape[0]):
        total = total + got_ref[i, base:extra, :].astype(F32)
    for k in range(4):
        count = min(extra - base, chunk - k * (extra - base))
        if count > 0:
            cut = slice(k * 2 * SMALLS, k * 2 * SMALLS + SMALLS)
            low = slice(k * 2 * SMALLS + SMALLS, (k + 1) * 2 * SMALLS)
            at = k * (extra - base)
            rest_ref[at : at + count, :] = total[:count, cut] + total[:count, low]


def place_more_body(meta_ref, row_ref, got_ref, old_ref, table_ref):
    lanes = got_ref.shape[2]
    slot_cap = got_ref.shape[1] // (table_ref.shape[1] // lanes)
    place_rows(row_ref[...], got_ref, table_ref, slot_cap, lanes)
    table_ref[...] += old_ref[...]


def on_device(
    token_ids, lengths, images, table, pos_table, ln1_gain, ln1_bias, w_qkv, w_out, b_out,
    ln2_gain, ln2_bias, w_up, b_up, w_down, b_down, w_head,
):
    n_mp, n_dp = lax.axis_size("mp"), lax.axis_size("dp")
    mp_rank, dp_rank = lax.axis_index("mp"), lax.axis_index("dp")
    captions, seq_len = token_ids.shape
    rows = captions * seq_len
    vocab_part, width = table.shape
    heads = width // HEAD_DIM
    own_width = width // n_mp
    ff = w_up.shape[1]
    owner_rows = vocab_part // n_dp
    slot_cap = -(-rows // (n_dp * n_mp * 16)) * 16
    slots = n_dp * slot_cap
    chunk = width // n_dp
    lanes = own_width + 2 * SMALLS
    n_all = captions * n_dp
    blocks = captions // CAP_BLOCK
    meta = jnp.stack([mp_rank, dp_rank * captions, dp_rank]).astype(I32)

    gather = functools.partial(lax.all_gather, axis_name="mp", axis=0)
    turned = jnp.swapaxes(w_qkv, 1, 2)
    shard = jnp.concatenate([turned, w_out[None]])
    image_f = images.astype(F32)
    image_unit = (
        image_f * lax.rsqrt(jnp.sum(image_f * image_f, -1, keepdims=True) + EPS)
    ).astype(BF)
    all_image = lax.all_gather(image_unit, ("dp", "mp"), axis=0, tiled=True)
    at_row = jnp.arange(8)[:, None]
    vecs = b_up.astype(F32)[None, :]
    for k, vec in enumerate((ln1_gain, ln1_bias, b_out, ln2_gain, ln2_bias, b_down)):
        vecs = jnp.where(at_row == k, vec.astype(F32)[None, :], vecs)

    valid = jnp.arange(seq_len)[None, :] < lengths[:, None]
    end_pick = jnp.arange(seq_len)[None, :] == (lengths - 1)[:, None]
    pos_pick = end_pick.astype(BF)
    local2 = token_ids - mp_rank * vocab_part
    owned2 = jnp.logical_and(local2 >= 0, local2 < vocab_part)
    own_pick = jnp.logical_and(end_pick, owned2).astype(BF)
    local = token_ids.reshape(rows) - mp_rank * vocab_part
    local = after(local, image_unit)
    emb = jnp.take(table, jnp.clip(local, 0, vocab_part - 1), axis=0, mode="clip")
    packed = token_ids + jnp.where(valid, VALID_BIT, 0) + jnp.where(end_pick, END_BIT, 0)
    packed = packed.astype(I32).reshape(1, rows)
    per_head = pltpu.VMEM((heads, captions, width), BF)
    per_head = pltpu.VMEM((heads, captions, width), BF)
    row_buffer = pltpu.VMEM((rows, width), BF)
    dma = pltpu.SemaphoreType.DMA
    ends, unit_rows, unit, inverse = vmem_call(
        functools.partial(rows_body, vocab_part),
        [
            ((captions, width), BF),
            ((rows, width), BF, False),
            ((rows, width), BF, False),
            ((rows, 128), F32, False),
        ],
        meta,
        [pos_table, vecs, packed],
        [fetch(emb, blocks)],
        [row_buffer, row_buffer, pltpu.VMEM((rows, 128), F32), dma((3 * blocks,))],
        flops=WORK,
        mib=28,
    )
    shards = everyone(shard, "mp", ends)
    wq, wk, wv, wo = (fetch_weight(shards, k) for k in range(4))
    pay, qk, x0p, q = vmem_call(
        functools.partial(attend_body, vocab_part),
        [
            ((captions, width + 128), BF),
            ((heads, captions, width), BF, False),
            ((captions, width), F32, True),
            ((captions, width), BF, True),
        ],
        meta,
        [gather(ends), pos_pick, pos_table, vecs, packed],
        [wq, wk, fetch(unit_rows, blocks), wv],
        [per_head, per_head, dma((n_mp,))],
        flops=WORK,
        mib=28,
    )
    ctx, lse, x1, u, part = vmem_call(
        hidden_body,
        [
            ((captions, width), F32, True),
            ((captions, width), F32, True),
            ((captions, width), F32, True),
            ((captions, ff), F32, True),
            ((captions, width), BF),
        ],
        meta,
        [gather(pay), vecs],
        [fetch(x0p), wo, fetch(w_up), fetch(w_down)],
        flops=WORK,
        mib=20,
    )
    pooled, proj, powers, sums = vmem_call(
        logits_body,
        [
            ((captions, width), BF, True),
            ((captions, width), F32, True),
            ((captions, n_all), F32, True),
            ((n_dp, 1, n_all + 128), F32),
        ],
        meta,
        [gather(part), vecs],
        [fetch(x1), fetch(w_head), fetch(all_image)],
        flops=WORK * 5,
    )
    all_sums = lax.all_to_all(sums, "dp", 0, 0, tiled=True)
    slot_table = vmem_call(
        functools.partial(slot_body, owner_rows, n_dp),
        [((8, rows), I32)],
        meta,
        [after(packed, sums)],
        flops=WORK * 7,
        mib=20,
    )[0]
    loss, dpooled, part, *halves, small_one = vmem_call(
        loss_body,
        [
            ((1, 128), F32),
            ((captions, width), F32),
            ((captions, width), BF),
            *[((n_dp // 2, chunk, ff + own_width), BF)] * 2,
            *[((n_dp // 2, chunk, ff), BF)] * 2,
            ((2, width), F32),
        ],
        meta,
        [after(all_sums, slot_table), vecs],
        [
            fetch(powers), fetch(all_image), fetch(proj), fetch(w_head), fetch(u), fetch(w_down),
            fetch(w_up), fetch(x1), fetch(pooled),
        ],
        [pltpu.VMEM((width, ff + own_width), F32), pltpu.VMEM((width, ff), F32)],
        flops=WORK * 8,
    )
    dp_bits = bits_of("dp")

    def next_half(total, bits):
        total = halve(total, "dp", bits, bits[0])
        bits.pop(0)
        return total

    one_step = len(dp_bits) == 1
    down = exchange_half(*halves[:2], "dp", DOWN_BIT, one_step)
    up = exchange_half(*halves[2:], "dp", UP_BIT, one_step)
    down_bits = [bit for bit in dp_bits if bit != DOWN_BIT]
    up_bits = [bit for bit in dp_bits if bit != UP_BIT]
    for bit in bits_of("mp"):
        part = part + lax.ppermute(part, "mp", [(i, i ^ bit) for i in range(n_mp)])
    parts = part[None]
    pair_rows = n_mp // 2 * (width + captions)
    dx1, wout, kept, *sent, a, probs, dscores, small_two = vmem_call(
        functools.partial(attend_back_body, vocab_part),
        [
            ((captions, width), F32),
            ((width, own_width), BF),
            ((pair_rows, 2 * own_width), BF),
            *[((pair_rows // 2, 2 * own_width), BF)] * 2,
            ((heads, captions, width), BF),
            ((blocks, heads * CAP_BLOCK, CAP_BLOCK * seq_len), BF),
            ((blocks, heads * CAP_BLOCK, CAP_BLOCK * seq_len), BF),
            ((3, width), F32),
        ],
        meta,
        [parts, packed, vecs, dpooled],
        [
            fetch(x1), fetch(ctx), wo, wv, fetch(lse), fetch(qk, blocks, 1),
            fetch(unit_rows, blocks), wk, fetch(q),
        ],
        [
            per_head, per_head, pltpu.VMEM((n_mp, width, 2 * own_width), BF),
            pltpu.VMEM((captions, width), BF),
        ],
        flops=WORK * 13,
    )
    got = [lax.ppermute(x, "mp", [(i, i ^ 1) for i in range(n_mp)]) for x in sent]
    last_rows = pair_rows - width
    kept, sent = vmem_call(
        between_body, [((last_rows, 2 * own_width), BF)] * 2, meta, [kept, *got], flops=WORK * 2, mib=12
    )
    got = lax.ppermute(sent, "mp", [(i, i ^ 2) for i in range(n_mp)])
    dx, pos_one, small_three, seg, digits, pooled_slots = vmem_call(
        functools.partial(rows_back_body, slot_cap),
        [
            ((rows, width), BF, False),
            ((seq_len, width), F32),
            ((2, width), F32),
            ((slots, width), F32),
            ((16, slots), F32),
            ((slots, captions), BF),
        ],
        meta,
        [after(probs, sent), dscores, a, vecs, slot_table, packed],
        [fetch(qk, blocks, 1), fetch(unit, blocks), fetch(inverse, blocks)],
        [row_buffer, dma((blocks,))],
        flops=WORK * 12,
        mib=32,
    )
    down, up = next_half(down, down_bits), next_half(up, up_bits)
    rest_rows = -(-chunk // 32) * 8
    send_rows = width // lanes * slot_cap
    dxp, send, kept, sent = vmem_call(
        functools.partial(query_back_body, n_mp),
        [
            ((captions, width), BF),
            ((n_dp, send_rows + rest_rows + NOTES, lanes), BF),
            *[((n_dp // 2, chunk, 4 * own_width), BF)] * 2,
        ],
        meta,
        [
            kept, got, wout, dx1, vecs, pos_pick, own_pick, slot_table, seg, digits, pooled_slots, pos_one,
            small_one, small_two, small_three,
        ],
        [fetch(x0p), wq],
        [
            pltpu.VMEM((width, 2 * SMALLS), F32), pltpu.VMEM((SMALLS, width), F32),
            pltpu.VMEM((width, 4 * own_width), F32),
        ],
        flops=WORK * 4,
        mib=24,
    )
    got = lax.all_to_all(send, "dp", 0, 0, tiled=True)
    wkvo = exchange_half(kept, sent, "dp", DOWN_BIT, one_step)
    bits = [bit for bit in dp_bits if bit != DOWN_BIT]
    while len(bits) > 1:
        wkvo = next_half(wkvo, bits)
    while down_bits:
        down = next_half(down, down_bits)
    while up_bits:
        up = next_half(up, up_bits)
    down, up = lax.optimization_barrier((down[0], up[0]))
    table_grad, rest, most_all = vmem_call(
        functools.partial(place_body, slot_cap, chunk),
        [((owner_rows, width), F32), ((chunk, SMALLS), F32), ((1, 128), F32)],
        meta,
        [got],
        (),
        [pltpu.VMEM((1, slots), F32)],
        flops=WORK * 3,
        mib=20,
    )
    most_all = most_all[0, 0].astype(I32)
    small = rest
    last = gather(jnp.concatenate([down[:, ff:], small, jnp.zeros_like(small)], 1))
    wkvo = lax.optimization_barrier(next_half(wkvo, bits)[0])

    def another(carry):
        turn, total = carry
        sent, digits = vmem_call(
            functools.partial(send_body, slot_cap),
            [((n_dp, send_rows, lanes), BF), ((16, slots), F32)],
            turn.reshape(1),
            [dx, dxp, slot_table, packed],
        )
        row = (digits[0] * NOTE_BASE + digits[1] - 1.0).astype(I32)
        row = lax.all_to_all(row.reshape(n_dp, slot_cap), "dp", 0, 0, tiled=True)
        sent = lax.all_to_all(sent, "dp", 0, 0, tiled=True)
        total = vmem_call(
            place_more_body,
            [((owner_rows, width), F32)],
            meta,
            [row.reshape(1, slots), sent, total],
        )[0]
        return turn + 1, total

    _, table_grad = lax.while_loop(
        lambda carry: carry[0] * slot_cap < most_all, another, (jnp.int32(1), table_grad)
    )
    w_head_grad = jnp.swapaxes(last[:, :, :own_width], 0, 1).reshape(chunk, width)
    shared = jnp.sum(last[:, :, own_width : own_width + SMALLS], 0)
    qkv_grad = jnp.stack(
        [wkvo[:, k * own_width : (k + 1) * own_width] for k in (3, 0, 1)]
    )
    return (
        loss[0, 0],
        table_grad,
        shared[:, :seq_len].T,
        shared[:, seq_len],
        shared[:, seq_len + 1],
        qkv_grad,
        wkvo[:, 2 * own_width : 3 * own_width].T,
        small[:, seq_len + 4],
        small[:, seq_len + 2],
        small[:, seq_len + 3],
        up,
        small[:, seq_len + 6],
        down[:, :ff].T,
        small[:, seq_len + 5],
        w_head_grad,
    )


def solution(mesh):
    placed = (
        P("dp", None),
        P("dp"),
        P(("dp", "mp"), None),
        P("mp", None),
        P(),
        P(),
        P(),
        P(None, None, "mp"),
        P("mp", None),
        P(),
        P(),
        P(),
        P(None, "mp"),
        P("mp"),
        P("mp", None),
        P(),
        P(),
    )
    return jax.shard_map(
        on_device,
        mesh=mesh,
        in_specs=placed,
        out_specs=(
            P(),
            P(("mp", "dp"), None),
            P(None, "dp"),
            P("dp"),
            P("dp"),
            P(None, "dp", "mp"),
            P("mp", "dp"),
            P("dp"),
            P("dp"),
            P("dp"),
            P("dp", "mp"),
            P(("mp", "dp")),
            P("mp", "dp"),
            P("dp"),
            P("dp", None),
        ),
        check_vma=False,
    )
```

profile of v0, /device:TPU:0, one launch (start us, length us, event | category | flops | bytes accessed | tf_op | source)
XLA Modules:
  0.0 237.1 jit_solution(10441029961739662374)
XLA Ops:
  7.3 1.4 pad_maximum_fusion.refs_5_.refs_9_.refs_14_.refs_3_.refs_6_.refs_10_.refs_17_.refs_16_
  8.7 3.0 %collective-permute-start.1 = (bf16[4,192,768]{2,1,0:T(8,128)(2,1)S(1)}, bf16[4,192,768]{2,1,0:T(8,128)(2,1)S(1)}, u32[]{:S(2)}, u32[]{:S(2)}) collective-permute-start(bf16[4,192,768]{2,1,0:T(8,128)(2,1)S(1)} %pad_maximum_fusion.refs_5_.refs_9_.refs_14_.refs_3_.refs_6_.refs_10_.refs_17_.refs_16_), channel_id=1, source_target_pairs={{0,2},{1,3},{2,0},{3,1},{4,6},{5,7},{6,4},{7,5},{8,10},{9,11},{10,... | collective-permute-start | bytes 3538952 | tf_op jit(solution)/shard_map/ppermute | solution.py:213
  11.9 0.7 fusion.4
  13.3 16.2 %gather_fusion = bf16[2048,768]{1,0:T(8,128)(2,1)} fusion(bf16[8000,768]{1,0:T(8,128)(2,1)} %param.22, s32[2048]{0:T(1024)S(1)} %clamp_clamp_fusion), kind=kCustom, calls=%fused_computation | custom fusion | bytes 6299648 | tf_op jit(solution)/shard_map/jit(_take)/gather | solution.py:885
  29.7 5.5 %shard_map.280 = (bf16[128,768]{1,0:T(8,128)(2,1)S(1)}, bf16[2048,768]{1,0:T(8,128)(2,1)}, bf16[2048,768]{1,0:T(8,128)(2,1)}, f32[2048,128]{1,0:T(8,128)}) custom-call(s32[3]{0:T(128)S(1)} %pad_add_fusion.meta_ref, bf16[16,768]{1,0:T(8,128)(2,1)S(1)} %copy-done, f32[8,768]{1,0:T(8,128)S(1)} %select_select_fusion.refs_1_.refs_3_.refs_2_.refs_4_, ...), custom_call_target="tpu_custom_call" | custom-call | flops 920000000 | bytes 1 | tf_op jit(solution)/shard_map/pallas_call | solution.py:149
  35.2 2.9 %collective-permute-done.1.refs_7_.refs_11_.refs_16_.refs_5_.refs_8_.refs_12_.refs_19_.refs_18_ = bf16[4,192,768]{2,1,0:T(8,128)(2,1)S(1)} collective-permute-done((bf16[4,192,768]{2,1,0:T(8,128)(2,1)S(1)}, bf16[4,192,768]{2,1,0:T(8,128)(2,1)S(1)}, u32[]{:S(2)}, u32[]{:S(2)}) %collective-permute-start.1) | collective-permute-done | bytes 1179680 | tf_op jit(solution)/shard_map/ppermute | solution.py:213
  38.1 9.6 %all-gather = bf16[512,768]{1,0:T(8,128)(2,1)S(1)} all-gather(bf16[128,768]{1,0:T(8,128)(2,1)S(1)} %get-tuple-element.171), channel_id=2, replica_groups=mesh['dp'=8,'mp'=4] {'mp'}, dimensions={0}, use_global_device_ids=true | all-gather | bytes 983040 | tf_op jit(solution)/shard_map/all_gather | solution.py:918
  47.7 1.1 copy-done.3
  48.8 7.4 %shard_map.281 = (bf16[128,896]{1,0:T(8,128)(2,1)S(1)}, bf16[12,128,768]{2,1,0:T(8,128)(2,1)}, f32[128,768]{1,0:T(8,128)}, bf16[128,768]{1,0:T(8,128)(2,1)}) custom-call(s32[3]{0:T(128)S(1)} %pad_add_fusion.meta_ref, bf16[4,128,768]{2,1,0:T(8,128)(2,1)S(1)} %bitcast.63, bf16[128,16]{1,0:T(8,128)(2,1)S(1)} %get-tuple-element.318.refs_1_.refs_5_, ...), custom_call_target="tpu_custom_call" | custom-call | flops 920000000 | bytes 1 | tf_op jit(solution)/shard_map/pallas_call | solution.py:149
  56.2 20.3 %all-gather.1 = bf16[512,896]{1,0:T(8,128)(2,1)S(1)} all-gather(bf16[128,896]{1,0:T(8,128)(2,1)S(1)} %get-tuple-element.174), channel_id=3, replica_groups=mesh['dp'=8,'mp'=4] {'mp'}, dimensions={0}, use_global_device_ids=true | all-gather | bytes 1146880 | tf_op jit(solution)/shard_map/all_gather | solution.py:934
  76.5 4.1 %shard_map.282 = (f32[128,768]{1,0:T(8,128)}, f32[128,768]{1,0:T(8,128)}, f32[128,768]{1,0:T(8,128)}, f32[128,768]{1,0:T(8,128)}, bf16[128,768]{1,0:T(8,128)(2,1)S(1)}) custom-call(s32[3]{0:T(128)S(1)} %pad_add_fusion.meta_ref, bf16[4,128,896]{2,1,0:T(8,128)(2,1)S(1)} %bitcast.62, f32[8,768]{1,0:T(8,128)S(1)} %select_select_fusion.refs_1_.refs_3_.refs_2_.refs_4_, ...), custom_call_target="tpu_custom_call" | custom-call | flops 920000000 | bytes 1 | tf_op jit(solution)/shard_map/pallas_call | solution.py:149
  80.6 8.7 %all-gather.2 = bf16[512,768]{1,0:T(8,128)(2,1)S(1)} all-gather(bf16[128,768]{1,0:T(8,128)(2,1)S(1)} %get-tuple-element.176), channel_id=4, replica_groups=mesh['dp'=8,'mp'=4] {'mp'}, dimensions={0}, use_global_device_ids=true | all-gather | bytes 983040 | tf_op jit(solution)/shard_map/all_gather | solution.py:948
  89.3 4.6 %shard_map.283 = (bf16[128,768]{1,0:T(8,128)(2,1)}, f32[128,768]{1,0:T(8,128)}, f32[128,1024]{1,0:T(8,128)}, f32[8,1,1152]{2,1,0:T(1,128)}) custom-call(s32[3]{0:T(128)S(1)} %pad_add_fusion.meta_ref, bf16[4,128,768]{2,1,0:T(8,128)(2,1)S(1)} %bitcast.64, f32[8,768]{1,0:T(8,128)S(1)} %select_select_fusion.refs_1_.refs_3_.refs_2_.refs_4_, ...), custom_call_target="tpu_custom_call" | custom-call | flops 4600000000 | bytes 1 | tf_op jit(solution)/shard_map/pallas_call | solution.py:149
  93.9 5.5 %all-to-all-start.2 = ((f32[8,1,1152]{2,1,0:T(1,128)}), f32[8,1,1152]{2,1,0:T(1,128)S(1)}, u32[]{:S(2)}, u32[]{:S(2)}) async-start(f32[8,1,1152]{2,1,0:T(1,128)} %get-tuple-element.178), calls=%async_computation.2 | async-start | bytes 73728 | tf_op jit(solution)/shard_map/all_to_all | solution.py:952
  99.5 7.0 %shard_map.284.refs_4_.refs_7_ = s32[8,2048]{1,0:T(8,128)S(1)} custom-call(s32[3]{0:T(128)S(1)} %pad_add_fusion.meta_ref, s32[1,2048]{1,0:T(1,128)S(1)} %reshape.201.refs_2_.refs_4_.refs_0_.refs_1_.refs_5_), custom_call_target="tpu_custom_call" | custom-call | flops 6440000000 | bytes 1 | tf_op jit(solution)/shard_map/pallas_call | solution.py:149
  106.5 7.2 %shard_map.285 = (f32[1,128]{1,0:T(1,128)}, f32[128,768]{1,0:T(8,128)S(1)}, bf16[128,768]{1,0:T(8,128)(2,1)S(1)}, bf16[4,96,960]{2,1,0:T(8,128)(2,1)S(1)}, bf16[...) custom-call(s32[3]{0:T(128)S(1)} %pad_add_fusion.meta_ref, ...), custom_call_target="tpu_custom_call" | custom-call | flops 7360000000 | bytes 1 | tf_op jit(solution)/shard_map/pallas_call | solution.py:149
  113.9 1.4 collective-permute-done.3
  115.2 0.7 add.136
  115.9 1.3 collective-permute-start.4
  117.9 2.0 collective-permute-start.11
  119.9 1.5 collective-permute-start.8
  121.4 1.9 collective-permute-done.4
  123.2 1.0 add_bitcast_fusion.3.refs_0_
  124.3 11.4 %shard_map.286 = (f32[128,768]{1,0:T(8,128)S(1)}, bf16[768,192]{1,0:T(8,128)(2,1)S(1)}, bf16[1792,384]{1,0:T(8,128)(2,1)S(1)}, bf16[896,384]{1,0:T(8,128)(2,1)S(...) custom-call(s32[3]{0:T(128)S(1)} %pad_add_fusion.meta_ref, ...), custom_call_target="tpu_custom_call" | custom-call | flops 11960000512 | bytes 1 | tf_op jit(solution)/shard_map/pallas_call | solution.py:149
  136.4 2.1 collective-permute-start.12
  139.3 1.1 collective-permute-start.9
  140.4 1.0 shard_map.287
  141.4 1.3 collective-permute-start.7
  142.8 12.6 %shard_map.288 = (bf16[2048,768]{1,0:T(8,128)(2,1)}, f32[16,768]{1,0:T(8,128)S(1)}, f32[2,768]{1,0:T(2,128)S(1)}, f32[512,768]{1,0:T(8,128)S(1)}, f32[16,512]{1,0:T(8,128)S(1)}, /*index=5*/bf16[512,128]{1,0:T(8,128)(2,1)S(1)}) custom-call(s32[3]{0:T(128)S(1)} %pad_add_fusion.meta_ref, bf16[8,192,256]{2,1,0:T(8,128)(2,1)S(1)} %get-tuple-element.200.refs_0_, ...), custom_call_target="tpu_custom_call" | custom-call | flops 11040000000 | bytes 1 | tf_op jit(solution)/shard_map/pallas_call | solution.py:149
  155.4 5.1 %collective-permute-done.7.refs_1_ = bf16[1024,384]{1,0:T(8,128)(2,1)S(1)} collective-permute-done((bf16[1024,384]{1,0:T(8,128)(2,1)S(1)}, bf16[1024,384]{1,0:T(8,128)(2,1)S(1)}, u32[]{:S(2)}, u32[]{:S(2)}) %collective-permute-start.7) | collective-permute-done | bytes 786464 | tf_op jit(solution)/shard_map/ppermute | solution.py:1025
  160.4 4.4 %shard_map.289 = (bf16[128,768]{1,0:T(8,128)(2,1)S(1)}, bf16[8,224,256]{2,1,0:T(8,128)(2,1)}, bf16[4,96,768]{2,1,0:T(8,128)(2,1)S(1)}, bf16[4,96,768]{2,1,0:T(8,128)(2,1)S(1)}) custom-call(s32[3]{0:T(128)S(1)} %pad_add_fusion.meta_ref, bf16[1024,384]{1,0:T(8,128)(2,1)S(1)} %get-tuple-element.195.refs_0_, ...), custom_call_target="tpu_custom_call" | custom-call | flops 3680000000 | bytes 1 | tf_op jit(solution)/shard_map/pallas_call | solution.py:149
  164.9 1.2 collective-permute-start.14
  166.2 2.4 %collective-permute-start.13 = (bf16[1,96,768]{2,1,0:T(8,128)(2,1)S(1)}, bf16[1,96,768]{2,1,0:T(8,128)(2,1)S(1)}, u32[]{:S(2)}, u32[]{:S(2)}) collective-permute-start(bf16[1,96,768]{2,1,0:T(8,128)(2,1)S(1)} %constant_dynamic-slice_fusion.3), channel_id=1, source_target_pairs={{0,16},{4,20},{8,24},{12,28},{16,0},{20,4},{24,8},{28,12},{1,17},{... | collective-permute-start | bytes 442376 | tf_op jit(solution)/shard_map/ppermute | solution.py:172
  169.4 9.3 %collective-permute-done.14 = bf16[4,96,768]{2,1,0:T(8,128)(2,1)S(1)} collective-permute-done((bf16[4,96,768]{2,1,0:T(8,128)(2,1)S(1)}, bf16[4,96,768]{2,1,0:T(8,128)(2,1)S(1)}, u32[]{:S(2)}, u32[]{:S(2)}) %collective-permute-start.14) | collective-permute-done | bytes 589856 | tf_op jit(solution)/shard_map/ppermute | solution.py:172
  179.2 1.3 collective-permute-start.15
  180.5 4.5 %all-to-all-start.3 = ((bf16[8,224,256]{2,1,0:T(8,128)(2,1)}), bf16[8,224,256]{2,1,0:T(8,128)(2,1)S(1)}, u32[]{:S(2)}, u32[]{:S(2)}) async-start(bf16[8,224,256]{2,1,0:T(8,128)(2,1)} %get-tuple-element.212), calls=%async_computation.3 | async-start | bytes 1835008 | tf_op jit(solution)/shard_map/all_to_all | solution.py:1066
  185.1 0.8 add_bitcast_fusion.2
  185.8 1.0 add_bitcast_fusion.1
  187.0 10.8 %collective-permute-done.15 = bf16[2,96,768]{1,2,0:T(8,128)(2,1)} collective-permute-done((bf16[2,96,768]{1,2,0:T(8,128)(2,1)S(1)}, bf16[2,96,768]{1,2,0:T(8,128)(2,1)}, u32[]{:S(2)}, u32[]{:S(2)}) %collective-permute-start.15) | collective-permute-done | bytes 294944 | tf_op jit(solution)/shard_map/ppermute | solution.py:172
  197.8 1.1 fusion
  198.9 2.7 %collective-permute-start.16 = (bf16[1,96,768]{1,2,0:T(8,128)(2,1)S(1)}, bf16[1,96,768]{1,2,0:T(8,128)(2,1)S(1)}, u32[]{:S(2)}, u32[]{:S(2)}) collective-permute-start(bf16[1,96,768]{1,2,0:T(8,128)(2,1)S(1)} %constant_dynamic-slice_fusion), channel_id=1, source_target_pairs={{0,16},{4,20},{8,24},{12,28},{16,0},{20,4},{24,8},{28,12},{1,17},{... | collective-permute-start | bytes 442376 | tf_op jit(solution)/shard_map/ppermute | solution.py:172
  201.7 0.7 slice_bitcast_fusion.1
  202.4 11.8 %collective-permute-done.16 = bf16[1,96,768]{1,2,0:T(8,128)(2,1)S(1)} collective-permute-done((bf16[1,96,768]{1,2,0:T(8,128)(2,1)S(1)}, bf16[1,96,768]{1,2,0:T(8,128)(2,1)S(1)}, u32[]{:S(2)}, u32[]{:S(2)}) %collective-permute-start.16) | collective-permute-done | bytes 147488 | tf_op jit(solution)/shard_map/ppermute | solution.py:172
  215.0 0.9 copy.67
  215.8 3.2 %shard_map.290 = (f32[1000,768]{1,0:T(8,128)}, f32[96,32]{1,0:T(8,128)S(1)}, f32[1,128]{1,0:T(1,128)S(1)}) custom-call(s32[3]{0:T(128)S(1)} %copy-done.9, bf16[8,224,256]{2,1,0:T(8,128)(2,1)S(1)} %all-to-all-done.3.refs_0_), custom_call_target="tpu_custom_call" | custom-call | flops 2760000000 | bytes 1 | tf_op jit(solution)/shard_map/pallas_call | solution.py:149
  219.1 0.8 slice_reduce_fusion.3
  220.0 7.3 %all-gather.3 = f32[384,256]{1,0:T(8,128)S(1)} all-gather(f32[96,256]{1,0:T(8,128)S(1)} %maximum_maximum_fusion), channel_id=5, replica_groups=mesh['dp'=8,'mp'=4] {'mp'}, dimensions={0}, use_global_device_ids=true | all-gather | bytes 491520 | tf_op jit(solution)/shard_map/all_gather | solution.py:1088
  228.4 1.0 reshape.208
  (109 shorter events, 7.4 us)
Async XLA Ops:
  7.2 4.5 %copy-start.7 = (bf16[32,768]{1,0:T(8,128)(2,1)S(1)}, bf16[32,768]{1,0:T(8,128)(2,1)}, u32[]{:S(2)}) copy-start(bf16[32,768]{1,0:T(8,128)(2,1)} %param.21) | copy-start | bytes 147460
  7.2 5.4 %copy-start.19 = (s32[128]{0:T(128)S(1)}, s32[128]{0:T(128)}, u32[]{:S(2)}) copy-start(s32[128]{0:T(128)} %param.20) | copy-start | bytes 1540
  7.2 5.4 %copy-start.10 = (s32[128,16]{0,1:T(8,128)S(1)}, s32[128,16]{0,1:T(8,128)}, u32[]{:S(2)}) copy-start(s32[128,16]{0,1:T(8,128)} %param.19) | copy-start | bytes 24580
  7.2 5.7 %copy-start.12 = (bf16[768]{0:T(1024)(128)(2,1)S(1)}, bf16[768]{0:T(1024)(128)(2,1)}, u32[]{:S(2)}) copy-start(bf16[768]{0:T(1024)(128)(2,1)} %param.24) | copy-start | bytes 4612
  7.2 5.7 %copy-start.13 = (bf16[768]{0:T(1024)(128)(2,1)S(1)}, bf16[768]{0:T(1024)(128)(2,1)}, u32[]{:S(2)}) copy-start(bf16[768]{0:T(1024)(128)(2,1)} %param.25) | copy-start | bytes 4612
  7.2 5.7 %copy-start.14 = (bf16[768]{0:T(1024)(128)(2,1)S(1)}, bf16[768]{0:T(1024)(128)(2,1)}, u32[]{:S(2)}) copy-start(bf16[768]{0:T(1024)(128)(2,1)} %param.28) | copy-start | bytes 4612
  7.2 5.8 %copy-start.15 = (bf16[768]{0:T(1024)(128)(2,1)S(1)}, bf16[768]{0:T(1024)(128)(2,1)}, u32[]{:S(2)}) copy-start(bf16[768]{0:T(1024)(128)(2,1)} %param.29) | copy-start | bytes 4612
  7.3 5.8 %copy-start.16 = (bf16[768]{0:T(1024)(128)(2,1)S(1)}, bf16[768]{0:T(1024)(128)(2,1)}, u32[]{:S(2)}) copy-start(bf16[768]{0:T(1024)(128)(2,1)} %param.30) | copy-start | bytes 4612
  7.3 5.8 %copy-start.17 = (bf16[768]{0:T(1024)(128)(2,1)S(1)}, bf16[768]{0:T(1024)(128)(2,1)}, u32[]{:S(2)}) copy-start(bf16[768]{0:T(1024)(128)(2,1)} %param.32) | copy-start | bytes 4612
  7.3 5.8 %copy-start.18 = (bf16[768]{0:T(1024)(128)(2,1)S(1)}, bf16[768]{0:T(1024)(128)(2,1)}, u32[]{:S(2)}) copy-start(bf16[768]{0:T(1024)(128)(2,1)} %param.34) | copy-start | bytes 4612
  7.3 82.0 %all-gather.6.cloned.1.call-start = ((), (), s32[]{:S(2)}) async-start(), calls=%async_computation.4 | async-start | bytes 1622016 | tf_op jit(solution)/shard_map/all_gather | solution.py:871
  8.7 20.8 %copy-start.1 = (bf16[4,192,768]{2,1,0:T(8,128)(2,1)}, bf16[4,192,768]{2,1,0:T(8,128)(2,1)S(1)}, u32[]{:S(2)}) copy-start(bf16[4,192,768]{2,1,0:T(8,128)(2,1)S(1)} %pad_maximum_fusion.refs_5_.refs_9_.refs_14_.refs_3_.refs_6_.refs_10_.refs_17_.refs_16_) | copy-start | bytes 3538948
  8.7 29.3 %collective-permute-start.1 = (bf16[4,192,768]{2,1,0:T(8,128)(2,1)S(1)}, bf16[4,192,768]{2,1,0:T(8,128)(2,1)S(1)}, u32[]{:S(2)}, u32[]{:S(2)}) collective-permute-start(bf16[4,192,768]{2,1,0:T(8,128)(2,1)S(1)} %pad_maximum_fusion.refs_5_.refs_9_.refs_14_.refs_3_.refs_6_.refs_10_.refs_17_.refs_16_), channel_id=1, source_target_pairs={{0,2},{1,3},{2,0},{3,1},{4,6},{5,7},{6,4},{7,5},{8,10},{9,11},{10,... | collective-permute-start | bytes 3538952 | tf_op jit(solution)/shard_map/ppermute | solution.py:213
  11.7 36.0 %collective-permute-start = (bf16[4,192,768]{2,1,0:T(8,128)(2,1)S(1)}, bf16[4,192,768]{2,1,0:T(8,128)(2,1)}, u32[]{:S(2)}, u32[]{:S(2)}) collective-permute-start(bf16[4,192,768]{2,1,0:T(8,128)(2,1)S(1)} %pad_maximum_fusion.refs_5_.refs_9_.refs_14_.refs_3_.refs_6_.refs_10_.refs_17_.refs_16_), channel_id=1, source_target_pairs={{0,1},{1,0},{2,3},{3,2},{4,5},{5,4},{6,7},{7,6},{8,9},{9,8},{10,11... | collective-permute-start | bytes 3538952 | tf_op jit(solution)/shard_map/ppermute | solution.py:213
  13.3 16.4 %copy-start = (bf16[16,768]{1,0:T(8,128)(2,1)S(1)}, bf16[16,768]{1,0:T(8,128)(2,1)}, u32[]{:S(2)}) copy-start(bf16[16,768]{1,0:T(8,128)(2,1)} %refs_2_.1) | copy-start | bytes 73732
  29.6 130.9 %copy-start.8 = (s32[3]{0:T(128)}, s32[3]{0:T(128)S(1)}, u32[]{:S(2)}) copy-start(s32[3]{0:T(128)S(1)} %pad_add_fusion.meta_ref) | copy-start | bytes 40
  38.0 9.7 %copy-start.2 = (bf16[4,192,768]{2,1,0:T(8,128)(2,1)}, bf16[4,192,768]{2,1,0:T(8,128)(2,1)S(1)}, u32[]{:S(2)}) copy-start(bf16[4,192,768]{2,1,0:T(8,128)(2,1)S(1)} %collective-permute-done.1.refs_7_.refs_11_.refs_16_.refs_5_.refs_8_.refs_12_.refs_19_.refs_18_) | copy-start | bytes 3538948
  38.0 9.6 %collective-permute-start.2 = (bf16[4,192,768]{2,1,0:T(8,128)(2,1)S(1)}, bf16[4,192,768]{2,1,0:T(8,128)(2,1)S(1)}, u32[]{:S(2)}, u32[]{:S(2)}) collective-permute-start(bf16[4,192,768]{2,1,0:T(8,128)(2,1)S(1)} %collective-permute-done.1.refs_7_.refs_11_.refs_16_.refs_5_.refs_8_.refs_12_.refs_19_.refs_18_), channel_id=1, source_target_pairs={{0,1},{1,0},{2,3},{3,2},{4,5},{5,4},{6,7},{7,6},{8,9},{9,8},{10,11... | collective-permute-start | bytes 3538952 | tf_op jit(solution)/shard_map/ppermute | solution.py:213
  47.7 1.1 copy-start.3
  93.9 12.6 %all-to-all-start.2 = ((f32[8,1,1152]{2,1,0:T(1,128)}), f32[8,1,1152]{2,1,0:T(1,128)S(1)}, u32[]{:S(2)}, u32[]{:S(2)}) async-start(f32[8,1,1152]{2,1,0:T(1,128)} %get-tuple-element.178), calls=%async_computation.2 | async-start | bytes 73728 | tf_op jit(solution)/shard_map/all_to_all | solution.py:952
  113.7 1.5 collective-permute-start.3
  115.9 7.3 %collective-permute-start.4 = (bf16[128,768]{1,0:T(8,128)(2,1)}, bf16[128,768]{1,0:T(8,128)(2,1)}, u32[]{:S(2)}, u32[]{:S(2)}) collective-permute-start(bf16[128,768]{1,0:T(8,128)(2,1)} %add.136), channel_id=1, source_target_pairs={{0,2},{1,3},{2,0},{3,1},{4,6},{5,7},{6,4},{7,5},{8,10},{9,11},{10,... | collective-permute-start | bytes 589832 | tf_op jit(solution)/shard_map/ppermute | solution.py:993
  117.9 18.4 %collective-permute-start.11 = (bf16[4,96,768]{2,1,0:T(8,128)(2,1)S(1)}, bf16[4,96,768]{2,1,0:T(8,128)(2,1)S(1)}, u32[]{:S(2)}, u32[]{:S(2)}) collective-permute-start(bf16[4,96,768]{2,1,0:T(8,128)(2,1)S(1)} %get-tuple-element.221), channel_id=1, source_target_pairs={{0,8},{4,12},{8,0},{12,4},{16,24},{20,28},{24,16},{28,20},{1,9},{5... | collective-permute-start | bytes 1769480 | tf_op jit(solution)/shard_map/ppermute | solution.py:172
  119.9 19.0 %collective-permute-start.8 = (bf16[4,96,960]{2,1,0:T(8,128)(2,1)S(1)}, bf16[4,96,960]{2,1,0:T(8,128)(2,1)S(1)}, u32[]{:S(2)}, u32[]{:S(2)}) collective-permute-start(bf16[4,96,960]{2,1,0:T(8,128)(2,1)S(1)} %get-tuple-element.219), channel_id=1, source_target_pairs={{0,4},{4,0},{8,12},{12,8},{16,20},{20,16},{24,28},{28,24},{1,5},{5... | collective-permute-start | bytes 2211848 | tf_op jit(solution)/shard_map/ppermute | solution.py:172
  135.6 4.7 %collective-permute-start.5 = (bf16[896,384]{1,0:T(8,128)(2,1)S(1)}, bf16[896,384]{1,0:T(8,128)(2,1)S(1)}, u32[]{:S(2)}, u32[]{:S(2)}) collective-permute-start(bf16[896,384]{1,0:T(8,128)(2,1)S(1)} %get-tuple-element.193), channel_id=1, source_target_pairs={{0,1},{1,0},{2,3},{3,2},{4,5},{5,4},{6,7},{7,6},{8,9},{9,8},{10,11... | collective-permute-start | bytes 2064392 | tf_op jit(solution)/shard_map/ppermute | solution.py:1020
  135.7 4.7 %collective-permute-start.6 = (bf16[896,384]{1,0:T(8,128)(2,1)S(1)}, bf16[896,384]{1,0:T(8,128)(2,1)S(1)}, u32[]{:S(2)}, u32[]{:S(2)}) collective-permute-start(bf16[896,384]{1,0:T(8,128)(2,1)S(1)} %get-tuple-element.194), channel_id=1, source_target_pairs={{0,1},{1,0},{2,3},{3,2},{4,5},{5,4},{6,7},{7,6},{8,9},{9,8},{10,11... | collective-permute-start | bytes 2064392 | tf_op jit(solution)/shard_map/ppermute | solution.py:1020
  136.4 29.6 %collective-permute-start.12 = (bf16[2,96,768]{2,1,0:T(8,128)(2,1)S(1)}, bf16[2,96,768]{2,1,0:T(8,128)(2,1)S(1)}, u32[]{:S(2)}, u32[]{:S(2)}) collective-permute-start(bf16[2,96,768]{2,1,0:T(8,128)(2,1)S(1)} %dynamic-slice_bitcast_fusion.1), channel_id=1, source_target_pairs={{0,4},{4,0},{8,12},{12,8},{16,20},{20,16},{24,28},{28,24},{1,5},{5... | collective-permute-start | bytes 884744 | tf_op jit(solution)/shard_map/ppermute | solution.py:172
  139.3 29.3 %collective-permute-start.9 = (bf16[2,96,960]{2,1,0:T(8,128)(2,1)S(1)}, bf16[2,96,960]{2,1,0:T(8,128)(2,1)S(1)}, u32[]{:S(2)}, u32[]{:S(2)}) collective-permute-start(bf16[2,96,960]{2,1,0:T(8,128)(2,1)S(1)} %dynamic-slice_bitcast_fusion), channel_id=1, source_target_pairs={{0,8},{4,12},{8,0},{12,4},{16,24},{20,28},{24,16},{28,20},{1,9},{5... | collective-permute-start | bytes 1105928 | tf_op jit(solution)/shard_map/ppermute | solution.py:172
  141.4 19.0 %collective-permute-start.7 = (bf16[1024,384]{1,0:T(8,128)(2,1)S(1)}, bf16[1024,384]{1,0:T(8,128)(2,1)S(1)}, u32[]{:S(2)}, u32[]{:S(2)}) collective-permute-start(bf16[1024,384]{1,0:T(8,128)(2,1)S(1)} %get-tuple-element.196), channel_id=1, source_target_pairs={{0,2},{1,3},{2,0},{3,1},{4,6},{5,7},{6,4},{7,5},{8,10},{9,11},{10,... | collective-permute-start | bytes 2359304 | tf_op jit(solution)/shard_map/ppermute | solution.py:1025
  164.9 13.9 %collective-permute-start.14 = (bf16[4,96,768]{2,1,0:T(8,128)(2,1)S(1)}, bf16[4,96,768]{2,1,0:T(8,128)(2,1)S(1)}, u32[]{:S(2)}, u32[]{:S(2)}) collective-permute-start(bf16[4,96,768]{2,1,0:T(8,128)(2,1)S(1)} %get-tuple-element.225), channel_id=1, source_target_pairs={{0,4},{4,0},{8,12},{12,8},{16,20},{20,16},{24,28},{28,24},{1,5},{5... | collective-permute-start | bytes 1769480 | tf_op jit(solution)/shard_map/ppermute | solution.py:172
  166.1 2.5 %copy-start.5 = (bf16[2,96,768]{2,1,0:T(8,128)(2,1)}, bf16[2,96,768]{2,1,0:T(8,128)(2,1)S(1)}, u32[]{:S(2)}) copy-start(bf16[2,96,768]{2,1,0:T(8,128)(2,1)S(1)} %fusion.2) | copy-start | bytes 884740
  166.2 18.9 %collective-permute-start.13 = (bf16[1,96,768]{2,1,0:T(8,128)(2,1)S(1)}, bf16[1,96,768]{2,1,0:T(8,128)(2,1)S(1)}, u32[]{:S(2)}, u32[]{:S(2)}) collective-permute-start(bf16[1,96,768]{2,1,0:T(8,128)(2,1)S(1)} %constant_dynamic-slice_fusion.3), channel_id=1, source_target_pairs={{0,16},{4,20},{8,24},{12,28},{16,0},{20,4},{24,8},{28,12},{1,17},{... | collective-permute-start | bytes 442376 | tf_op jit(solution)/shard_map/ppermute | solution.py:172
  168.8 17.0 %collective-permute-start.10 = (bf16[1,96,960]{2,1,0:T(8,128)(2,1)S(1)}, bf16[1,96,960]{2,1,0:T(8,128)(2,1)}, u32[]{:S(2)}, u32[]{:S(2)}) collective-permute-start(bf16[1,96,960]{2,1,0:T(8,128)(2,1)S(1)} %constant_dynamic-slice_fusion.4), channel_id=1, source_target_pairs={{0,16},{4,20},{8,24},{12,28},{16,0},{20,4},{24,8},{28,12},{1,17},{... | collective-permute-start | bytes 552968 | tf_op jit(solution)/shard_map/ppermute | solution.py:172
  178.9 6.1 %copy-start.6 = (bf16[2,96,768]{2,1,0:T(8,128)(2,1)S(1)}, bf16[2,96,768]{2,1,0:T(8,128)(2,1)}, u32[]{:S(2)}) copy-start(bf16[2,96,768]{2,1,0:T(8,128)(2,1)} %copy-done.5) | copy-start | bytes 884740
  179.2 18.6 %collective-permute-start.15 = (bf16[2,96,768]{1,2,0:T(8,128)(2,1)S(1)}, bf16[2,96,768]{1,2,0:T(8,128)(2,1)}, u32[]{:S(2)}, u32[]{:S(2)}) collective-permute-start(bf16[2,96,768]{1,2,0:T(8,128)(2,1)S(1)} %bitcast.75), channel_id=1, source_target_pairs={{0,8},{4,12},{8,0},{12,4},{16,24},{20,28},{24,16},{28,20},{1,9},{5... | collective-permute-start | bytes 884744 | tf_op jit(solution)/shard_map/ppermute | solution.py:172
  180.5 35.3 %all-to-all-start.3 = ((bf16[8,224,256]{2,1,0:T(8,128)(2,1)}), bf16[8,224,256]{2,1,0:T(8,128)(2,1)S(1)}, u32[]{:S(2)}, u32[]{:S(2)}) async-start(bf16[8,224,256]{2,1,0:T(8,128)(2,1)} %get-tuple-element.212), calls=%async_computation.3 | async-start | bytes 1835008 | tf_op jit(solution)/shard_map/all_to_all | solution.py:1066
  186.8 27.5 %copy-start.4 = (f32[96,960]{1,0:T(8,128)}, f32[96,960]{1,0:T(8,128)S(1)}, u32[]{:S(2)}) copy-start(f32[96,960]{1,0:T(8,128)S(1)} %add_bitcast_fusion.1) | copy-start | bytes 1105924
  198.9 16.9 %copy-start.9 = (s32[3]{0:T(128)S(1)}, s32[3]{0:T(128)}, u32[]{:S(2)}) copy-start(s32[3]{0:T(128)} %copy-done.8) | copy-start | bytes 40
  198.9 15.3 %collective-permute-start.16 = (bf16[1,96,768]{1,2,0:T(8,128)(2,1)S(1)}, bf16[1,96,768]{1,2,0:T(8,128)(2,1)S(1)}, u32[]{:S(2)}, u32[]{:S(2)}) collective-permute-start(bf16[1,96,768]{1,2,0:T(8,128)(2,1)S(1)} %constant_dynamic-slice_fusion), channel_id=1, source_target_pairs={{0,16},{4,20},{8,24},{12,28},{16,0},{20,4},{24,8},{28,12},{1,17},{... | collective-permute-start | bytes 442376 | tf_op jit(solution)/shard_map/ppermute | solution.py:172
  215.8 4.0 %slice-start = ((f32[96,960]{1,0:T(8,128)}), f32[96,192]{1,0:T(8,128)S(1)}, s32[]{:S(2)}) async-start(f32[96,960]{1,0:T(8,128)} %copy-done.4), calls=%async_computation.5 | async-start | bytes 196608 | tf_op jit(solution)/shard_map/slice | solution.py:1088
  215.8 4.0 %copy-start.11 = (f32[256]{0:T(256)S(1)}, f32[256]{0:T(256)}, u32[]{:S(2)}) copy-start(f32[256]{0:T(256)} %pad.5.clone) | copy-start | bytes 3076
Sparse Core Ops, SparseCore 0:
  12.7 56.7 all-gather.5
where the time goes:
time: 240 us; the launch traced here: 237 us
  Pallas kernels  68.4 us (29%)
  blocking collectives  46 us (19%)
  waiting for transfers between devices  43.6 us (18%)
  starting transfers between devices  31.4 us (13%)
  local copies, waits for them, and re-layouts  24.6 us (10%)
  between operations  14.9 us (6%)
  other arithmetic  8.26 us (3%)
    pallas_call x11, Pallas kernels, vmem_call(): pl.pallas_call(kernel, out_shape=[pltpu.HBM(*o[:2]) if len(o) > 2 else ja...  68.4 us
    ppermute x9, waiting for transfers between devices, exchange_half(): got = lax.ppermute(sent, axis, [(i, i ^ bit) for i in range(count)])  32.3 us
    all_gather x1, blocking collectives, on_device(): gather(pay)  20.3 us
    gather x1, local copies, waits for them, and re-layouts, on_device(): jnp.take(table, jnp.clip(local, 0, vocab_part - 1), axis=0, mode='clip')  16.2 us
    ppermute x9, starting transfers between devices, exchange_half(): got = lax.ppermute(sent, axis, [(i, i ^ bit) for i in range(count)])  15 us
    all_gather x1, blocking collectives, on_device(): gather(ends)  9.64 us
    all_gather x1, blocking collectives, on_device(): gather(part)  8.73 us
    all_gather x1, blocking collectives, on_device(): gather(jnp.concatenate([down[:, ff:], small, jnp.zeros_like(small)], 1))  7.29 us
  transfers between devices with their start and end apart: 20, of which 8 were waited for; matrix products, arithmetic and copies ran while one was open for 11% of the time, Pallas kernels for 23%

commit v1 on v0

--- a/solution.py
+++ b/solution.py
@@ -20,6 +20,7 @@
 CAP_BLOCK = 16
 SMALLS = 32
 NOTES = 8
+HALF = 4
 VALID_BIT = 1 << 20
 END_BIT = 1 << 21
 NOTE_BASE = 32
@@ -271,10 +272,14 @@
         copy.start()
         pending.append(copy)
 
-    for block in range(captions // CAP_BLOCK):
+    blocks = captions // CAP_BLOCK
+    for block in range(blocks):
         here = pl.ds(block * block_rows, block_rows)
+        if block % HALF == 0:
+            for k in range(block, min(block + HALF, blocks)):
+                emb.wait(k)
         packed = packed_ref[:, block * block_rows : (block + 1) * block_rows]
-        low = emb.wait(block)[here, :]
+        low = emb.ref[here, :]
         ids, _, is_end = unpack(packed)
         shape = (CAP_BLOCK, block_rows)
         mark = jnp.logical_and(is_end, ids // vocab_part == meta_ref[0])
@@ -283,11 +288,14 @@
         end_ref[block * CAP_BLOCK : (block + 1) * CAP_BLOCK] = ends.astype(BF)
         unit, inverse = normalize(low.astype(F32) + pos)
         unit_ref[here, :] = unit.astype(BF)
-        write_back(unit_ref.at[here], unit_out.at[here])
         inv_ref[here, :] = jnp.broadcast_to(inverse, (block_rows, 128))
-        write_back(inv_ref.at[here], inv_out.at[here])
         rows_ref[here, :] = (unit * gain + bias).astype(BF)
-        write_back(rows_ref.at[here], rows_out.at[here])
+        if block % HALF == HALF - 1 or block == blocks - 1:
+            low_row = block // HALF * HALF * block_rows
+            done = pl.ds(low_row, (block + 1) * block_rows - low_row)
+            write_back(unit_ref.at[done], unit_out.at[done])
+            write_back(inv_ref.at[done], inv_out.at[done])
+            write_back(rows_ref.at[done], rows_out.at[done])
     for copy in pending:
         copy.wait()
 
@@ -427,11 +435,9 @@
 
 
 def loss_body(
-    meta_ref, sums_ref, vec_ref, e, images, proj, wh, u, wdown, wup, x1, pooled,
-    loss_ref, dpooled_ref, part_ref, down_kept, down_sent, up_kept, up_sent, small_ref,
-    down_ref, up_ref,
+    meta_ref, sums_ref, vec_ref, e, images, proj, wh, u, wdown, wup,
+    loss_ref, dpooled_ref, part_ref, du_ref, dproj_ref,
 ):
-    width = dpooled_ref.shape[1]
     sums = jnp.sum(sums_ref[...], 0)
     n_all = sums.shape[1] - 128
     cols = sums[:, :n_all]
@@ -447,25 +453,37 @@
     inv = lax.rsqrt(jnp.sum(proj * proj, -1, keepdims=True) + EPS)
     along = jnp.sum(proj * dtext, -1, keepdims=True)
     dproj = (inv * dtext - inv * inv * inv * proj * along).astype(BF)
+    dproj_ref[...] = dproj
     dpooled = nt(dproj, wh.value())
     dpooled_ref[...] = dpooled
-    dy = dpooled.astype(BF)
     u = u.value()
     th = jnp.tanh(GELU_C * (u + 0.044715 * u * u * u))
     slope = 0.5 * (1.0 + th) + 0.5 * u * (1.0 - th * th) * (
         GELU_C * (1.0 + 3.0 * 0.044715 * u * u)
     )
-    du = (nt(dy, wdown.value()) * slope).astype(BF)
+    du = (nt(dpooled.astype(BF), wdown.value()) * slope).astype(BF)
+    du_ref[...] = du
     part_ref[...] = nt(du, wup.value()).astype(BF)
+
+
+def weights_body(
+    meta_ref, vec_ref, dpooled_ref, du_ref, dproj_ref, u, x1, pooled,
+    down_kept, down_sent, up_kept, up_sent, small_ref, down_ref, up_ref,
+):
+    width = dpooled_ref.shape[1]
+    dy, du, dproj = dpooled_ref[...].astype(BF), du_ref[...], dproj_ref[...]
+    u = u.value()
+    th = jnp.tanh(GELU_C * (u + 0.044715 * u * u * u))
     hidden = (0.5 * u * (1.0 + th)).astype(BF)
     unit, _ = normalize(x1.value())
     h2 = (unit * vec_ref[3:4] + vec_ref[4:5]).astype(BF)
     ff = u.shape[1]
     own_width = down_ref.shape[1] - ff
     pick = own_columns(meta_ref[0] * own_width, width, own_width)
-    down_ref[:, :ff] = tn(dy, hidden)
-    up_ref[...] = tn(h2, du)
-    down_ref[:, ff:] = tn(pooled.value(), nn(dproj, pick).astype(BF))
+    kind = down_ref.dtype
+    down_ref[:, :ff] = tn(dy, hidden).astype(kind)
+    up_ref[...] = tn(h2, du).astype(kind)
+    down_ref[:, ff:] = tn(pooled.value(), nn(dproj, pick).astype(BF)).astype(kind)
     chunk = down_kept.shape[1]
     n_dp = 2 * down_kept.shape[0]
     for ref, bit, kept, sent in (
@@ -679,12 +697,17 @@
     seq_len, width = posg_ref.shape
     block_rows = dx_ref.shape[0] // blocks
     gain = vec_ref[0:1]
-    qk_ref, unit_ref, inv_ref = qk_all.wait(), unit_all.wait(), inv_all.wait()
+    qk_ref, unit_ref, inv_ref = qk_all.ref, unit_all.ref, inv_all.ref
     pending = []
     gain_grad = jnp.zeros((1, width), F32)
     bias_grad = jnp.zeros((1, width), F32)
     pos_grad = jnp.zeros((seq_len, width), F32)
     for block in range(blocks):
+        if block % HALF == 0:
+            for k in range(block, min(block + HALF, blocks)):
+                qk_all.wait(k)
+                unit_all.wait(k)
+                inv_all.wait(k)
         caps = pl.ds(block * CAP_BLOCK, CAP_BLOCK)
         here = pl.ds(block * block_rows, block_rows)
         a = a_ref[:, caps, :].reshape(heads * CAP_BLOCK, width)
@@ -958,24 +981,37 @@
         flops=WORK * 7,
         mib=20,
     )[0]
-    loss, dpooled, part, *halves, small_one = vmem_call(
+    loss, dpooled, part, du, dproj = vmem_call(
         loss_body,
         [
             ((1, 128), F32),
             ((captions, width), F32),
             ((captions, width), BF),
+            ((captions, ff), BF),
+            ((captions, width), BF),
+        ],
+        meta,
+        [after(all_sums, slot_table), vecs],
+        [
+            fetch(powers), fetch(all_image), fetch(proj), fetch(w_head), fetch(u), fetch(w_down),
+            fetch(w_up),
+        ],
+        flops=WORK * 5,
+    )
+    kind = BF if chunk % 16 == 0 else F32
+    *halves, small_one = vmem_call(
+        weights_body,
+        [
             *[((n_dp // 2, chunk, ff + own_width), BF)] * 2,
             *[((n_dp // 2, chunk, ff), BF)] * 2,
             ((2, width), F32),
         ],
         meta,
-        [after(all_sums, slot_table), vecs],
-        [
-            fetch(powers), fetch(all_image), fetch(proj), fetch(w_head), fetch(u), fetch(w_down),
-            fetch(w_up), fetch(x1), fetch(pooled),
-        ],
-        [pltpu.VMEM((width, ff + own_width), F32), pltpu.VMEM((width, ff), F32)],
-        flops=WORK * 8,
+        [vecs, dpooled, du, dproj],
+        [fetch(u), fetch(x1), fetch(pooled)],
+        [pltpu.VMEM((width, ff + own_width), kind), pltpu.VMEM((width, ff), kind)],
+        flops=WORK * 4,
+        mib=24,
     )
     dp_bits = bits_of("dp")
 

time: 240 us -> 232 us (0.967)
  starting transfers between devices: 31.4 us -> 26.5 us
  Pallas kernels: 68.4 us -> 70.9 us
    ppermute x9, starting transfers between devices: 15 us -> 10.5 us  [exchange_half(): got = lax.ppermute(sent, axis, [(i, i ^ bit) for i in range(count)])]
    pallas_call x11 -> x12, Pallas kernels: 68.4 us -> 70.9 us  [vmem_call(): pl.pallas_call(kernel, out_shape=[pltpu.HBM(*o[:2]) if len(o) > 2 else ja...]
    ppermute x9, waiting for transfers between devices: 32.3 us -> 34.8 us  [exchange_half(): got = lax.ppermute(sent, axis, [(i, i ^ bit) for i in range(count)])]
  transfers between devices with their start and end apart: 20 -> 20, of which waited for: 8 -> 7; matrix products, arithmetic and copies ran while one was open for 11% -> 11% of each run, Pallas kernels for 23% -> 25%
where the time goes in v1:
time: 232 us; the launch traced here: 230 us
  Pallas kernels  70.9 us (31%)
  blocking collectives  44.8 us (19%)
  waiting for transfers between devices  41.6 us (18%)
  starting transfers between devices  26.5 us (11%)
  local copies, waits for them, and re-layouts  24.7 us (11%)
  between operations  14.9 us (6%)
  other arithmetic  6.5 us (3%)
    pallas_call x12, Pallas kernels, vmem_call(): pl.pallas_call(kernel, out_shape=[pltpu.HBM(*o[:2]) if len(o) > 2 else ja...  70.9 us
    ppermute x9, waiting for transfers between devices, exchange_half(): got = lax.ppermute(sent, axis, [(i, i ^ bit) for i in range(count)])  34.8 us
    all_gather x1, blocking collectives, on_device(): gather(pay)  20.3 us
    gather x1, local copies, waits for them, and re-layouts, on_device(): jnp.take(table, jnp.clip(local, 0, vocab_part - 1), axis=0, mode='clip')  16.2 us
    ppermute x9, starting transfers between devices, exchange_half(): got = lax.ppermute(sent, axis, [(i, i ^ bit) for i in range(count)])  10.5 us
    all_gather x1, blocking collectives, on_device(): gather(ends)  9.64 us
    all_gather x1, blocking collectives, on_device(): gather(part)  8.73 us
    all_gather x1, blocking collectives, on_device(): gather(jnp.concatenate([down[:, ff:], small, jnp.zeros_like(small)], 1))  6.15 us
  transfers between devices with their start and end apart: 20, of which 7 were waited for; matrix products, arithmetic and copies ran while one was open for 11% of the time, Pallas kernels for 25%

profile of v1, /device:TPU:0, one launch (start us, length us, event | category | flops | bytes accessed | tf_op | source)
XLA Modules:
  0.0 229.8 jit_solution(11402545731611725281)
XLA Ops:
  7.3 1.4 pad_maximum_fusion.refs_5_.refs_9_.refs_14_.refs_3_.refs_6_.refs_10_.refs_17_.refs_16_
  8.7 3.0 %collective-permute-start.1 = (bf16[4,192,768]{2,1,0:T(8,128)(2,1)S(1)}, bf16[4,192,768]{2,1,0:T(8,128)(2,1)S(1)}, u32[]{:S(2)}, u32[]{:S(2)}) collective-permute-start(bf16[4,192,768]{2,1,0:T(8,128)(2,1)S(1)} %pad_maximum_fusion.refs_5_.refs_9_.refs_14_.refs_3_.refs_6_.refs_10_.refs_17_.refs_16_), channel_id=1, source_target_pairs={{0,2},{1,3},{2,0},{3,1},{4,6},{5,7},{6,4},{7,5},{8,10},{9,11},{10,... | collective-permute-start | bytes 3538952 | tf_op jit(solution)/shard_map/ppermute | solution.py:214
  11.9 0.7 fusion.4
  13.3 16.2 %gather_fusion = bf16[2048,768]{1,0:T(8,128)(2,1)} fusion(bf16[8000,768]{1,0:T(8,128)(2,1)} %param.22, s32[2048]{0:T(1024)S(1)} %clamp_clamp_fusion), kind=kCustom, calls=%fused_computation | custom fusion | bytes 6299648 | tf_op jit(solution)/shard_map/jit(_take)/gather | solution.py:908
  29.6 6.6 %shard_map.280 = (bf16[128,768]{1,0:T(8,128)(2,1)S(1)}, bf16[2048,768]{1,0:T(8,128)(2,1)}, bf16[2048,768]{1,0:T(8,128)(2,1)}, f32[2048,128]{1,0:T(8,128)}) custom-call(s32[3]{0:T(128)S(1)} %pad_add_fusion.meta_ref, bf16[16,768]{1,0:T(8,128)(2,1)S(1)} %copy-done, f32[8,768]{1,0:T(8,128)S(1)} %select_select_fusion.refs_1_.refs_3_.refs_2_.refs_0_.refs_4_, ...), custom_call_target="tpu_custom_call" | custom-call | flops 920000000 | bytes 1 | tf_op jit(solution)/shard_map/pallas_call | solution.py:150
  36.3 1.8 collective-permute-done.1.refs_7_.refs_11_.refs_16_.refs_5_.refs_8_.refs_12_.refs_19_.refs_18_
  38.1 9.6 %all-gather = bf16[512,768]{1,0:T(8,128)(2,1)S(1)} all-gather(bf16[128,768]{1,0:T(8,128)(2,1)S(1)} %get-tuple-element.173), channel_id=2, replica_groups=mesh['dp'=8,'mp'=4] {'mp'}, dimensions={0}, use_global_device_ids=true | all-gather | bytes 983040 | tf_op jit(solution)/shard_map/all_gather | solution.py:941
  47.7 1.1 copy-done.3
  48.8 7.4 %shard_map.281 = (bf16[128,896]{1,0:T(8,128)(2,1)S(1)}, bf16[12,128,768]{2,1,0:T(8,128)(2,1)}, f32[128,768]{1,0:T(8,128)}, bf16[128,768]{1,0:T(8,128)(2,1)}) custom-call(s32[3]{0:T(128)S(1)} %pad_add_fusion.meta_ref, bf16[4,128,768]{2,1,0:T(8,128)(2,1)S(1)} %bitcast.63, bf16[128,16]{1,0:T(8,128)(2,1)S(1)} %get-tuple-element.322.refs_1_.refs_5_, ...), custom_call_target="tpu_custom_call" | custom-call | flops 920000000 | bytes 1 | tf_op jit(solution)/shard_map/pallas_call | solution.py:150
  56.2 20.3 %all-gather.1 = bf16[512,896]{1,0:T(8,128)(2,1)S(1)} all-gather(bf16[128,896]{1,0:T(8,128)(2,1)S(1)} %get-tuple-element.176), channel_id=3, replica_groups=mesh['dp'=8,'mp'=4] {'mp'}, dimensions={0}, use_global_device_ids=true | all-gather | bytes 1146880 | tf_op jit(solution)/shard_map/all_gather | solution.py:957
  76.5 4.1 %shard_map.282 = (f32[128,768]{1,0:T(8,128)}, f32[128,768]{1,0:T(8,128)}, f32[128,768]{1,0:T(8,128)}, f32[128,768]{1,0:T(8,128)}, bf16[128,768]{1,0:T(8,128)(2,1)S(1)}) custom-call(s32[3]{0:T(128)S(1)} %pad_add_fusion.meta_ref, bf16[4,128,896]{2,1,0:T(8,128)(2,1)S(1)} %bitcast.62, f32[8,768]{1,0:T(8,128)S(1)} %select_select_fusion.refs_1_.refs_3_.refs_2_.refs_0_.refs_4_, ...), custom_call_target="tpu_custom_call" | custom-call | flops 920000000 | bytes 1 | tf_op jit(solution)/shard_map/pallas_call | solution.py:150
  80.6 8.7 %all-gather.2 = bf16[512,768]{1,0:T(8,128)(2,1)S(1)} all-gather(bf16[128,768]{1,0:T(8,128)(2,1)S(1)} %get-tuple-element.178), channel_id=4, replica_groups=mesh['dp'=8,'mp'=4] {'mp'}, dimensions={0}, use_global_device_ids=true | all-gather | bytes 983040 | tf_op jit(solution)/shard_map/all_gather | solution.py:971
  89.4 4.6 %shard_map.283 = (bf16[128,768]{1,0:T(8,128)(2,1)}, f32[128,768]{1,0:T(8,128)}, f32[128,1024]{1,0:T(8,128)}, f32[8,1,1152]{2,1,0:T(1,128)}) custom-call(s32[3]{0:T(128)S(1)} %pad_add_fusion.meta_ref, bf16[4,128,768]{2,1,0:T(8,128)(2,1)S(1)} %bitcast.64, f32[8,768]{1,0:T(8,128)S(1)} %select_select_fusion.refs_1_.refs_3_.refs_2_.refs_0_.refs_4_, ...), custom_call_target="tpu_custom_call" | custom-call | flops 4600000000 | bytes 1 | tf_op jit(solution)/shard_map/pallas_call | solution.py:150
  94.0 5.5 %all-to-all-start.2 = ((f32[8,1,1152]{2,1,0:T(1,128)}), f32[8,1,1152]{2,1,0:T(1,128)S(1)}, u32[]{:S(2)}, u32[]{:S(2)}) async-start(f32[8,1,1152]{2,1,0:T(1,128)} %get-tuple-element.180), calls=%async_computation.2 | async-start | bytes 73728 | tf_op jit(solution)/shard_map/all_to_all | solution.py:975
  99.5 7.0 %shard_map.284.refs_4_.refs_7_ = s32[8,2048]{1,0:T(8,128)S(1)} custom-call(s32[3]{0:T(128)S(1)} %pad_add_fusion.meta_ref, s32[1,2048]{1,0:T(1,128)S(1)} %reshape.201.refs_2_.refs_4_.refs_0_.refs_1_.refs_5_), custom_call_target="tpu_custom_call" | custom-call | flops 6440000000 | bytes 1 | tf_op jit(solution)/shard_map/pallas_call | solution.py:150
  106.6 5.1 %shard_map.285 = (f32[1,128]{1,0:T(1,128)}, f32[128,768]{1,0:T(8,128)S(1)}, bf16[128,768]{1,0:T(8,128)(2,1)S(1)}, bf16[128,768]{1,0:T(8,128)(2,1)S(1)}, bf16[128,768]{1,0:T(8,128)(2,1)S(1)}) custom-call(s32[3]{0:T(128)S(1)} %pad_add_fusion.meta_ref, f32[8,1,1152]{2,1,0:T(1,128)S(1)} %all-to-all-done.2.refs_0_, ...), custom_call_target="tpu_custom_call" | custom-call | flops 4600000000 | bytes 1 | tf_op jit(solution)/shard_map/pallas_call | solution.py:150
  111.9 1.3 collective-permute-done.3
  113.2 1.3 collective-permute-start.4
  114.5 3.4 %shard_map.289 = (bf16[4,96,960]{2,1,0:T(8,128)(2,1)S(1)}, bf16[4,96,960]{2,1,0:T(8,128)(2,1)S(1)}, bf16[4,96,768]{2,1,0:T(8,128)(2,1)S(1)}, bf16[4,96,768]{2,1,0:T(8,128)(2,1)S(1)}, f32[2,768]{1,0:T(2,128)S(1)}) custom-call(s32[3]{0:T(128)S(1)} %pad_add_fusion.meta_ref, f32[8,768]{1,0:T(8,128)S(1)} %select_select_fusion.refs_1_.refs_3_.refs_2_.refs_0_.refs_4_, ...), custom_call_target="tpu_custom_call" | custom-call | flops 3680000000 | bytes 1 | tf_op jit(solution)/shard_map/pallas_call | solution.py:150
  118.0 2.1 collective-permute-start.11
  120.0 1.5 collective-permute-start.8
  121.5 11.4 %shard_map.286 = (f32[128,768]{1,0:T(8,128)S(1)}, bf16[768,192]{1,0:T(8,128)(2,1)S(1)}, bf16[1792,384]{1,0:T(8,128)(2,1)S(1)}, bf16[896,384]{1,0:T(8,128)(2,1)S(...) custom-call(s32[3]{0:T(128)S(1)} %pad_add_fusion.meta_ref, ...), custom_call_target="tpu_custom_call" | custom-call | flops 11960000512 | bytes 1 | tf_op jit(solution)/shard_map/pallas_call | solution.py:150
  133.7 1.7 collective-permute-start.12
  135.4 5.1 %collective-permute-done.8 = bf16[4,96,960]{2,1,0:T(8,128)(2,1)S(1)} collective-permute-done((bf16[4,96,960]{2,1,0:T(8,128)(2,1)S(1)}, bf16[4,96,960]{2,1,0:T(8,128)(2,1)S(1)}, u32[]{:S(2)}, u32[]{:S(2)}) %collective-permute-start.8) | collective-permute-done | bytes 737312 | tf_op jit(solution)/shard_map/ppermute | solution.py:173
  141.0 1.0 shard_map.287
  142.0 0.8 collective-permute-start.7
  142.8 12.6 %shard_map.288 = (bf16[2048,768]{1,0:T(8,128)(2,1)}, f32[16,768]{1,0:T(8,128)S(1)}, f32[2,768]{1,0:T(2,128)S(1)}, f32[512,768]{1,0:T(8,128)S(1)}, f32[16,512]{1,0:T(8,128)S(1)}, /*index=5*/bf16[512,128]{1,0:T(8,128)(2,1)S(1)}) custom-call(s32[3]{0:T(128)S(1)} %pad_add_fusion.meta_ref, bf16[8,192,256]{2,1,0:T(8,128)(2,1)S(1)} %get-tuple-element.201.refs_0_, ...), custom_call_target="tpu_custom_call" | custom-call | flops 11040000000 | bytes 1 | tf_op jit(solution)/shard_map/pallas_call | solution.py:150
  155.4 3.7 %collective-permute-done.7.refs_1_ = bf16[1024,384]{1,0:T(8,128)(2,1)S(1)} collective-permute-done((bf16[1024,384]{1,0:T(8,128)(2,1)S(1)}, bf16[1024,384]{1,0:T(8,128)(2,1)S(1)}, u32[]{:S(2)}, u32[]{:S(2)}) %collective-permute-start.7) | collective-permute-done | bytes 786464 | tf_op jit(solution)/shard_map/ppermute | solution.py:1061
  159.1 4.4 %shard_map.290 = (bf16[128,768]{1,0:T(8,128)(2,1)S(1)}, bf16[8,224,256]{2,1,0:T(8,128)(2,1)}, bf16[4,96,768]{2,1,0:T(8,128)(2,1)S(1)}, bf16[4,96,768]{2,1,0:T(8,128)(2,1)S(1)}) custom-call(s32[3]{0:T(128)S(1)} %pad_add_fusion.meta_ref, bf16[1024,384]{1,0:T(8,128)(2,1)S(1)} %get-tuple-element.196.refs_0_, ...), custom_call_target="tpu_custom_call" | custom-call | flops 3680000000 | bytes 1 | tf_op jit(solution)/shard_map/pallas_call | solution.py:150
  163.5 1.4 collective-permute-start.14
  165.0 0.7 constant_dynamic-slice_fusion.3
  165.7 2.4 %collective-permute-start.13 = (bf16[1,96,768]{2,1,0:T(8,128)(2,1)}, bf16[1,96,768]{2,1,0:T(8,128)(2,1)}, u32[]{:S(2)}, u32[]{:S(2)}) collective-permute-start(bf16[1,96,768]{2,1,0:T(8,128)(2,1)} %constant_dynamic-slice_fusion.3), channel_id=1, source_target_pairs={{0,16},{4,20},{8,24},{12,28},{16,0},{20,4},{24,8},{28,12},{1,17},{... | collective-permute-start | bytes 442376 | tf_op jit(solution)/shard_map/ppermute | solution.py:173
  168.9 6.6 %collective-permute-done.14 = bf16[4,96,768]{2,1,0:T(8,128)(2,1)S(1)} collective-permute-done((bf16[4,96,768]{2,1,0:T(8,128)(2,1)S(1)}, bf16[4,96,768]{2,1,0:T(8,128)(2,1)S(1)}, u32[]{:S(2)}, u32[]{:S(2)}) %collective-permute-start.14) | collective-permute-done | bytes 589856 | tf_op jit(solution)/shard_map/ppermute | solution.py:173
  175.9 0.8 collective-permute-start.15
  176.7 4.5 %all-to-all-start.3 = ((bf16[8,224,256]{2,1,0:T(8,128)(2,1)}), bf16[8,224,256]{2,1,0:T(8,128)(2,1)S(1)}, u32[]{:S(2)}, u32[]{:S(2)}) async-start(bf16[8,224,256]{2,1,0:T(8,128)(2,1)} %get-tuple-element.216), calls=%async_computation.3 | async-start | bytes 1835008 | tf_op jit(solution)/shard_map/all_to_all | solution.py:1102
  181.2 1.7 add_bitcast_fusion.2
  182.9 1.0 add_bitcast_fusion.1
  184.1 13.3 %collective-permute-done.15 = bf16[2,96,768]{1,2,0:T(8,128)(2,1)S(1)} collective-permute-done((bf16[2,96,768]{1,2,0:T(8,128)(2,1)S(1)}, bf16[2,96,768]{1,2,0:T(8,128)(2,1)S(1)}, u32[]{:S(2)}, u32[]{:S(2)}) %collective-permute-start.15) | collective-permute-done | bytes 294944 | tf_op jit(solution)/shard_map/ppermute | solution.py:173
  197.7 0.7 slice_bitcast_fusion.1
  198.4 9.7 %collective-permute-done.16 = bf16[1,96,768]{1,2,0:T(8,128)(2,1)S(1)} collective-permute-done((bf16[1,96,768]{1,2,0:T(8,128)(2,1)S(1)}, bf16[1,96,768]{1,2,0:T(8,128)(2,1)S(1)}, u32[]{:S(2)}, u32[]{:S(2)}) %collective-permute-start.16) | collective-permute-done | bytes 147488 | tf_op jit(solution)/shard_map/ppermute | solution.py:173
  208.2 0.7 slice_bitcast_fusion.2
  208.9 0.9 copy.67
  209.7 3.2 %shard_map.291 = (f32[1000,768]{1,0:T(8,128)}, f32[96,32]{1,0:T(8,128)S(1)}, f32[1,128]{1,0:T(1,128)S(1)}) custom-call(s32[3]{0:T(128)S(1)} %pad_add_fusion.meta_ref, bf16[8,224,256]{2,1,0:T(8,128)(2,1)S(1)} %all-to-all-done.3.refs_0_), custom_call_target="tpu_custom_call" | custom-call | flops 2760000000 | bytes 1 | tf_op jit(solution)/shard_map/pallas_call | solution.py:150
  213.0 0.8 slice_reduce_fusion.3
  213.9 6.1 %all-gather.3 = f32[384,256]{1,0:T(8,128)S(1)} all-gather(f32[96,256]{1,0:T(8,128)S(1)} %maximum_maximum_fusion), channel_id=5, replica_groups=mesh['dp'=8,'mp'=4] {'mp'}, dimensions={0}, use_global_device_ids=true | all-gather | bytes 491520 | tf_op jit(solution)/shard_map/all_gather | solution.py:1124
  220.2 0.7 slice_reduce_fusion.1
  221.2 1.0 reshape.208
  222.1 0.7 copy.66
  (100 shorter events, 4.7 us)
Async XLA Ops:
  7.2 4.5 %copy-start.5 = (bf16[32,768]{1,0:T(8,128)(2,1)S(1)}, bf16[32,768]{1,0:T(8,128)(2,1)}, u32[]{:S(2)}) copy-start(bf16[32,768]{1,0:T(8,128)(2,1)} %param.21) | copy-start | bytes 147460
  7.2 5.4 %copy-start.14 = (s32[128]{0:T(128)S(1)}, s32[128]{0:T(128)}, u32[]{:S(2)}) copy-start(s32[128]{0:T(128)} %param.20) | copy-start | bytes 1540
  7.2 5.4 %copy-start.6 = (s32[128,16]{0,1:T(8,128)S(1)}, s32[128,16]{0,1:T(8,128)}, u32[]{:S(2)}) copy-start(s32[128,16]{0,1:T(8,128)} %param.19) | copy-start | bytes 24580
  7.2 5.7 %copy-start.7 = (bf16[768]{0:T(1024)(128)(2,1)S(1)}, bf16[768]{0:T(1024)(128)(2,1)}, u32[]{:S(2)}) copy-start(bf16[768]{0:T(1024)(128)(2,1)} %param.24) | copy-start | bytes 4612
  7.2 5.7 %copy-start.8 = (bf16[768]{0:T(1024)(128)(2,1)S(1)}, bf16[768]{0:T(1024)(128)(2,1)}, u32[]{:S(2)}) copy-start(bf16[768]{0:T(1024)(128)(2,1)} %param.25) | copy-start | bytes 4612
  7.2 5.7 %copy-start.9 = (bf16[768]{0:T(1024)(128)(2,1)S(1)}, bf16[768]{0:T(1024)(128)(2,1)}, u32[]{:S(2)}) copy-start(bf16[768]{0:T(1024)(128)(2,1)} %param.28) | copy-start | bytes 4612
  7.2 5.8 %copy-start.10 = (bf16[768]{0:T(1024)(128)(2,1)S(1)}, bf16[768]{0:T(1024)(128)(2,1)}, u32[]{:S(2)}) copy-start(bf16[768]{0:T(1024)(128)(2,1)} %param.29) | copy-start | bytes 4612
  7.3 5.8 %copy-start.11 = (bf16[768]{0:T(1024)(128)(2,1)S(1)}, bf16[768]{0:T(1024)(128)(2,1)}, u32[]{:S(2)}) copy-start(bf16[768]{0:T(1024)(128)(2,1)} %param.30) | copy-start | bytes 4612
  7.3 5.8 %copy-start.12 = (bf16[768]{0:T(1024)(128)(2,1)S(1)}, bf16[768]{0:T(1024)(128)(2,1)}, u32[]{:S(2)}) copy-start(bf16[768]{0:T(1024)(128)(2,1)} %param.32) | copy-start | bytes 4612
  7.3 5.8 %copy-start.13 = (bf16[768]{0:T(1024)(128)(2,1)S(1)}, bf16[768]{0:T(1024)(128)(2,1)}, u32[]{:S(2)}) copy-start(bf16[768]{0:T(1024)(128)(2,1)} %param.34) | copy-start | bytes 4612
  7.3 82.1 %all-gather.6.cloned.1.call-start = ((), (), s32[]{:S(2)}) async-start(), calls=%async_computation.4 | async-start | bytes 1622016 | tf_op jit(solution)/shard_map/all_gather | solution.py:894
  8.7 20.7 %copy-start.1 = (bf16[4,192,768]{2,1,0:T(8,128)(2,1)}, bf16[4,192,768]{2,1,0:T(8,128)(2,1)S(1)}, u32[]{:S(2)}) copy-start(bf16[4,192,768]{2,1,0:T(8,128)(2,1)S(1)} %pad_maximum_fusion.refs_5_.refs_9_.refs_14_.refs_3_.refs_6_.refs_10_.refs_17_.refs_16_) | copy-start | bytes 3538948
  8.7 29.3 %collective-permute-start.1 = (bf16[4,192,768]{2,1,0:T(8,128)(2,1)S(1)}, bf16[4,192,768]{2,1,0:T(8,128)(2,1)S(1)}, u32[]{:S(2)}, u32[]{:S(2)}) collective-permute-start(bf16[4,192,768]{2,1,0:T(8,128)(2,1)S(1)} %pad_maximum_fusion.refs_5_.refs_9_.refs_14_.refs_3_.refs_6_.refs_10_.refs_17_.refs_16_), channel_id=1, source_target_pairs={{0,2},{1,3},{2,0},{3,1},{4,6},{5,7},{6,4},{7,5},{8,10},{9,11},{10,... | collective-permute-start | bytes 3538952 | tf_op jit(solution)/shard_map/ppermute | solution.py:214
  11.7 36.0 %collective-permute-start = (bf16[4,192,768]{2,1,0:T(8,128)(2,1)S(1)}, bf16[4,192,768]{2,1,0:T(8,128)(2,1)}, u32[]{:S(2)}, u32[]{:S(2)}) collective-permute-start(bf16[4,192,768]{2,1,0:T(8,128)(2,1)S(1)} %pad_maximum_fusion.refs_5_.refs_9_.refs_14_.refs_3_.refs_6_.refs_10_.refs_17_.refs_16_), channel_id=1, source_target_pairs={{0,1},{1,0},{2,3},{3,2},{4,5},{5,4},{6,7},{7,6},{8,9},{9,8},{10,11... | collective-permute-start | bytes 3538952 | tf_op jit(solution)/shard_map/ppermute | solution.py:214
  13.3 16.4 %copy-start = (bf16[16,768]{1,0:T(8,128)(2,1)S(1)}, bf16[16,768]{1,0:T(8,128)(2,1)}, u32[]{:S(2)}) copy-start(bf16[16,768]{1,0:T(8,128)(2,1)} %refs_2_.1) | copy-start | bytes 73732
  38.0 9.7 %copy-start.2 = (bf16[4,192,768]{2,1,0:T(8,128)(2,1)}, bf16[4,192,768]{2,1,0:T(8,128)(2,1)S(1)}, u32[]{:S(2)}) copy-start(bf16[4,192,768]{2,1,0:T(8,128)(2,1)S(1)} %collective-permute-done.1.refs_7_.refs_11_.refs_16_.refs_5_.refs_8_.refs_12_.refs_19_.refs_18_) | copy-start | bytes 3538948
  38.0 9.6 %collective-permute-start.2 = (bf16[4,192,768]{2,1,0:T(8,128)(2,1)S(1)}, bf16[4,192,768]{2,1,0:T(8,128)(2,1)S(1)}, u32[]{:S(2)}, u32[]{:S(2)}) collective-permute-start(bf16[4,192,768]{2,1,0:T(8,128)(2,1)S(1)} %collective-permute-done.1.refs_7_.refs_11_.refs_16_.refs_5_.refs_8_.refs_12_.refs_19_.refs_18_), channel_id=1, source_target_pairs={{0,1},{1,0},{2,3},{3,2},{4,5},{5,4},{6,7},{7,6},{8,9},{9,8},{10,11... | collective-permute-start | bytes 3538952 | tf_op jit(solution)/shard_map/ppermute | solution.py:214
  47.7 1.1 copy-start.3
  94.0 12.6 %all-to-all-start.2 = ((f32[8,1,1152]{2,1,0:T(1,128)}), f32[8,1,1152]{2,1,0:T(1,128)S(1)}, u32[]{:S(2)}, u32[]{:S(2)}) async-start(f32[8,1,1152]{2,1,0:T(1,128)} %get-tuple-element.180), calls=%async_computation.2 | async-start | bytes 73728 | tf_op jit(solution)/shard_map/all_to_all | solution.py:975
  111.6 1.5 collective-permute-start.3
  113.2 8.3 %collective-permute-start.4 = (bf16[128,768]{1,0:T(8,128)(2,1)S(1)}, bf16[128,768]{1,0:T(8,128)(2,1)S(1)}, u32[]{:S(2)}, u32[]{:S(2)}) collective-permute-start(bf16[128,768]{1,0:T(8,128)(2,1)S(1)} %add.136), channel_id=1, source_target_pairs={{0,2},{1,3},{2,0},{3,1},{4,6},{5,7},{6,4},{7,5},{8,10},{9,11},{10,... | collective-permute-start | bytes 589832 | tf_op jit(solution)/shard_map/ppermute | solution.py:1029
  118.0 15.6 %collective-permute-start.11 = (bf16[4,96,768]{2,1,0:T(8,128)(2,1)S(1)}, bf16[4,96,768]{2,1,0:T(8,128)(2,1)S(1)}, u32[]{:S(2)}, u32[]{:S(2)}) collective-permute-start(bf16[4,96,768]{2,1,0:T(8,128)(2,1)S(1)} %get-tuple-element.225), channel_id=1, source_target_pairs={{0,8},{4,12},{8,0},{12,4},{16,24},{20,28},{24,16},{28,20},{1,9},{5... | collective-permute-start | bytes 1769480 | tf_op jit(solution)/shard_map/ppermute | solution.py:173
  120.0 20.5 %collective-permute-start.8 = (bf16[4,96,960]{2,1,0:T(8,128)(2,1)S(1)}, bf16[4,96,960]{2,1,0:T(8,128)(2,1)S(1)}, u32[]{:S(2)}, u32[]{:S(2)}) collective-permute-start(bf16[4,96,960]{2,1,0:T(8,128)(2,1)S(1)} %get-tuple-element.223), channel_id=1, source_target_pairs={{0,4},{4,0},{8,12},{12,8},{16,20},{20,16},{24,28},{28,24},{1,5},{5... | collective-permute-start | bytes 2211848 | tf_op jit(solution)/shard_map/ppermute | solution.py:173
  133.0 8.0 %collective-permute-start.5 = (bf16[896,384]{1,0:T(8,128)(2,1)S(1)}, bf16[896,384]{1,0:T(8,128)(2,1)S(1)}, u32[]{:S(2)}, u32[]{:S(2)}) collective-permute-start(bf16[896,384]{1,0:T(8,128)(2,1)S(1)} %get-tuple-element.194), channel_id=1, source_target_pairs={{0,1},{1,0},{2,3},{3,2},{4,5},{5,4},{6,7},{7,6},{8,9},{9,8},{10,11... | collective-permute-start | bytes 2064392 | tf_op jit(solution)/shard_map/ppermute | solution.py:1056
  133.0 7.9 %collective-permute-start.6 = (bf16[896,384]{1,0:T(8,128)(2,1)S(1)}, bf16[896,384]{1,0:T(8,128)(2,1)S(1)}, u32[]{:S(2)}, u32[]{:S(2)}) collective-permute-start(bf16[896,384]{1,0:T(8,128)(2,1)S(1)} %get-tuple-element.195), channel_id=1, source_target_pairs={{0,1},{1,0},{2,3},{3,2},{4,5},{5,4},{6,7},{7,6},{8,9},{9,8},{10,11... | collective-permute-start | bytes 2064392 | tf_op jit(solution)/shard_map/ppermute | solution.py:1056
  133.7 31.2 %collective-permute-start.12 = (bf16[2,96,768]{2,1,0:T(8,128)(2,1)S(1)}, bf16[2,96,768]{2,1,0:T(8,128)(2,1)S(1)}, u32[]{:S(2)}, u32[]{:S(2)}) collective-permute-start(bf16[2,96,768]{2,1,0:T(8,128)(2,1)S(1)} %dynamic-slice_bitcast_fusion.1), channel_id=1, source_target_pairs={{0,4},{4,0},{8,12},{12,8},{16,20},{20,16},{24,28},{28,24},{1,5},{5... | collective-permute-start | bytes 884744 | tf_op jit(solution)/shard_map/ppermute | solution.py:173
  140.9 27.2 %collective-permute-start.9 = (bf16[2,96,960]{2,1,0:T(8,128)(2,1)S(1)}, bf16[2,96,960]{2,1,0:T(8,128)(2,1)S(1)}, u32[]{:S(2)}, u32[]{:S(2)}) collective-permute-start(bf16[2,96,960]{2,1,0:T(8,128)(2,1)S(1)} %dynamic-slice_bitcast_fusion), channel_id=1, source_target_pairs={{0,8},{4,12},{8,0},{12,4},{16,24},{20,28},{24,16},{28,20},{1,9},{5... | collective-permute-start | bytes 1105928 | tf_op jit(solution)/shard_map/ppermute | solution.py:173
  142.0 17.1 %collective-permute-start.7 = (bf16[1024,384]{1,0:T(8,128)(2,1)S(1)}, bf16[1024,384]{1,0:T(8,128)(2,1)S(1)}, u32[]{:S(2)}, u32[]{:S(2)}) collective-permute-start(bf16[1024,384]{1,0:T(8,128)(2,1)S(1)} %get-tuple-element.197), channel_id=1, source_target_pairs={{0,2},{1,3},{2,0},{3,1},{4,6},{5,7},{6,4},{7,5},{8,10},{9,11},{10,... | collective-permute-start | bytes 2359304 | tf_op jit(solution)/shard_map/ppermute | solution.py:1061
  163.5 12.0 %collective-permute-start.14 = (bf16[4,96,768]{2,1,0:T(8,128)(2,1)S(1)}, bf16[4,96,768]{2,1,0:T(8,128)(2,1)S(1)}, u32[]{:S(2)}, u32[]{:S(2)}) collective-permute-start(bf16[4,96,768]{2,1,0:T(8,128)(2,1)S(1)} %get-tuple-element.229), channel_id=1, source_target_pairs={{0,4},{4,0},{8,12},{12,8},{16,20},{20,16},{24,28},{28,24},{1,5},{5... | collective-permute-start | bytes 1769480 | tf_op jit(solution)/shard_map/ppermute | solution.py:173
  165.7 15.5 %collective-permute-start.13 = (bf16[1,96,768]{2,1,0:T(8,128)(2,1)}, bf16[1,96,768]{2,1,0:T(8,128)(2,1)}, u32[]{:S(2)}, u32[]{:S(2)}) collective-permute-start(bf16[1,96,768]{2,1,0:T(8,128)(2,1)} %constant_dynamic-slice_fusion.3), channel_id=1, source_target_pairs={{0,16},{4,20},{8,24},{12,28},{16,0},{20,4},{24,8},{28,12},{1,17},{... | collective-permute-start | bytes 442376 | tf_op jit(solution)/shard_map/ppermute | solution.py:173
  168.2 14.7 %collective-permute-start.10 = (bf16[1,96,960]{2,1,0:T(8,128)(2,1)S(1)}, bf16[1,96,960]{2,1,0:T(8,128)(2,1)}, u32[]{:S(2)}, u32[]{:S(2)}) collective-permute-start(bf16[1,96,960]{2,1,0:T(8,128)(2,1)S(1)} %constant_dynamic-slice_fusion.4), channel_id=1, source_target_pairs={{0,16},{4,20},{8,24},{12,28},{16,0},{20,4},{24,8},{28,12},{1,17},{... | collective-permute-start | bytes 552968 | tf_op jit(solution)/shard_map/ppermute | solution.py:173
  175.9 21.5 %collective-permute-start.15 = (bf16[2,96,768]{1,2,0:T(8,128)(2,1)S(1)}, bf16[2,96,768]{1,2,0:T(8,128)(2,1)S(1)}, u32[]{:S(2)}, u32[]{:S(2)}) collective-permute-start(bf16[2,96,768]{1,2,0:T(8,128)(2,1)S(1)} %bitcast.75), channel_id=1, source_target_pairs={{0,8},{4,12},{8,0},{12,4},{16,24},{20,28},{24,16},{28,20},{1,9},{5... | collective-permute-start | bytes 884744 | tf_op jit(solution)/shard_map/ppermute | solution.py:173
  176.7 33.1 %all-to-all-start.3 = ((bf16[8,224,256]{2,1,0:T(8,128)(2,1)}), bf16[8,224,256]{2,1,0:T(8,128)(2,1)S(1)}, u32[]{:S(2)}, u32[]{:S(2)}) async-start(bf16[8,224,256]{2,1,0:T(8,128)(2,1)} %get-tuple-element.216), calls=%async_computation.3 | async-start | bytes 1835008 | tf_op jit(solution)/shard_map/all_to_all | solution.py:1102
  183.9 24.3 %copy-start.4 = (f32[96,960]{1,0:T(8,128)}, f32[96,960]{1,0:T(8,128)S(1)}, u32[]{:S(2)}) copy-start(f32[96,960]{1,0:T(8,128)S(1)} %add_bitcast_fusion.1) | copy-start | bytes 1105924
  197.6 10.5 %collective-permute-start.16 = (bf16[1,96,768]{1,2,0:T(8,128)(2,1)S(1)}, bf16[1,96,768]{1,2,0:T(8,128)(2,1)S(1)}, u32[]{:S(2)}, u32[]{:S(2)}) collective-permute-start(bf16[1,96,768]{1,2,0:T(8,128)(2,1)S(1)} %constant_dynamic-slice_fusion), channel_id=1, source_target_pairs={{0,16},{4,20},{8,24},{12,28},{16,0},{20,4},{24,8},{28,12},{1,17},{... | collective-permute-start | bytes 442376 | tf_op jit(solution)/shard_map/ppermute | solution.py:173
  209.7 4.0 %slice-start = ((f32[96,960]{1,0:T(8,128)}), f32[96,192]{1,0:T(8,128)S(1)}, s32[]{:S(2)}) async-start(f32[96,960]{1,0:T(8,128)} %copy-done.4), calls=%async_computation.5 | async-start | bytes 196608 | tf_op jit(solution)/shard_map/slice | solution.py:1124
Sparse Core Ops, SparseCore 0:
  12.7 56.7 all-gather.5

commit v2 on v1

--- a/solution.py
+++ b/solution.py
@@ -175,13 +175,15 @@
     return total if last else total.astype(BF)
 
 
-def halve(total, axis, bits, bit):
+def halve(total, axis, bits, bit, hold=None):
     low = 1 << bits.index(bit)
     pairs = total.reshape((total.shape[0] // (2 * low), 2, low) + total.shape[1:])
     shape = (total.shape[0] // 2,) + total.shape[1:]
     mine = (lax.axis_index(axis) // bit) % 2
     sent = lax.dynamic_index_in_dim(pairs, 1 - mine, 1, keepdims=False).reshape(shape)
     kept = lax.dynamic_index_in_dim(pairs, mine, 1, keepdims=False).reshape(shape)
+    if hold is not None:
+        kept = after(kept, hold)
     return exchange_half(kept, sent, axis, bit, len(bits) == 1)
 
 
@@ -1015,8 +1017,8 @@
     )
     dp_bits = bits_of("dp")
 
-    def next_half(total, bits):
-        total = halve(total, "dp", bits, bits[0])
+    def next_half(total, bits, hold=None):
+        total = halve(total, "dp", bits, bits[0], hold)
         bits.pop(0)
         return total
 
@@ -1076,7 +1078,7 @@
         flops=WORK * 12,
         mib=32,
     )
-    down, up = next_half(down, down_bits), next_half(up, up_bits)
+    down, up = next_half(down, down_bits), next_half(up, up_bits, seg)
     rest_rows = -(-chunk // 32) * 8
     send_rows = width // lanes * slot_cap
     dxp, send, kept, sent = vmem_call(
@@ -1122,7 +1124,7 @@
     most_all = most_all[0, 0].astype(I32)
     small = rest
     last = gather(jnp.concatenate([down[:, ff:], small, jnp.zeros_like(small)], 1))
-    wkvo = lax.optimization_barrier(next_half(wkvo, bits)[0])
+    wkvo = lax.optimization_barrier(next_half(wkvo, bits, last)[0])
 
     def another(carry):
         turn, total = carry

time: 232 us -> 227 us (0.978)
  waiting for transfers between devices: 41.6 us -> 28.9 us
  other arithmetic: 6.5 us -> 9.73 us
  starting transfers between devices: 26.5 us -> 29.1 us
    ppermute x9, waiting for transfers between devices: 34.8 us -> 24.4 us  [exchange_half(): got = lax.ppermute(sent, axis, [(i, i ^ bit) for i in range(count)])]
    convert_element_type x6, other arithmetic: 0.92 us -> 4.14 us  [exchange_half(): return total if last else total.astype(BF)]
    ppermute x9, starting transfers between devices: 10.5 us -> 13.5 us  [exchange_half(): got = lax.ppermute(sent, axis, [(i, i ^ bit) for i in range(count)])]
    ppermute x1, waiting for transfers between devices: 3.7 us -> 0.73 us  [on_device(): got = lax.ppermute(sent, 'mp', [(i, i ^ 2) for i in range(n_mp)])]
  transfers between devices with their start and end apart: 20 -> 20, of which waited for: 7 -> 7; matrix products, arithmetic and copies ran while one was open for 11% -> 14% of each run, Pallas kernels for 25% -> 27%
where the time goes in v2:
time: 227 us; the launch traced here: 224 us
  Pallas kernels  70.9 us (31%)
  blocking collectives  44.2 us (19%)
  starting transfers between devices  29.1 us (13%)
  waiting for transfers between devices  28.9 us (13%)
  local copies, waits for them, and re-layouts  26.7 us (12%)
  between operations  14.9 us (7%)
  other arithmetic  9.73 us (4%)
    pallas_call x12, Pallas kernels, vmem_call(): pl.pallas_call(kernel, out_shape=[pltpu.HBM(*o[:2]) if len(o) > 2 else ja...  70.9 us
    ppermute x9, waiting for transfers between devices, exchange_half(): got = lax.ppermute(sent, axis, [(i, i ^ bit) for i in range(count)])  24.4 us
    all_gather x1, blocking collectives, on_device(): gather(pay)  20.4 us
    gather x1, local copies, waits for them, and re-layouts, on_device(): jnp.take(table, jnp.clip(local, 0, vocab_part - 1), axis=0, mode='clip')  16.2 us
    ppermute x9, starting transfers between devices, exchange_half(): got = lax.ppermute(sent, axis, [(i, i ^ bit) for i in range(count)])  13.5 us
    all_gather x1, blocking collectives, on_device(): gather(ends)  8.88 us
    all_gather x1, blocking collectives, on_device(): gather(part)  8.72 us
    all_gather x1, blocking collectives, on_device(): gather(jnp.concatenate([down[:, ff:], small, jnp.zeros_like(small)], 1))  6.15 us
  transfers between devices with their start and end apart: 20, of which 7 were waited for; matrix products, arithmetic and copies ran while one was open for 14% of the time, Pallas kernels for 27%

profile of v2, /device:TPU:0, one launch (start us, length us, event | category | flops | bytes accessed | tf_op | source)
XLA Modules:
  0.0 224.5 jit_solution(12180256666658707157)
XLA Ops:
  7.3 1.4 pad_maximum_fusion.refs_5_.refs_9_.refs_14_.refs_3_.refs_6_.refs_10_.refs_17_.refs_16_
  9.2 2.6 %collective-permute-start.1 = (bf16[4,192,768]{2,1,0:T(8,128)(2,1)S(1)}, bf16[4,192,768]{2,1,0:T(8,128)(2,1)}, u32[]{:S(2)}, u32[]{:S(2)}) collective-permute-start(bf16[4,192,768]{2,1,0:T(8,128)(2,1)S(1)} %pad_maximum_fusion.refs_5_.refs_9_.refs_14_.refs_3_.refs_6_.refs_10_.refs_17_.refs_16_), channel_id=1, source_target_pairs={{0,2},{1,3},{2,0},{3,1},{4,6},{5,7},{6,4},{7,5},{8,10},{9,11},{10,... | collective-permute-start | bytes 3538952 | tf_op jit(solution)/shard_map/ppermute | solution.py:216
  13.4 16.2 %gather_fusion = bf16[2048,768]{1,0:T(8,128)(2,1)} fusion(bf16[8000,768]{1,0:T(8,128)(2,1)} %param.22, s32[2048]{0:T(1024)S(1)} %clamp_clamp_fusion), kind=kCustom, calls=%fused_computation | custom fusion | bytes 6299648 | tf_op jit(solution)/shard_map/jit(_take)/gather | solution.py:910
  29.8 6.6 %shard_map.280 = (bf16[128,768]{1,0:T(8,128)(2,1)S(1)}, bf16[2048,768]{1,0:T(8,128)(2,1)}, bf16[2048,768]{1,0:T(8,128)(2,1)}, f32[2048,128]{1,0:T(8,128)}) custom-call(s32[3]{0:T(128)S(1)} %pad_add_fusion.meta_ref, bf16[16,768]{1,0:T(8,128)(2,1)S(1)} %copy-done, f32[8,768]{1,0:T(8,128)S(1)} %select_select_fusion.refs_1_.refs_3_.refs_2_.refs_0_.refs_4_, ...), custom_call_target="tpu_custom_call" | custom-call | flops 920000000 | bytes 1 | tf_op jit(solution)/shard_map/pallas_call | solution.py:150
  36.4 2.4 %collective-permute-done.1.refs_7_.refs_11_.refs_16_.refs_5_.refs_8_.refs_12_.refs_19_.refs_18_ = bf16[4,192,768]{2,1,0:T(8,128)(2,1)} collective-permute-done((bf16[4,192,768]{2,1,0:T(8,128)(2,1)S(1)}, bf16[4,192,768]{2,1,0:T(8,128)(2,1)}, u32[]{:S(2)}, u32[]{:S(2)}) %collective-permute-start.1) | collective-permute-done | bytes 1179680 | tf_op jit(solution)/shard_map/ppermute | solution.py:216
  38.8 8.9 %all-gather = bf16[512,768]{1,0:T(8,128)(2,1)S(1)} all-gather(bf16[128,768]{1,0:T(8,128)(2,1)S(1)} %get-tuple-element.175), channel_id=2, replica_groups=mesh['dp'=8,'mp'=4] {'mp'}, dimensions={0}, use_global_device_ids=true | all-gather | bytes 983040 | tf_op jit(solution)/shard_map/all_gather | solution.py:943
  47.7 1.0 copy-done.2
  49.2 7.4 %shard_map.281 = (bf16[128,896]{1,0:T(8,128)(2,1)S(1)}, bf16[12,128,768]{2,1,0:T(8,128)(2,1)}, f32[128,768]{1,0:T(8,128)}, bf16[128,768]{1,0:T(8,128)(2,1)}) custom-call(s32[3]{0:T(128)S(1)} %pad_add_fusion.meta_ref, bf16[4,128,768]{2,1,0:T(8,128)(2,1)S(1)} %bitcast.60, bf16[128,16]{1,0:T(8,128)(2,1)S(1)} %get-tuple-element.330.refs_1_.refs_5_, ...), custom_call_target="tpu_custom_call" | custom-call | flops 920000000 | bytes 1 | tf_op jit(solution)/shard_map/pallas_call | solution.py:150
  56.6 20.4 %all-gather.1 = bf16[512,896]{1,0:T(8,128)(2,1)S(1)} all-gather(bf16[128,896]{1,0:T(8,128)(2,1)S(1)} %get-tuple-element.178), channel_id=3, replica_groups=mesh['dp'=8,'mp'=4] {'mp'}, dimensions={0}, use_global_device_ids=true | all-gather | bytes 1146880 | tf_op jit(solution)/shard_map/all_gather | solution.py:959
  77.0 4.1 %shard_map.282 = (f32[128,768]{1,0:T(8,128)}, f32[128,768]{1,0:T(8,128)}, f32[128,768]{1,0:T(8,128)}, f32[128,768]{1,0:T(8,128)}, bf16[128,768]{1,0:T(8,128)(2,1)S(1)}) custom-call(s32[3]{0:T(128)S(1)} %pad_add_fusion.meta_ref, bf16[4,128,896]{2,1,0:T(8,128)(2,1)S(1)} %bitcast.59, f32[8,768]{1,0:T(8,128)S(1)} %select_select_fusion.refs_1_.refs_3_.refs_2_.refs_0_.refs_4_, ...), custom_call_target="tpu_custom_call" | custom-call | flops 920000000 | bytes 1 | tf_op jit(solution)/shard_map/pallas_call | solution.py:150
  81.1 8.7 %all-gather.2 = bf16[512,768]{1,0:T(8,128)(2,1)S(1)} all-gather(bf16[128,768]{1,0:T(8,128)(2,1)S(1)} %get-tuple-element.180), channel_id=4, replica_groups=mesh['dp'=8,'mp'=4] {'mp'}, dimensions={0}, use_global_device_ids=true | all-gather | bytes 983040 | tf_op jit(solution)/shard_map/all_gather | solution.py:973
  89.8 4.6 %shard_map.283 = (bf16[128,768]{1,0:T(8,128)(2,1)}, f32[128,768]{1,0:T(8,128)}, f32[128,1024]{1,0:T(8,128)}, f32[8,1,1152]{2,1,0:T(1,128)}) custom-call(s32[3]{0:T(128)S(1)} %pad_add_fusion.meta_ref, bf16[4,128,768]{2,1,0:T(8,128)(2,1)S(1)} %bitcast.61, f32[8,768]{1,0:T(8,128)S(1)} %select_select_fusion.refs_1_.refs_3_.refs_2_.refs_0_.refs_4_, ...), custom_call_target="tpu_custom_call" | custom-call | flops 4600000000 | bytes 1 | tf_op jit(solution)/shard_map/pallas_call | solution.py:150
  94.5 6.0 %all-to-all-start.2 = ((f32[8,1,1152]{2,1,0:T(1,128)}), f32[8,1,1152]{2,1,0:T(1,128)S(1)}, u32[]{:S(2)}, u32[]{:S(2)}) async-start(f32[8,1,1152]{2,1,0:T(1,128)} %get-tuple-element.182), calls=%async_computation.2 | async-start | bytes 73728 | tf_op jit(solution)/shard_map/all_to_all | solution.py:977
  100.4 7.0 %shard_map.284.refs_4_.refs_7_ = s32[8,2048]{1,0:T(8,128)S(1)} custom-call(s32[3]{0:T(128)S(1)} %pad_add_fusion.meta_ref, s32[1,2048]{1,0:T(1,128)S(1)} %reshape.199.refs_2_.refs_4_.refs_0_.refs_1_.refs_5_), custom_call_target="tpu_custom_call" | custom-call | flops 6440000000 | bytes 1 | tf_op jit(solution)/shard_map/pallas_call | solution.py:150
  107.5 5.1 %shard_map.285 = (f32[1,128]{1,0:T(1,128)}, f32[128,768]{1,0:T(8,128)S(1)}, bf16[128,768]{1,0:T(8,128)(2,1)S(1)}, bf16[128,768]{1,0:T(8,128)(2,1)S(1)}, bf16[128,768]{1,0:T(8,128)(2,1)S(1)}) custom-call(s32[3]{0:T(128)S(1)} %pad_add_fusion.meta_ref, f32[8,1,1152]{2,1,0:T(1,128)S(1)} %all-to-all-done.2.refs_0_, ...), custom_call_target="tpu_custom_call" | custom-call | flops 4600000000 | bytes 1 | tf_op jit(solution)/shard_map/pallas_call | solution.py:150
  112.8 1.3 collective-permute-done.3
  114.1 1.6 collective-permute-start.4
  115.7 3.4 %shard_map.289 = (bf16[4,96,960]{2,1,0:T(8,128)(2,1)S(1)}, bf16[4,96,960]{2,1,0:T(8,128)(2,1)S(1)}, bf16[4,96,768]{2,1,0:T(8,128)(2,1)S(1)}, bf16[4,96,768]{2,1,0:T(8,128)(2,1)S(1)}, f32[2,768]{1,0:T(2,128)S(1)}) custom-call(s32[3]{0:T(128)S(1)} %pad_add_fusion.meta_ref, f32[8,768]{1,0:T(8,128)S(1)} %select_select_fusion.refs_1_.refs_3_.refs_2_.refs_0_.refs_4_, ...), custom_call_target="tpu_custom_call" | custom-call | flops 3680000000 | bytes 1 | tf_op jit(solution)/shard_map/pallas_call | solution.py:150
  119.1 2.1 collective-permute-start.8
  121.2 1.5 collective-permute-start.11
  122.7 11.4 %shard_map.286 = (f32[128,768]{1,0:T(8,128)S(1)}, bf16[768,192]{1,0:T(8,128)(2,1)S(1)}, bf16[1792,384]{1,0:T(8,128)(2,1)S(1)}, bf16[896,384]{1,0:T(8,128)(2,1)S(...) custom-call(s32[3]{0:T(128)S(1)} %pad_add_fusion.meta_ref, ...), custom_call_target="tpu_custom_call" | custom-call | flops 11960000512 | bytes 1 | tf_op jit(solution)/shard_map/pallas_call | solution.py:150
  134.7 1.3 collective-permute-done.11
  136.6 2.9 %collective-permute-done.8 = bf16[4,96,960]{2,1,0:T(8,128)(2,1)S(1)} collective-permute-done((bf16[4,96,960]{2,1,0:T(8,128)(2,1)S(1)}, bf16[4,96,960]{2,1,0:T(8,128)(2,1)S(1)}, u32[]{:S(2)}, u32[]{:S(2)}) %collective-permute-start.8) | collective-permute-done | bytes 737312 | tf_op jit(solution)/shard_map/ppermute | solution.py:173
  139.9 0.8 dynamic-slice_bitcast_fusion
  140.7 2.1 collective-permute-start.9
  142.7 1.0 shard_map.287
  144.4 12.6 %shard_map.288 = (bf16[2048,768]{1,0:T(8,128)(2,1)}, f32[16,768]{1,0:T(8,128)S(1)}, f32[2,768]{1,0:T(2,128)S(1)}, f32[512,768]{1,0:T(8,128)S(1)}, f32[16,512]{1,0:T(8,128)S(1)}, /*index=5*/bf16[512,128]{1,0:T(8,128)(2,1)S(1)}) custom-call(s32[3]{0:T(128)S(1)} %pad_add_fusion.meta_ref, bf16[8,192,256]{2,1,0:T(8,128)(2,1)S(1)} %get-tuple-element.203.refs_0_, ...), custom_call_target="tpu_custom_call" | custom-call | flops 11040000000 | bytes 1 | tf_op jit(solution)/shard_map/pallas_call | solution.py:150
  157.1 0.7 constant_dynamic-slice_fusion.4
  157.8 2.4 %collective-permute-start.13 = (bf16[1,96,768]{2,1,0:T(8,128)(2,1)}, bf16[1,96,768]{2,1,0:T(8,128)(2,1)}, u32[]{:S(2)}, u32[]{:S(2)}) collective-permute-start(bf16[1,96,768]{2,1,0:T(8,128)(2,1)} %constant_dynamic-slice_fusion.4), channel_id=1, source_target_pairs={{0,16},{4,20},{8,24},{12,28},{16,0},{20,4},{24,8},{28,12},{1,17},{... | collective-permute-start | bytes 442376 | tf_op jit(solution)/shard_map/ppermute | solution.py:173
  160.1 0.7 collective-permute-done.7.refs_1_
  160.9 4.4 %shard_map.290 = (bf16[128,768]{1,0:T(8,128)(2,1)S(1)}, bf16[8,224,256]{2,1,0:T(8,128)(2,1)}, bf16[4,96,768]{2,1,0:T(8,128)(2,1)S(1)}, bf16[4,96,768]{2,1,0:T(8,128)(2,1)S(1)}) custom-call(s32[3]{0:T(128)S(1)} %pad_add_fusion.meta_ref, bf16[1024,384]{1,0:T(8,128)(2,1)S(1)} %get-tuple-element.198.refs_0_, ...), custom_call_target="tpu_custom_call" | custom-call | flops 3680000000 | bytes 1 | tf_op jit(solution)/shard_map/pallas_call | solution.py:150
  165.3 1.5 collective-permute-start.14
  166.8 3.7 %all-to-all-start.3 = ((bf16[8,224,256]{2,1,0:T(8,128)(2,1)}), bf16[8,224,256]{2,1,0:T(8,128)(2,1)S(1)}, u32[]{:S(2)}, u32[]{:S(2)}) async-start(bf16[8,224,256]{2,1,0:T(8,128)(2,1)} %get-tuple-element.218), calls=%async_computation.3 | async-start | bytes 1835008 | tf_op jit(solution)/shard_map/all_to_all | solution.py:1104
  170.5 1.2 fusion.1
  171.7 0.8 constant_dynamic-slice_fusion.5
  172.4 2.9 %collective-permute-start.10 = (bf16[1,96,960]{2,1,0:T(8,128)(2,1)}, bf16[1,96,960]{2,1,0:T(8,128)(2,1)}, u32[]{:S(2)}, u32[]{:S(2)}) collective-permute-start(bf16[1,96,960]{2,1,0:T(8,128)(2,1)} %constant_dynamic-slice_fusion.5), channel_id=1, source_target_pairs={{0,16},{4,20},{8,24},{12,28},{16,0},{20,4},{24,8},{28,12},{1,17},{... | collective-permute-start | bytes 552968 | tf_op jit(solution)/shard_map/ppermute | solution.py:173
  175.4 1.7 add_bitcast_fusion.2
  177.0 7.7 %collective-permute-done.14 = bf16[4,96,768]{2,1,0:T(8,128)(2,1)} collective-permute-done((bf16[4,96,768]{2,1,0:T(8,128)(2,1)S(1)}, bf16[4,96,768]{2,1,0:T(8,128)(2,1)}, u32[]{:S(2)}, u32[]{:S(2)}) %collective-permute-start.14) | collective-permute-done | bytes 589856 | tf_op jit(solution)/shard_map/ppermute | solution.py:173
  184.8 1.3 add_convert_fusion.1
  186.4 12.4 %collective-permute-done.10 = bf16[1,96,960]{2,1,0:T(8,128)(2,1)} collective-permute-done((bf16[1,96,960]{2,1,0:T(8,128)(2,1)}, bf16[1,96,960]{2,1,0:T(8,128)(2,1)}, u32[]{:S(2)}, u32[]{:S(2)}) %collective-permute-start.10) | collective-permute-done | bytes 184352 | tf_op jit(solution)/shard_map/ppermute | solution.py:173
  198.9 1.0 add_bitcast_fusion.1
  199.9 0.8 slice_bitcast_fusion.1
  200.9 1.1 fusion
  202.7 3.2 %shard_map.291 = (f32[1000,768]{1,0:T(8,128)}, f32[96,32]{1,0:T(8,128)S(1)}, f32[1,128]{1,0:T(1,128)S(1)}) custom-call(s32[3]{0:T(128)S(1)} %pad_add_fusion.meta_ref, bf16[8,224,256]{2,1,0:T(8,128)(2,1)S(1)} %all-to-all-done.3.refs_0_), custom_call_target="tpu_custom_call" | custom-call | flops 2760000000 | bytes 1 | tf_op jit(solution)/shard_map/pallas_call | solution.py:150
  206.0 6.1 %all-gather.3 = f32[384,256]{1,0:T(8,128)S(1)} all-gather(f32[96,256]{1,0:T(8,128)S(1)} %maximum_maximum_fusion), channel_id=5, replica_groups=mesh['dp'=8,'mp'=4] {'mp'}, dimensions={0}, use_global_device_ids=true | all-gather | bytes 491520 | tf_op jit(solution)/shard_map/all_gather | solution.py:1126
  213.8 0.8 slice_reduce_fusion.3
  215.3 0.9 copy.63
  216.5 1.0 reshape.207
  (108 shorter events, 8.9 us)
Async XLA Ops:
  7.2 4.6 %copy-start.9 = (bf16[32,768]{1,0:T(8,128)(2,1)S(1)}, bf16[32,768]{1,0:T(8,128)(2,1)}, u32[]{:S(2)}) copy-start(bf16[32,768]{1,0:T(8,128)(2,1)} %param.21) | copy-start | bytes 147460
  7.2 5.5 %copy-start.10 = (s32[128,16]{0,1:T(8,128)S(1)}, s32[128,16]{0,1:T(8,128)}, u32[]{:S(2)}) copy-start(s32[128,16]{0,1:T(8,128)} %param.19) | copy-start | bytes 24580
  7.2 5.6 %copy-start.18 = (s32[128]{0:T(128)S(1)}, s32[128]{0:T(128)}, u32[]{:S(2)}) copy-start(s32[128]{0:T(128)} %param.20) | copy-start | bytes 1540
  7.2 5.8 %copy-start.11 = (bf16[768]{0:T(1024)(128)(2,1)S(1)}, bf16[768]{0:T(1024)(128)(2,1)}, u32[]{:S(2)}) copy-start(bf16[768]{0:T(1024)(128)(2,1)} %param.32) | copy-start | bytes 4612
  7.2 5.8 %copy-start.12 = (bf16[768]{0:T(1024)(128)(2,1)S(1)}, bf16[768]{0:T(1024)(128)(2,1)}, u32[]{:S(2)}) copy-start(bf16[768]{0:T(1024)(128)(2,1)} %param.24) | copy-start | bytes 4612
  7.2 5.8 %copy-start.13 = (bf16[768]{0:T(1024)(128)(2,1)S(1)}, bf16[768]{0:T(1024)(128)(2,1)}, u32[]{:S(2)}) copy-start(bf16[768]{0:T(1024)(128)(2,1)} %param.25) | copy-start | bytes 4612
  7.2 5.8 %copy-start.14 = (bf16[768]{0:T(1024)(128)(2,1)S(1)}, bf16[768]{0:T(1024)(128)(2,1)}, u32[]{:S(2)}) copy-start(bf16[768]{0:T(1024)(128)(2,1)} %param.28) | copy-start | bytes 4612
  7.3 5.8 %copy-start.15 = (bf16[768]{0:T(1024)(128)(2,1)S(1)}, bf16[768]{0:T(1024)(128)(2,1)}, u32[]{:S(2)}) copy-start(bf16[768]{0:T(1024)(128)(2,1)} %param.29) | copy-start | bytes 4612
  7.3 5.9 %copy-start.16 = (bf16[768]{0:T(1024)(128)(2,1)S(1)}, bf16[768]{0:T(1024)(128)(2,1)}, u32[]{:S(2)}) copy-start(bf16[768]{0:T(1024)(128)(2,1)} %param.30) | copy-start | bytes 4612
  7.3 5.9 %copy-start.17 = (bf16[768]{0:T(1024)(128)(2,1)S(1)}, bf16[768]{0:T(1024)(128)(2,1)}, u32[]{:S(2)}) copy-start(bf16[768]{0:T(1024)(128)(2,1)} %param.34) | copy-start | bytes 4612
  7.3 82.6 %all-gather.6.cloned.1.call-start = ((), (), s32[]{:S(2)}) async-start(), calls=%async_computation.4 | async-start | bytes 1622016 | tf_op jit(solution)/shard_map/all_gather | solution.py:896
  8.7 20.9 %copy-start.1 = (bf16[4,192,768]{2,1,0:T(8,128)(2,1)}, bf16[4,192,768]{2,1,0:T(8,128)(2,1)S(1)}, u32[]{:S(2)}) copy-start(bf16[4,192,768]{2,1,0:T(8,128)(2,1)S(1)} %pad_maximum_fusion.refs_5_.refs_9_.refs_14_.refs_3_.refs_6_.refs_10_.refs_17_.refs_16_) | copy-start | bytes 3538948
  8.7 39.0 %collective-permute-start = (bf16[4,192,768]{2,1,0:T(8,128)(2,1)S(1)}, bf16[4,192,768]{2,1,0:T(8,128)(2,1)S(1)}, u32[]{:S(2)}, u32[]{:S(2)}) collective-permute-start(bf16[4,192,768]{2,1,0:T(8,128)(2,1)S(1)} %pad_maximum_fusion.refs_5_.refs_9_.refs_14_.refs_3_.refs_6_.refs_10_.refs_17_.refs_16_), channel_id=1, source_target_pairs={{0,1},{1,0},{2,3},{3,2},{4,5},{5,4},{6,7},{7,6},{8,9},{9,8},{10,11... | collective-permute-start | bytes 3538952 | tf_op jit(solution)/shard_map/ppermute | solution.py:216
  9.2 29.6 %collective-permute-start.1 = (bf16[4,192,768]{2,1,0:T(8,128)(2,1)S(1)}, bf16[4,192,768]{2,1,0:T(8,128)(2,1)}, u32[]{:S(2)}, u32[]{:S(2)}) collective-permute-start(bf16[4,192,768]{2,1,0:T(8,128)(2,1)S(1)} %pad_maximum_fusion.refs_5_.refs_9_.refs_14_.refs_3_.refs_6_.refs_10_.refs_17_.refs_16_), channel_id=1, source_target_pairs={{0,2},{1,3},{2,0},{3,1},{4,6},{5,7},{6,4},{7,5},{8,10},{9,11},{10,... | collective-permute-start | bytes 3538952 | tf_op jit(solution)/shard_map/ppermute | solution.py:216
  13.3 16.4 %copy-start = (bf16[16,768]{1,0:T(8,128)(2,1)S(1)}, bf16[16,768]{1,0:T(8,128)(2,1)}, u32[]{:S(2)}) copy-start(bf16[16,768]{1,0:T(8,128)(2,1)} %refs_2_.1) | copy-start | bytes 73732
  38.8 8.9 %collective-permute-start.2 = (bf16[4,192,768]{2,1,0:T(8,128)(2,1)}, bf16[4,192,768]{2,1,0:T(8,128)(2,1)S(1)}, u32[]{:S(2)}, u32[]{:S(2)}) collective-permute-start(bf16[4,192,768]{2,1,0:T(8,128)(2,1)} %collective-permute-done.1.refs_7_.refs_11_.refs_16_.refs_5_.refs_8_.refs_12_.refs_19_.refs_18_), channel_id=1, source_target_pairs={{0,1},{1,0},{2,3},{3,2},{4,5},{5,4},{6,7},{7,6},{8,9},{9,8},{10,11... | collective-permute-start | bytes 3538952 | tf_op jit(solution)/shard_map/ppermute | solution.py:216
  47.7 1.0 copy-start.2
  47.7 1.5 copy-start.3
  94.5 13.0 %all-to-all-start.2 = ((f32[8,1,1152]{2,1,0:T(1,128)}), f32[8,1,1152]{2,1,0:T(1,128)S(1)}, u32[]{:S(2)}, u32[]{:S(2)}) async-start(f32[8,1,1152]{2,1,0:T(1,128)} %get-tuple-element.182), calls=%async_computation.2 | async-start | bytes 73728 | tf_op jit(solution)/shard_map/all_to_all | solution.py:977
  112.5 1.5 collective-permute-start.3
  114.1 8.5 %collective-permute-start.4 = (bf16[128,768]{1,0:T(8,128)(2,1)S(1)}, bf16[128,768]{1,0:T(8,128)(2,1)S(1)}, u32[]{:S(2)}, u32[]{:S(2)}) collective-permute-start(bf16[128,768]{1,0:T(8,128)(2,1)S(1)} %add.136), channel_id=1, source_target_pairs={{0,2},{1,3},{2,0},{3,1},{4,6},{5,7},{6,4},{7,5},{8,10},{9,11},{10,... | collective-permute-start | bytes 589832 | tf_op jit(solution)/shard_map/ppermute | solution.py:1031
  119.1 20.5 %collective-permute-start.8 = (bf16[4,96,960]{2,1,0:T(8,128)(2,1)S(1)}, bf16[4,96,960]{2,1,0:T(8,128)(2,1)S(1)}, u32[]{:S(2)}, u32[]{:S(2)}) collective-permute-start(bf16[4,96,960]{2,1,0:T(8,128)(2,1)S(1)} %get-tuple-element.225), channel_id=1, source_target_pairs={{0,4},{4,0},{8,12},{12,8},{16,20},{20,16},{24,28},{28,24},{1,5},{5... | collective-permute-start | bytes 2211848 | tf_op jit(solution)/shard_map/ppermute | solution.py:173
  121.2 14.8 %collective-permute-start.11 = (bf16[4,96,768]{2,1,0:T(8,128)(2,1)S(1)}, bf16[4,96,768]{2,1,0:T(8,128)(2,1)S(1)}, u32[]{:S(2)}, u32[]{:S(2)}) collective-permute-start(bf16[4,96,768]{2,1,0:T(8,128)(2,1)S(1)} %get-tuple-element.227), channel_id=1, source_target_pairs={{0,8},{4,12},{8,0},{12,4},{16,24},{20,28},{24,16},{28,20},{1,9},{5... | collective-permute-start | bytes 1769480 | tf_op jit(solution)/shard_map/ppermute | solution.py:173
  134.1 8.6 %collective-permute-start.5 = (bf16[896,384]{1,0:T(8,128)(2,1)S(1)}, bf16[896,384]{1,0:T(8,128)(2,1)S(1)}, u32[]{:S(2)}, u32[]{:S(2)}) collective-permute-start(bf16[896,384]{1,0:T(8,128)(2,1)S(1)} %get-tuple-element.196), channel_id=1, source_target_pairs={{0,1},{1,0},{2,3},{3,2},{4,5},{5,4},{6,7},{7,6},{8,9},{9,8},{10,11... | collective-permute-start | bytes 2064392 | tf_op jit(solution)/shard_map/ppermute | solution.py:1058
  134.2 8.6 %collective-permute-start.6 = (bf16[896,384]{1,0:T(8,128)(2,1)S(1)}, bf16[896,384]{1,0:T(8,128)(2,1)S(1)}, u32[]{:S(2)}, u32[]{:S(2)}) collective-permute-start(bf16[896,384]{1,0:T(8,128)(2,1)S(1)} %get-tuple-element.197), channel_id=1, source_target_pairs={{0,1},{1,0},{2,3},{3,2},{4,5},{5,4},{6,7},{7,6},{8,9},{9,8},{10,11... | collective-permute-start | bytes 2064392 | tf_op jit(solution)/shard_map/ppermute | solution.py:1058
  136.2 20.8 %collective-permute-start.12 = (bf16[2,96,768]{2,1,0:T(8,128)(2,1)S(1)}, bf16[2,96,768]{2,1,0:T(8,128)(2,1)S(1)}, u32[]{:S(2)}, u32[]{:S(2)}) collective-permute-start(bf16[2,96,768]{2,1,0:T(8,128)(2,1)S(1)} %get-tuple-element.323), channel_id=1, source_target_pairs={{0,4},{4,0},{8,12},{12,8},{16,20},{20,16},{24,28},{28,24},{1,5},{5... | collective-permute-start | bytes 884744 | tf_op jit(solution)/shard_map/ppermute | solution.py:173
  140.7 29.8 %collective-permute-start.9 = (bf16[2,96,960]{2,1,0:T(8,128)(2,1)}, bf16[2,96,960]{2,1,0:T(8,128)(2,1)}, u32[]{:S(2)}, u32[]{:S(2)}) collective-permute-start(bf16[2,96,960]{2,1,0:T(8,128)(2,1)} %dynamic-slice_bitcast_fusion), channel_id=1, source_target_pairs={{0,8},{4,12},{8,0},{12,4},{16,24},{20,28},{24,16},{28,20},{1,9},{5... | collective-permute-start | bytes 1105928 | tf_op jit(solution)/shard_map/ppermute | solution.py:173
  143.8 17.1 %collective-permute-start.7 = (bf16[1024,384]{1,0:T(8,128)(2,1)S(1)}, bf16[1024,384]{1,0:T(8,128)(2,1)S(1)}, u32[]{:S(2)}, u32[]{:S(2)}) collective-permute-start(bf16[1024,384]{1,0:T(8,128)(2,1)S(1)} %get-tuple-element.199), channel_id=1, source_target_pairs={{0,2},{1,3},{2,0},{3,1},{4,6},{5,7},{6,4},{7,5},{8,10},{9,11},{10,... | collective-permute-start | bytes 2359304 | tf_op jit(solution)/shard_map/ppermute | solution.py:1063
  157.1 3.8 %copy-start.7 = (bf16[2,96,768]{2,1,0:T(8,128)(2,1)}, bf16[2,96,768]{2,1,0:T(8,128)(2,1)S(1)}, u32[]{:S(2)}) copy-start(bf16[2,96,768]{2,1,0:T(8,128)(2,1)S(1)} %add_convert_fusion.3) | copy-start | bytes 884740
  157.8 17.6 %collective-permute-start.13 = (bf16[1,96,768]{2,1,0:T(8,128)(2,1)}, bf16[1,96,768]{2,1,0:T(8,128)(2,1)}, u32[]{:S(2)}, u32[]{:S(2)}) collective-permute-start(bf16[1,96,768]{2,1,0:T(8,128)(2,1)} %constant_dynamic-slice_fusion.4), channel_id=1, source_target_pairs={{0,16},{4,20},{8,24},{12,28},{16,0},{20,4},{24,8},{28,12},{1,17},{... | collective-permute-start | bytes 442376 | tf_op jit(solution)/shard_map/ppermute | solution.py:173
  165.3 19.4 %collective-permute-start.14 = (bf16[4,96,768]{2,1,0:T(8,128)(2,1)S(1)}, bf16[4,96,768]{2,1,0:T(8,128)(2,1)}, u32[]{:S(2)}, u32[]{:S(2)}) collective-permute-start(bf16[4,96,768]{2,1,0:T(8,128)(2,1)S(1)} %get-tuple-element.232), channel_id=1, source_target_pairs={{0,4},{4,0},{8,12},{12,8},{16,20},{20,16},{24,28},{28,24},{1,5},{5... | collective-permute-start | bytes 1769480 | tf_op jit(solution)/shard_map/ppermute | solution.py:173
  166.8 35.9 %all-to-all-start.3 = ((bf16[8,224,256]{2,1,0:T(8,128)(2,1)}), bf16[8,224,256]{2,1,0:T(8,128)(2,1)S(1)}, u32[]{:S(2)}, u32[]{:S(2)}) async-start(bf16[8,224,256]{2,1,0:T(8,128)(2,1)} %get-tuple-element.218), calls=%async_computation.3 | async-start | bytes 1835008 | tf_op jit(solution)/shard_map/all_to_all | solution.py:1104
  170.5 4.9 %copy-start.8 = (bf16[2,96,768]{2,1,0:T(8,128)(2,1)S(1)}, bf16[2,96,768]{2,1,0:T(8,128)(2,1)}, u32[]{:S(2)}) copy-start(bf16[2,96,768]{2,1,0:T(8,128)(2,1)} %copy-done.7) | copy-start | bytes 884740
  171.7 13.1 %copy-start.5 = (bf16[2,96,960]{2,1,0:T(8,128)(2,1)}, bf16[2,96,960]{2,1,0:T(8,128)(2,1)S(1)}, u32[]{:S(2)}) copy-start(bf16[2,96,960]{2,1,0:T(8,128)(2,1)S(1)} %fusion.1) | copy-start | bytes 1105924
  172.4 26.4 %collective-permute-start.10 = (bf16[1,96,960]{2,1,0:T(8,128)(2,1)}, bf16[1,96,960]{2,1,0:T(8,128)(2,1)}, u32[]{:S(2)}, u32[]{:S(2)}) collective-permute-start(bf16[1,96,960]{2,1,0:T(8,128)(2,1)} %constant_dynamic-slice_fusion.5), channel_id=1, source_target_pairs={{0,16},{4,20},{8,24},{12,28},{16,0},{20,4},{24,8},{28,12},{1,17},{... | collective-permute-start | bytes 552968 | tf_op jit(solution)/shard_map/ppermute | solution.py:173
  184.8 14.1 %copy-start.6 = (bf16[2,96,960]{2,1,0:T(8,128)(2,1)S(1)}, bf16[2,96,960]{2,1,0:T(8,128)(2,1)}, u32[]{:S(2)}) copy-start(bf16[2,96,960]{2,1,0:T(8,128)(2,1)} %copy-done.5) | copy-start | bytes 1105924
  186.3 14.6 %collective-permute-start.15 = (bf16[2,96,768]{1,2,0:T(8,128)(2,1)S(1)}, bf16[2,96,768]{1,2,0:T(8,128)(2,1)}, u32[]{:S(2)}, u32[]{:S(2)}) collective-permute-start(bf16[2,96,768]{1,2,0:T(8,128)(2,1)S(1)} %bitcast.71), channel_id=1, source_target_pairs={{0,8},{4,12},{8,0},{12,4},{16,24},{20,28},{24,16},{28,20},{1,9},{5... | collective-permute-start | bytes 884744 | tf_op jit(solution)/shard_map/ppermute | solution.py:173
  199.9 2.2 copy-start.4
  202.1 3.9 %slice-start = ((f32[96,960]{1,0:T(8,128)}), f32[96,192]{1,0:T(8,128)S(1)}, s32[]{:S(2)}) async-start(f32[96,960]{1,0:T(8,128)} %copy-done.4), calls=%async_computation.5 | async-start | bytes 196608 | tf_op jit(solution)/shard_map/slice | solution.py:1126
  202.1 12.5 %collective-permute-start.16 = (bf16[1,96,768]{1,2,0:T(8,128)(2,1)S(1)}, bf16[1,96,768]{1,2,0:T(8,128)(2,1)S(1)}, u32[]{:S(2)}, u32[]{:S(2)}) collective-permute-start(bf16[1,96,768]{1,2,0:T(8,128)(2,1)S(1)} %get-tuple-element.329), channel_id=1, source_target_pairs={{0,16},{4,20},{8,24},{12,28},{16,0},{20,4},{24,8},{28,12},{1,17},{... | collective-permute-start | bytes 442376 | tf_op jit(solution)/shard_map/ppermute | solution.py:173
Sparse Core Ops, SparseCore 0:
  12.8 56.4 all-gather.5

commit v3 on v2

--- a/solution.py
+++ b/solution.py
@@ -878,7 +878,7 @@
     own_width = width // n_mp
     ff = w_up.shape[1]
     owner_rows = vocab_part // n_dp
-    slot_cap = -(-rows // (n_dp * n_mp * 16)) * 16
+    slot_cap = -(-7 * rows // (n_dp * n_mp * 64)) * 8
     slots = n_dp * slot_cap
     chunk = width // n_dp
     lanes = own_width + 2 * SMALLS

time: 227 us -> 221 us (0.974)
  waiting for transfers between devices: 28.9 us -> 26.3 us
    ppermute x9, waiting for transfers between devices: 24.4 us -> 21.4 us  [exchange_half(): got = lax.ppermute(sent, axis, [(i, i ^ bit) for i in range(count)])]
  transfers between devices with their start and end apart: 20 -> 20, of which waited for: 7 -> 7; matrix products, arithmetic and copies ran while one was open for 14% -> 13% of each run, Pallas kernels for 27% -> 28%
where the time goes in v3:
time: 221 us; the launch traced here: 219 us
  Pallas kernels  70.5 us (32%)
  blocking collectives  44.2 us (20%)
  starting transfers between devices  28.9 us (13%)
  waiting for transfers between devices  26.3 us (12%)
  local copies, waits for them, and re-layouts  25.1 us (11%)
  between operations  14.9 us (7%)
  other arithmetic  8.64 us (4%)
    pallas_call x12, Pallas kernels, vmem_call(): pl.pallas_call(kernel, out_shape=[pltpu.HBM(*o[:2]) if len(o) > 2 else ja...  70.5 us
    ppermute x9, waiting for transfers between devices, exchange_half(): got = lax.ppermute(sent, axis, [(i, i ^ bit) for i in range(count)])  21.4 us
    all_gather x1, blocking collectives, on_device(): gather(pay)  20.4 us
    gather x1, local copies, waits for them, and re-layouts, on_device(): jnp.take(table, jnp.clip(local, 0, vocab_part - 1), axis=0, mode='clip')  16.2 us
    ppermute x9, starting transfers between devices, exchange_half(): got = lax.ppermute(sent, axis, [(i, i ^ bit) for i in range(count)])  13.4 us
    all_gather x1, blocking collectives, on_device(): gather(ends)  8.88 us
    all_gather x1, blocking collectives, on_device(): gather(part)  8.72 us
    all_gather x1, blocking collectives, on_device(): gather(jnp.concatenate([down[:, ff:], small, jnp.zeros_like(small)], 1))  6.15 us
  transfers between devices with their start and end apart: 20, of which 7 were waited for; matrix products, arithmetic and copies ran while one was open for 13% of the time, Pallas kernels for 28%

profile of v3, /device:TPU:0, one launch (start us, length us, event | category | flops | bytes accessed | tf_op | source)
XLA Modules:
  0.0 218.6 jit_solution(6433795808698571493)
XLA Ops:
  7.3 1.4 pad_maximum_fusion.refs_5_.refs_9_.refs_14_.refs_3_.refs_6_.refs_10_.refs_17_.refs_16_
  9.2 2.6 %collective-permute-start.1 = (bf16[4,192,768]{2,1,0:T(8,128)(2,1)S(1)}, bf16[4,192,768]{2,1,0:T(8,128)(2,1)}, u32[]{:S(2)}, u32[]{:S(2)}) collective-permute-start(bf16[4,192,768]{2,1,0:T(8,128)(2,1)S(1)} %pad_maximum_fusion.refs_5_.refs_9_.refs_14_.refs_3_.refs_6_.refs_10_.refs_17_.refs_16_), channel_id=1, source_target_pairs={{0,2},{1,3},{2,0},{3,1},{4,6},{5,7},{6,4},{7,5},{8,10},{9,11},{10,... | collective-permute-start | bytes 3538952 | tf_op jit(solution)/shard_map/ppermute | solution.py:216
  11.9 0.7 fusion.3
  13.4 16.2 %gather_fusion = bf16[2048,768]{1,0:T(8,128)(2,1)} fusion(bf16[8000,768]{1,0:T(8,128)(2,1)} %param.22, s32[2048]{0:T(1024)S(1)} %clamp_clamp_fusion), kind=kCustom, calls=%fused_computation | custom fusion | bytes 6299648 | tf_op jit(solution)/shard_map/jit(_take)/gather | solution.py:910
  29.8 6.6 %shard_map.280 = (bf16[128,768]{1,0:T(8,128)(2,1)S(1)}, bf16[2048,768]{1,0:T(8,128)(2,1)}, bf16[2048,768]{1,0:T(8,128)(2,1)}, f32[2048,128]{1,0:T(8,128)}) custom-call(s32[3]{0:T(128)S(1)} %pad_add_fusion.meta_ref, bf16[16,768]{1,0:T(8,128)(2,1)S(1)} %copy-done, f32[8,768]{1,0:T(8,128)S(1)} %select_select_fusion.refs_1_.refs_3_.refs_2_.refs_0_.refs_4_, ...), custom_call_target="tpu_custom_call" | custom-call | flops 920000000 | bytes 1 | tf_op jit(solution)/shard_map/pallas_call | solution.py:150
  36.4 2.5 %collective-permute-done.1.refs_7_.refs_11_.refs_16_.refs_5_.refs_8_.refs_12_.refs_19_.refs_18_ = bf16[4,192,768]{2,1,0:T(8,128)(2,1)} collective-permute-done((bf16[4,192,768]{2,1,0:T(8,128)(2,1)S(1)}, bf16[4,192,768]{2,1,0:T(8,128)(2,1)}, u32[]{:S(2)}, u32[]{:S(2)}) %collective-permute-start.1) | collective-permute-done | bytes 1179680 | tf_op jit(solution)/shard_map/ppermute | solution.py:216
  38.8 8.9 %all-gather = bf16[512,768]{1,0:T(8,128)(2,1)S(1)} all-gather(bf16[128,768]{1,0:T(8,128)(2,1)S(1)} %get-tuple-element.175), channel_id=2, replica_groups=mesh['dp'=8,'mp'=4] {'mp'}, dimensions={0}, use_global_device_ids=true | all-gather | bytes 983040 | tf_op jit(solution)/shard_map/all_gather | solution.py:943
  47.7 1.0 copy-done.2
  49.2 7.4 %shard_map.281 = (bf16[128,896]{1,0:T(8,128)(2,1)S(1)}, bf16[12,128,768]{2,1,0:T(8,128)(2,1)}, f32[128,768]{1,0:T(8,128)}, bf16[128,768]{1,0:T(8,128)(2,1)}) custom-call(s32[3]{0:T(128)S(1)} %pad_add_fusion.meta_ref, bf16[4,128,768]{2,1,0:T(8,128)(2,1)S(1)} %bitcast.60, bf16[128,16]{1,0:T(8,128)(2,1)S(1)} %get-tuple-element.330.refs_1_.refs_5_, ...), custom_call_target="tpu_custom_call" | custom-call | flops 920000000 | bytes 1 | tf_op jit(solution)/shard_map/pallas_call | solution.py:150
  56.6 20.4 %all-gather.1 = bf16[512,896]{1,0:T(8,128)(2,1)S(1)} all-gather(bf16[128,896]{1,0:T(8,128)(2,1)S(1)} %get-tuple-element.178), channel_id=3, replica_groups=mesh['dp'=8,'mp'=4] {'mp'}, dimensions={0}, use_global_device_ids=true | all-gather | bytes 1146880 | tf_op jit(solution)/shard_map/all_gather | solution.py:959
  77.0 4.1 %shard_map.282 = (f32[128,768]{1,0:T(8,128)}, f32[128,768]{1,0:T(8,128)}, f32[128,768]{1,0:T(8,128)}, f32[128,768]{1,0:T(8,128)}, bf16[128,768]{1,0:T(8,128)(2,1)S(1)}) custom-call(s32[3]{0:T(128)S(1)} %pad_add_fusion.meta_ref, bf16[4,128,896]{2,1,0:T(8,128)(2,1)S(1)} %bitcast.59, f32[8,768]{1,0:T(8,128)S(1)} %select_select_fusion.refs_1_.refs_3_.refs_2_.refs_0_.refs_4_, ...), custom_call_target="tpu_custom_call" | custom-call | flops 920000000 | bytes 1 | tf_op jit(solution)/shard_map/pallas_call | solution.py:150
  81.1 8.7 %all-gather.2 = bf16[512,768]{1,0:T(8,128)(2,1)S(1)} all-gather(bf16[128,768]{1,0:T(8,128)(2,1)S(1)} %get-tuple-element.180), channel_id=4, replica_groups=mesh['dp'=8,'mp'=4] {'mp'}, dimensions={0}, use_global_device_ids=true | all-gather | bytes 983040 | tf_op jit(solution)/shard_map/all_gather | solution.py:973
  89.8 4.6 %shard_map.283 = (bf16[128,768]{1,0:T(8,128)(2,1)}, f32[128,768]{1,0:T(8,128)}, f32[128,1024]{1,0:T(8,128)}, f32[8,1,1152]{2,1,0:T(1,128)}) custom-call(s32[3]{0:T(128)S(1)} %pad_add_fusion.meta_ref, bf16[4,128,768]{2,1,0:T(8,128)(2,1)S(1)} %bitcast.61, f32[8,768]{1,0:T(8,128)S(1)} %select_select_fusion.refs_1_.refs_3_.refs_2_.refs_0_.refs_4_, ...), custom_call_target="tpu_custom_call" | custom-call | flops 4600000000 | bytes 1 | tf_op jit(solution)/shard_map/pallas_call | solution.py:150
  94.5 6.0 %all-to-all-start.2 = ((f32[8,1,1152]{2,1,0:T(1,128)}), f32[8,1,1152]{2,1,0:T(1,128)S(1)}, u32[]{:S(2)}, u32[]{:S(2)}) async-start(f32[8,1,1152]{2,1,0:T(1,128)} %get-tuple-element.182), calls=%async_computation.2 | async-start | bytes 73728 | tf_op jit(solution)/shard_map/all_to_all | solution.py:977
  100.4 7.0 %shard_map.284.refs_4_.refs_7_ = s32[8,2048]{1,0:T(8,128)S(1)} custom-call(s32[3]{0:T(128)S(1)} %pad_add_fusion.meta_ref, s32[1,2048]{1,0:T(1,128)S(1)} %reshape.199.refs_2_.refs_4_.refs_0_.refs_1_.refs_5_), custom_call_target="tpu_custom_call" | custom-call | flops 6440000000 | bytes 1 | tf_op jit(solution)/shard_map/pallas_call | solution.py:150
  107.5 5.0 %shard_map.285 = (f32[1,128]{1,0:T(1,128)}, f32[128,768]{1,0:T(8,128)S(1)}, bf16[128,768]{1,0:T(8,128)(2,1)S(1)}, bf16[128,768]{1,0:T(8,128)(2,1)S(1)}, bf16[128,768]{1,0:T(8,128)(2,1)S(1)}) custom-call(s32[3]{0:T(128)S(1)} %pad_add_fusion.meta_ref, f32[8,1,1152]{2,1,0:T(1,128)S(1)} %all-to-all-done.2.refs_0_, ...), custom_call_target="tpu_custom_call" | custom-call | flops 4600000000 | bytes 1 | tf_op jit(solution)/shard_map/pallas_call | solution.py:150
  112.8 1.3 collective-permute-done.3
  114.1 1.6 collective-permute-start.4
  115.7 3.4 %shard_map.289 = (bf16[4,96,960]{2,1,0:T(8,128)(2,1)S(1)}, bf16[4,96,960]{2,1,0:T(8,128)(2,1)S(1)}, bf16[4,96,768]{2,1,0:T(8,128)(2,1)S(1)}, bf16[4,96,768]{2,1,0:T(8,128)(2,1)S(1)}, f32[2,768]{1,0:T(2,128)S(1)}) custom-call(s32[3]{0:T(128)S(1)} %pad_add_fusion.meta_ref, f32[8,768]{1,0:T(8,128)S(1)} %select_select_fusion.refs_1_.refs_3_.refs_2_.refs_0_.refs_4_, ...), custom_call_target="tpu_custom_call" | custom-call | flops 3680000000 | bytes 1 | tf_op jit(solution)/shard_map/pallas_call | solution.py:150
  119.1 2.1 collective-permute-start.8
  121.2 1.5 collective-permute-start.11
  122.7 11.4 %shard_map.286 = (f32[128,768]{1,0:T(8,128)S(1)}, bf16[768,192]{1,0:T(8,128)(2,1)S(1)}, bf16[1792,384]{1,0:T(8,128)(2,1)S(1)}, bf16[896,384]{1,0:T(8,128)(2,1)S(...) custom-call(s32[3]{0:T(128)S(1)} %pad_add_fusion.meta_ref, ...), custom_call_target="tpu_custom_call" | custom-call | flops 11960000512 | bytes 1 | tf_op jit(solution)/shard_map/pallas_call | solution.py:150
  134.7 1.3 collective-permute-done.11
  136.6 2.9 %collective-permute-done.8 = bf16[4,96,960]{2,1,0:T(8,128)(2,1)S(1)} collective-permute-done((bf16[4,96,960]{2,1,0:T(8,128)(2,1)S(1)}, bf16[4,96,960]{2,1,0:T(8,128)(2,1)S(1)}, u32[]{:S(2)}, u32[]{:S(2)}) %collective-permute-start.8) | collective-permute-done | bytes 737312 | tf_op jit(solution)/shard_map/ppermute | solution.py:173
  139.9 2.1 collective-permute-start.9
  142.0 1.0 shard_map.287
  143.6 12.2 %shard_map.288 = (bf16[2048,768]{1,0:T(8,128)(2,1)}, f32[16,768]{1,0:T(8,128)S(1)}, f32[2,768]{1,0:T(2,128)S(1)}, f32[448,768]{1,0:T(8,128)S(1)}, f32[16,448]{1,0:T(8,128)S(1)}, /*index=5*/bf16[448,128]{1,0:T(8,128)(2,1)S(1)}) custom-call(s32[3]{0:T(128)S(1)} %pad_add_fusion.meta_ref, bf16[8,192,256]{2,1,0:T(8,128)(2,1)S(1)} %get-tuple-element.203.refs_0_, ...), custom_call_target="tpu_custom_call" | custom-call | flops 11040000000 | bytes 1 | tf_op jit(solution)/shard_map/pallas_call | solution.py:150
  156.0 0.7 constant_dynamic-slice_fusion.4
  156.7 2.4 %collective-permute-start.13 = (bf16[1,96,768]{2,1,0:T(8,128)(2,1)}, bf16[1,96,768]{2,1,0:T(8,128)(2,1)}, u32[]{:S(2)}, u32[]{:S(2)}) collective-permute-start(bf16[1,96,768]{2,1,0:T(8,128)(2,1)} %constant_dynamic-slice_fusion.4), channel_id=1, source_target_pairs={{0,16},{4,20},{8,24},{12,28},{16,0},{20,4},{24,8},{28,12},{1,17},{... | collective-permute-start | bytes 442376 | tf_op jit(solution)/shard_map/ppermute | solution.py:173
  159.0 1.1 collective-permute-done.7.refs_1_
  160.1 4.4 %shard_map.290 = (bf16[128,768]{1,0:T(8,128)(2,1)S(1)}, bf16[8,200,256]{2,1,0:T(8,128)(2,1)}, bf16[4,96,768]{2,1,0:T(8,128)(2,1)S(1)}, bf16[4,96,768]{2,1,0:T(8,128)(2,1)S(1)}) custom-call(s32[3]{0:T(128)S(1)} %pad_add_fusion.meta_ref, bf16[1024,384]{1,0:T(8,128)(2,1)S(1)} %get-tuple-element.198.refs_0_, ...), custom_call_target="tpu_custom_call" | custom-call | flops 3680000000 | bytes 1 | tf_op jit(solution)/shard_map/pallas_call | solution.py:150
  164.6 1.5 collective-permute-start.14
  166.3 2.4 %collective-permute-start.10 = (bf16[1,96,960]{2,1,0:T(8,128)(2,1)S(1)}, bf16[1,96,960]{2,1,0:T(8,128)(2,1)}, u32[]{:S(2)}, u32[]{:S(2)}) collective-permute-start(bf16[1,96,960]{2,1,0:T(8,128)(2,1)S(1)} %constant_dynamic-slice_fusion.5), channel_id=1, source_target_pairs={{0,16},{4,20},{8,24},{12,28},{16,0},{20,4},{24,8},{28,12},{1,17},{... | collective-permute-start | bytes 552968 | tf_op jit(solution)/shard_map/ppermute | solution.py:173
  168.7 3.5 %all-to-all-start.3 = ((bf16[8,200,256]{2,1,0:T(8,128)(2,1)}), bf16[8,200,256]{2,1,0:T(8,128)(2,1)S(1)}, u32[]{:S(2)}, u32[]{:S(2)}) async-start(bf16[8,200,256]{2,1,0:T(8,128)(2,1)} %get-tuple-element.218), calls=%async_computation.3 | async-start | bytes 1638400 | tf_op jit(solution)/shard_map/all_to_all | solution.py:1104
  172.3 1.7 add_bitcast_fusion.2
  174.0 7.3 %collective-permute-done.14 = bf16[4,96,768]{2,1,0:T(8,128)(2,1)} collective-permute-done((bf16[4,96,768]{2,1,0:T(8,128)(2,1)S(1)}, bf16[4,96,768]{2,1,0:T(8,128)(2,1)}, u32[]{:S(2)}, u32[]{:S(2)}) %collective-permute-start.14) | collective-permute-done | bytes 589856 | tf_op jit(solution)/shard_map/ppermute | solution.py:173
  181.3 1.3 add_convert_fusion.1
  182.8 0.8 collective-permute-start.15
  183.6 1.0 add_bitcast_fusion.1
  184.6 0.8 slice_bitcast_fusion.1
  185.6 9.9 %collective-permute-done.15 = bf16[2,96,768]{1,2,0:T(8,128)(2,1)} collective-permute-done((bf16[2,96,768]{1,2,0:T(8,128)(2,1)S(1)}, bf16[2,96,768]{1,2,0:T(8,128)(2,1)}, u32[]{:S(2)}, u32[]{:S(2)}) %collective-permute-start.15) | collective-permute-done | bytes 294944 | tf_op jit(solution)/shard_map/ppermute | solution.py:173
  195.4 1.1 fusion
  196.9 3.2 %shard_map.291 = (f32[1000,768]{1,0:T(8,128)}, f32[96,32]{1,0:T(8,128)S(1)}, f32[1,128]{1,0:T(1,128)S(1)}) custom-call(s32[3]{0:T(128)S(1)} %pad_add_fusion.meta_ref, bf16[8,200,256]{2,1,0:T(8,128)(2,1)S(1)} %all-to-all-done.3.refs_0_), custom_call_target="tpu_custom_call" | custom-call | flops 2760000000 | bytes 1 | tf_op jit(solution)/shard_map/pallas_call | solution.py:150
  200.2 6.1 %all-gather.3 = f32[384,256]{1,0:T(8,128)S(1)} all-gather(f32[96,256]{1,0:T(8,128)S(1)} %maximum_maximum_fusion), channel_id=5, replica_groups=mesh['dp'=8,'mp'=4] {'mp'}, dimensions={0}, use_global_device_ids=true | all-gather | bytes 491520 | tf_op jit(solution)/shard_map/all_gather | solution.py:1126
  206.5 0.7 slice_reduce_fusion.1
  207.9 0.8 slice_reduce_fusion.3
  209.5 0.9 copy.63
  210.6 1.0 reshape.207
  (100 shorter events, 7.2 us)
Async XLA Ops:
  7.2 4.6 %copy-start.5 = (bf16[32,768]{1,0:T(8,128)(2,1)S(1)}, bf16[32,768]{1,0:T(8,128)(2,1)}, u32[]{:S(2)}) copy-start(bf16[32,768]{1,0:T(8,128)(2,1)} %param.21) | copy-start | bytes 147460
  7.2 5.5 %copy-start.6 = (s32[128,16]{0,1:T(8,128)S(1)}, s32[128,16]{0,1:T(8,128)}, u32[]{:S(2)}) copy-start(s32[128,16]{0,1:T(8,128)} %param.19) | copy-start | bytes 24580
  7.2 5.6 %copy-start.14 = (s32[128]{0:T(128)S(1)}, s32[128]{0:T(128)}, u32[]{:S(2)}) copy-start(s32[128]{0:T(128)} %param.20) | copy-start | bytes 1540
  7.2 5.8 %copy-start.7 = (bf16[768]{0:T(1024)(128)(2,1)S(1)}, bf16[768]{0:T(1024)(128)(2,1)}, u32[]{:S(2)}) copy-start(bf16[768]{0:T(1024)(128)(2,1)} %param.32) | copy-start | bytes 4612
  7.2 5.8 %copy-start.8 = (bf16[768]{0:T(1024)(128)(2,1)S(1)}, bf16[768]{0:T(1024)(128)(2,1)}, u32[]{:S(2)}) copy-start(bf16[768]{0:T(1024)(128)(2,1)} %param.24) | copy-start | bytes 4612
  7.2 5.8 %copy-start.9 = (bf16[768]{0:T(1024)(128)(2,1)S(1)}, bf16[768]{0:T(1024)(128)(2,1)}, u32[]{:S(2)}) copy-start(bf16[768]{0:T(1024)(128)(2,1)} %param.25) | copy-start | bytes 4612
  7.2 5.8 %copy-start.10 = (bf16[768]{0:T(1024)(128)(2,1)S(1)}, bf16[768]{0:T(1024)(128)(2,1)}, u32[]{:S(2)}) copy-start(bf16[768]{0:T(1024)(128)(2,1)} %param.28) | copy-start | bytes 4612
  7.3 5.8 %copy-start.11 = (bf16[768]{0:T(1024)(128)(2,1)S(1)}, bf16[768]{0:T(1024)(128)(2,1)}, u32[]{:S(2)}) copy-start(bf16[768]{0:T(1024)(128)(2,1)} %param.29) | copy-start | bytes 4612
  7.3 5.9 %copy-start.12 = (bf16[768]{0:T(1024)(128)(2,1)S(1)}, bf16[768]{0:T(1024)(128)(2,1)}, u32[]{:S(2)}) copy-start(bf16[768]{0:T(1024)(128)(2,1)} %param.30) | copy-start | bytes 4612
  7.3 5.9 %copy-start.13 = (bf16[768]{0:T(1024)(128)(2,1)S(1)}, bf16[768]{0:T(1024)(128)(2,1)}, u32[]{:S(2)}) copy-start(bf16[768]{0:T(1024)(128)(2,1)} %param.34) | copy-start | bytes 4612
  7.3 82.6 %all-gather.6.cloned.1.call-start = ((), (), s32[]{:S(2)}) async-start(), calls=%async_computation.4 | async-start | bytes 1622016 | tf_op jit(solution)/shard_map/all_gather | solution.py:896
  8.7 20.8 %copy-start.1 = (bf16[4,192,768]{2,1,0:T(8,128)(2,1)}, bf16[4,192,768]{2,1,0:T(8,128)(2,1)S(1)}, u32[]{:S(2)}) copy-start(bf16[4,192,768]{2,1,0:T(8,128)(2,1)S(1)} %pad_maximum_fusion.refs_5_.refs_9_.refs_14_.refs_3_.refs_6_.refs_10_.refs_17_.refs_16_) | copy-start | bytes 3538948
  8.7 39.0 %collective-permute-start = (bf16[4,192,768]{2,1,0:T(8,128)(2,1)S(1)}, bf16[4,192,768]{2,1,0:T(8,128)(2,1)S(1)}, u32[]{:S(2)}, u32[]{:S(2)}) collective-permute-start(bf16[4,192,768]{2,1,0:T(8,128)(2,1)S(1)} %pad_maximum_fusion.refs_5_.refs_9_.refs_14_.refs_3_.refs_6_.refs_10_.refs_17_.refs_16_), channel_id=1, source_target_pairs={{0,1},{1,0},{2,3},{3,2},{4,5},{5,4},{6,7},{7,6},{8,9},{9,8},{10,11... | collective-permute-start | bytes 3538952 | tf_op jit(solution)/shard_map/ppermute | solution.py:216
  9.2 29.6 %collective-permute-start.1 = (bf16[4,192,768]{2,1,0:T(8,128)(2,1)S(1)}, bf16[4,192,768]{2,1,0:T(8,128)(2,1)}, u32[]{:S(2)}, u32[]{:S(2)}) collective-permute-start(bf16[4,192,768]{2,1,0:T(8,128)(2,1)S(1)} %pad_maximum_fusion.refs_5_.refs_9_.refs_14_.refs_3_.refs_6_.refs_10_.refs_17_.refs_16_), channel_id=1, source_target_pairs={{0,2},{1,3},{2,0},{3,1},{4,6},{5,7},{6,4},{7,5},{8,10},{9,11},{10,... | collective-permute-start | bytes 3538952 | tf_op jit(solution)/shard_map/ppermute | solution.py:216
  13.3 16.4 %copy-start = (bf16[16,768]{1,0:T(8,128)(2,1)S(1)}, bf16[16,768]{1,0:T(8,128)(2,1)}, u32[]{:S(2)}) copy-start(bf16[16,768]{1,0:T(8,128)(2,1)} %refs_2_.1) | copy-start | bytes 73732
  38.8 8.9 %collective-permute-start.2 = (bf16[4,192,768]{2,1,0:T(8,128)(2,1)}, bf16[4,192,768]{2,1,0:T(8,128)(2,1)S(1)}, u32[]{:S(2)}, u32[]{:S(2)}) collective-permute-start(bf16[4,192,768]{2,1,0:T(8,128)(2,1)} %collective-permute-done.1.refs_7_.refs_11_.refs_16_.refs_5_.refs_8_.refs_12_.refs_19_.refs_18_), channel_id=1, source_target_pairs={{0,1},{1,0},{2,3},{3,2},{4,5},{5,4},{6,7},{7,6},{8,9},{9,8},{10,11... | collective-permute-start | bytes 3538952 | tf_op jit(solution)/shard_map/ppermute | solution.py:216
  47.7 1.0 copy-start.2
  47.7 1.5 copy-start.3
  94.5 13.0 %all-to-all-start.2 = ((f32[8,1,1152]{2,1,0:T(1,128)}), f32[8,1,1152]{2,1,0:T(1,128)S(1)}, u32[]{:S(2)}, u32[]{:S(2)}) async-start(f32[8,1,1152]{2,1,0:T(1,128)} %get-tuple-element.182), calls=%async_computation.2 | async-start | bytes 73728 | tf_op jit(solution)/shard_map/all_to_all | solution.py:977
  112.5 1.5 collective-permute-start.3
  114.1 8.5 %collective-permute-start.4 = (bf16[128,768]{1,0:T(8,128)(2,1)S(1)}, bf16[128,768]{1,0:T(8,128)(2,1)S(1)}, u32[]{:S(2)}, u32[]{:S(2)}) collective-permute-start(bf16[128,768]{1,0:T(8,128)(2,1)S(1)} %add.136), channel_id=1, source_target_pairs={{0,2},{1,3},{2,0},{3,1},{4,6},{5,7},{6,4},{7,5},{8,10},{9,11},{10,... | collective-permute-start | bytes 589832 | tf_op jit(solution)/shard_map/ppermute | solution.py:1031
  119.1 20.5 %collective-permute-start.8 = (bf16[4,96,960]{2,1,0:T(8,128)(2,1)S(1)}, bf16[4,96,960]{2,1,0:T(8,128)(2,1)S(1)}, u32[]{:S(2)}, u32[]{:S(2)}) collective-permute-start(bf16[4,96,960]{2,1,0:T(8,128)(2,1)S(1)} %get-tuple-element.225), channel_id=1, source_target_pairs={{0,4},{4,0},{8,12},{12,8},{16,20},{20,16},{24,28},{28,24},{1,5},{5... | collective-permute-start | bytes 2211848 | tf_op jit(solution)/shard_map/ppermute | solution.py:173
  121.2 14.8 %collective-permute-start.11 = (bf16[4,96,768]{2,1,0:T(8,128)(2,1)S(1)}, bf16[4,96,768]{2,1,0:T(8,128)(2,1)S(1)}, u32[]{:S(2)}, u32[]{:S(2)}) collective-permute-start(bf16[4,96,768]{2,1,0:T(8,128)(2,1)S(1)} %get-tuple-element.227), channel_id=1, source_target_pairs={{0,8},{4,12},{8,0},{12,4},{16,24},{20,28},{24,16},{28,20},{1,9},{5... | collective-permute-start | bytes 1769480 | tf_op jit(solution)/shard_map/ppermute | solution.py:173
  134.1 7.9 %collective-permute-start.5 = (bf16[896,384]{1,0:T(8,128)(2,1)S(1)}, bf16[896,384]{1,0:T(8,128)(2,1)S(1)}, u32[]{:S(2)}, u32[]{:S(2)}) collective-permute-start(bf16[896,384]{1,0:T(8,128)(2,1)S(1)} %get-tuple-element.196), channel_id=1, source_target_pairs={{0,1},{1,0},{2,3},{3,2},{4,5},{5,4},{6,7},{7,6},{8,9},{9,8},{10,11... | collective-permute-start | bytes 2064392 | tf_op jit(solution)/shard_map/ppermute | solution.py:1058
  134.2 7.8 %collective-permute-start.6 = (bf16[896,384]{1,0:T(8,128)(2,1)S(1)}, bf16[896,384]{1,0:T(8,128)(2,1)S(1)}, u32[]{:S(2)}, u32[]{:S(2)}) collective-permute-start(bf16[896,384]{1,0:T(8,128)(2,1)S(1)} %get-tuple-element.197), channel_id=1, source_target_pairs={{0,1},{1,0},{2,3},{3,2},{4,5},{5,4},{6,7},{7,6},{8,9},{9,8},{10,11... | collective-permute-start | bytes 2064392 | tf_op jit(solution)/shard_map/ppermute | solution.py:1058
  136.2 19.7 %collective-permute-start.12 = (bf16[2,96,768]{2,1,0:T(8,128)(2,1)S(1)}, bf16[2,96,768]{2,1,0:T(8,128)(2,1)S(1)}, u32[]{:S(2)}, u32[]{:S(2)}) collective-permute-start(bf16[2,96,768]{2,1,0:T(8,128)(2,1)S(1)} %get-tuple-element.323), channel_id=1, source_target_pairs={{0,4},{4,0},{8,12},{12,8},{16,20},{20,16},{24,28},{28,24},{1,5},{5... | collective-permute-start | bytes 884744 | tf_op jit(solution)/shard_map/ppermute | solution.py:173
  139.9 26.2 %collective-permute-start.9 = (bf16[2,96,960]{2,1,0:T(8,128)(2,1)S(1)}, bf16[2,96,960]{2,1,0:T(8,128)(2,1)S(1)}, u32[]{:S(2)}, u32[]{:S(2)}) collective-permute-start(bf16[2,96,960]{2,1,0:T(8,128)(2,1)S(1)} %dynamic-slice_bitcast_fusion), channel_id=1, source_target_pairs={{0,8},{4,12},{8,0},{12,4},{16,24},{20,28},{24,16},{28,20},{1,9},{5... | collective-permute-start | bytes 1105928 | tf_op jit(solution)/shard_map/ppermute | solution.py:173
  143.0 17.1 %collective-permute-start.7 = (bf16[1024,384]{1,0:T(8,128)(2,1)S(1)}, bf16[1024,384]{1,0:T(8,128)(2,1)S(1)}, u32[]{:S(2)}, u32[]{:S(2)}) collective-permute-start(bf16[1024,384]{1,0:T(8,128)(2,1)S(1)} %get-tuple-element.199), channel_id=1, source_target_pairs={{0,2},{1,3},{2,0},{3,1},{4,6},{5,7},{6,4},{7,5},{8,10},{9,11},{10,... | collective-permute-start | bytes 2359304 | tf_op jit(solution)/shard_map/ppermute | solution.py:1063
  156.7 15.6 %collective-permute-start.13 = (bf16[1,96,768]{2,1,0:T(8,128)(2,1)}, bf16[1,96,768]{2,1,0:T(8,128)(2,1)}, u32[]{:S(2)}, u32[]{:S(2)}) collective-permute-start(bf16[1,96,768]{2,1,0:T(8,128)(2,1)} %constant_dynamic-slice_fusion.4), channel_id=1, source_target_pairs={{0,16},{4,20},{8,24},{12,28},{16,0},{20,4},{24,8},{28,12},{1,17},{... | collective-permute-start | bytes 442376 | tf_op jit(solution)/shard_map/ppermute | solution.py:173
  164.6 16.7 %collective-permute-start.14 = (bf16[4,96,768]{2,1,0:T(8,128)(2,1)S(1)}, bf16[4,96,768]{2,1,0:T(8,128)(2,1)}, u32[]{:S(2)}, u32[]{:S(2)}) collective-permute-start(bf16[4,96,768]{2,1,0:T(8,128)(2,1)S(1)} %get-tuple-element.232), channel_id=1, source_target_pairs={{0,4},{4,0},{8,12},{12,8},{16,20},{20,16},{24,28},{28,24},{1,5},{5... | collective-permute-start | bytes 1769480 | tf_op jit(solution)/shard_map/ppermute | solution.py:173
  166.3 17.3 %collective-permute-start.10 = (bf16[1,96,960]{2,1,0:T(8,128)(2,1)S(1)}, bf16[1,96,960]{2,1,0:T(8,128)(2,1)}, u32[]{:S(2)}, u32[]{:S(2)}) collective-permute-start(bf16[1,96,960]{2,1,0:T(8,128)(2,1)S(1)} %constant_dynamic-slice_fusion.5), channel_id=1, source_target_pairs={{0,16},{4,20},{8,24},{12,28},{16,0},{20,4},{24,8},{28,12},{1,17},{... | collective-permute-start | bytes 552968 | tf_op jit(solution)/shard_map/ppermute | solution.py:173
  168.7 28.1 %all-to-all-start.3 = ((bf16[8,200,256]{2,1,0:T(8,128)(2,1)}), bf16[8,200,256]{2,1,0:T(8,128)(2,1)S(1)}, u32[]{:S(2)}, u32[]{:S(2)}) async-start(bf16[8,200,256]{2,1,0:T(8,128)(2,1)} %get-tuple-element.218), calls=%async_computation.3 | async-start | bytes 1638400 | tf_op jit(solution)/shard_map/all_to_all | solution.py:1104
  182.8 12.7 %collective-permute-start.15 = (bf16[2,96,768]{1,2,0:T(8,128)(2,1)S(1)}, bf16[2,96,768]{1,2,0:T(8,128)(2,1)}, u32[]{:S(2)}, u32[]{:S(2)}) collective-permute-start(bf16[2,96,768]{1,2,0:T(8,128)(2,1)S(1)} %bitcast.71), channel_id=1, source_target_pairs={{0,8},{4,12},{8,0},{12,4},{16,24},{20,28},{24,16},{28,20},{1,9},{5... | collective-permute-start | bytes 884744 | tf_op jit(solution)/shard_map/ppermute | solution.py:173
  184.6 12.1 %copy-start.4 = (f32[96,960]{1,0:T(8,128)}, f32[96,960]{1,0:T(8,128)S(1)}, u32[]{:S(2)}) copy-start(f32[96,960]{1,0:T(8,128)S(1)} %add_bitcast_fusion.1) | copy-start | bytes 1105924
  196.6 3.5 %slice-start = ((f32[96,960]{1,0:T(8,128)}), f32[96,192]{1,0:T(8,128)S(1)}, s32[]{:S(2)}) async-start(f32[96,960]{1,0:T(8,128)} %copy-done.4), calls=%async_computation.5 | async-start | bytes 196608 | tf_op jit(solution)/shard_map/slice | solution.py:1126
  196.6 12.1 %collective-permute-start.16 = (bf16[1,96,768]{1,2,0:T(8,128)(2,1)S(1)}, bf16[1,96,768]{1,2,0:T(8,128)(2,1)S(1)}, u32[]{:S(2)}, u32[]{:S(2)}) collective-permute-start(bf16[1,96,768]{1,2,0:T(8,128)(2,1)S(1)} %get-tuple-element.329), channel_id=1, source_target_pairs={{0,16},{4,20},{8,24},{12,28},{16,0},{20,4},{24,8},{28,12},{1,17},{... | collective-permute-start | bytes 442376 | tf_op jit(solution)/shard_map/ppermute | solution.py:173
Sparse Core Ops, SparseCore 0:
  12.8 56.4 all-gather.5
